TPU v7x, 32 devices: a whole 2x2x4 slice. The times are simulated.
32 devices in a mesh: dp: 16 (over z, x, core), seq: 2 (over y).
Axes of the slice: x: 2, y: 2, z: 4, core: 2. Of those that a mesh axis runs over, the one named last changes fastest.
Arguments:
- tokens: bfloat16 [16, 768, 1024], P('dp', 'seq'), may hold values from -6 to 6
- masks: int32 [16, 6, 6], P('dp', 'seq'), may hold values from 0 to 1, as said below
- ln_gain: float32 [1024], replicated, may hold values from 0.25 to 1.75
- ln_bias: float32 [1024], replicated, may hold values from -3 to 3
- w_qkv: bfloat16 [1024, 3072], P('dp'), may hold values from -0.4 to 0.4
- qkv_bias: float32 [3072], replicated, may hold values from -3 to 3
- w_out: bfloat16 [1024, 1024], P('dp'), may hold values from -0.1875 to 0.1875
- out_bias: float32 [1024], replicated, may hold values from -2 to 2
Outputs:
- updated: bfloat16 [16, 768, 1024], P('dp', 'seq')
- context: bfloat16 [16, 768, 1024], P('dp', 'seq')
Inputs may be any that keep to these rules, and one draw needn't show every extreme that they name: Entries are 0 or 1; every diagonal entry masks[s, b, b] is 1.
All inputs are finite; a program needn't handle non-finite values.
Results may differ from a plain program's by a relative error of at most 0.012.
Values may be sent and summed in bfloat16 or wider, within the bound.
No kernel may reach another device: no remote copies, remote signals or barrier semaphores. Data moves between devices by JAX's collectives and lax.ppermute only.
A program may use at most 192 MiB of HBM per device.

v0:
```python
import jax
import jax.numpy as jnp
from jax import lax
from jax.sharding import PartitionSpec as P

D = 1024
HEADS = 16
BLOCK = 128


NEG_FILL = -1e30
EPSILON = 1e-06


def from_behind(block, axis, distance):
    devices = range(lax.axis_size(axis))
    route = [((i - distance) % len(devices), i) for i in devices]
    return lax.ppermute(block, axis, route)


def layer_norm(sheet, ln_gain, ln_bias):
    values = sheet.astype(jnp.float32)
    center = jnp.mean(values, axis=-1, keepdims=True)
    spread = jnp.mean(jnp.square(values - center), axis=-1, keepdims=True)
    normed = (values - center) * lax.rsqrt(spread + EPSILON)
    return (normed * ln_gain + ln_bias).astype(jnp.bfloat16)


def row_adder(left_operand, shard_piece):
    return jnp.dot(left_operand, shard_piece, preferred_element_type=jnp.float32)


def attend(state_now, key_piece, value_piece, first_row, queries, mask_rows):
    key_rows = key_piece.shape[0]
    query_blocks = mask_rows.shape[0]
    head_dim = D // HEADS
    scaling = head_dim ** (-0.5)
    block_ids = (first_row + lax.iota(jnp.int32, key_rows)) // BLOCK
    picker = (block_ids[:, None] == lax.iota(jnp.int32, mask_rows.shape[1])[None, :]).astype(
        jnp.float32
    )
    tile_mask = jnp.dot(mask_rows.astype(jnp.float32), picker.T)
    allowed = jnp.broadcast_to(
        (tile_mask > 0.5)[:, None, :], (query_blocks, BLOCK, key_rows)
    ).reshape(query_blocks * BLOCK, key_rows)
    active = jnp.any(allowed)

    def update(inner):
        run_max, run_sum, weighted = inner
        token_count = weighted.shape[0]
        key_heads = key_piece.reshape(key_rows, HEADS, head_dim)
        value_heads = value_piece.reshape(key_rows, HEADS, head_dim)
        scores = (
            jnp.einsum("qhd,khd->hqk", queries, key_heads, preferred_element_type=jnp.float32)
            * scaling
        )
        masked = jnp.where(allowed[None], scores, NEG_FILL)
        new_max = jnp.maximum(run_max, jnp.max(masked, axis=2))
        weights = jnp.where(allowed[None], jnp.exp(scores - new_max[:, :, None]), 0.0)
        factor = jnp.exp(run_max - new_max)
        new_sum = run_sum * factor + jnp.sum(weights, axis=2)
        mixed = jnp.einsum(
            "hqk,khd->qhd",
            weights.astype(jnp.bfloat16),
            value_heads,
            preferred_element_type=jnp.float32,
        )
        rescaled = weighted.reshape(token_count, HEADS, head_dim) * factor.T[:, :, None]
        return (new_max, new_sum, (rescaled + mixed).reshape(token_count, HEADS * head_dim))

    def unchanged(inner):
        return inner

    return lax.cond(active, update, unchanged, state_now)


def on_device(tokens, masks, ln_gain, ln_bias, w_qkv, qkv_bias, w_out, out_bias):
    sheet = tokens[0]
    mask_rows = masks[0]
    tokens_here = sheet.shape[0]
    width = sheet.shape[1]
    head_dim = D // HEADS
    normed = layer_norm(sheet, ln_gain, ln_bias)
    packed_raw = row_adder(normed, lax.all_gather(w_qkv, "dp", axis=0, tiled=True))
    packed = (packed_raw + qkv_bias).astype(jnp.bfloat16)
    queries = packed[:, :width].reshape(tokens_here, HEADS, head_dim)
    key_part = packed[:, width : 2 * width]
    value_part = packed[:, 2 * width :]
    start_state = (
        jnp.full((HEADS, tokens_here), NEG_FILL, jnp.float32),
        jnp.zeros((HEADS, tokens_here), jnp.float32),
        jnp.zeros((tokens_here, width), jnp.float32),
    )
    position = lax.axis_index("seq")
    loop_size = lax.axis_size("seq")
    own_state = attend(
        start_state, key_part, value_part, position * tokens_here, queries, mask_rows
    )

    def hop_step(hop_index, loop_state):
        moving, inner = loop_state
        moving = from_behind(moving, "seq", 1)
        source = (position - hop_index) % loop_size
        inner = attend(inner, moving[0], moving[1], source * tokens_here, queries, mask_rows)
        return (moving, inner)

    moved_last, final_state = lax.fori_loop(
        1, loop_size, hop_step, (jnp.stack([key_part, value_part]), own_state)
    )
    run_max, run_sum, weighted = final_state
    context = (
        (weighted.reshape(tokens_here, HEADS, head_dim) / run_sum.T[:, :, None])
        .reshape(tokens_here, width)
        .astype(jnp.bfloat16)
    )
    projected = row_adder(context, lax.all_gather(w_out, "dp", axis=0, tiled=True))
    updated = (sheet.astype(jnp.float32) + projected + out_bias).astype(jnp.bfloat16)
    return (updated[None], context[None])


def solution(mesh):
    placed = (
        P("dp", "seq", None),
        P("dp", "seq", None),
        P(),
        P(),
        P("dp", None),
        P(),
        P("dp", None),
        P(),
    )
    return jax.shard_map(
        on_device,
        mesh=mesh,
        in_specs=placed,
        out_specs=(P("dp", "seq", None), P("dp", "seq", None)),
        check_vma=False,
    )
```

profile of v0, /device:TPU:0, one launch (start us, length us, event | category | flops | bytes accessed | tf_op | source)
XLA Modules:
  0.0 142.9 jit_solution(11460875865751832251)
XLA Ops:
  8.6 1.3 convert_reduce_fusion
  10.0 1.5 %fusion.25 = f32[384]{0:T(512)S(1)} fusion(bf16[1,384,1024]{2,1,0:T(8,128)(2,1)} %param.12, f32[384]{0:T(512)S(1)} %broadcast_multiply_fusion), kind=kLoop, calls=%fused_computation.32 | loop fusion | flops 1572480 | bytes 789504 | tf_op jit(solution)/shard_map/reduce_sum | solution.py:24
  11.5 63.4 %all-gather.3.cloned.1.call-done = bf16[1024,3072]{1,0:T(8,128)(2,1)} async-done(((bf16[64,3072]{1,0:T(8,128)(2,1)}), bf16[1024,3072]{1,0:T(8,128)(2,1)}) %all-gather.3.cloned.1.call-update) | async-done | bytes 6291472 | tf_op jit(solution)/shard_map/all_gather | solution.py:84
  74.9 5.7 %add_convert_fusion = bf16[384,3072]{1,0:T(8,128)(2,1)S(1)} fusion(bf16[1024,3072]{1,0:T(8,128)(2,1)} %all-gather.3.cloned.1.call-done, f32[3072]{0:T(1024)} %param.17, bf16[1,384,1024]{2,1,0:T(8,128)(2,1)} %param.12, f32[1024]{0:T(1024)} %param.15, f32[1024]{0:T(1024)} %param.14, f32[384]{0:T(512)S(1)} %add_rsqrt_fusion, f32[384]{0:T(512)S(1)} %broadcast_multiply_fusion), kind=kOutput, calls=%fused_computation.25 | convolution fusion | flops 2420637696 | bytes 9460736 | tf_op jit(solution)/shard_map/dot_general | solution.py:30
  81.1 1.3 pad_maximum_fusion
  82.4 1.5 %collective-permute-start = (bf16[2,384,1024]{2,1,0:T(8,128)(2,1)}, bf16[2,384,1024]{2,1,0:T(8,128)(2,1)}, u32[]{:S(2)}, u32[]{:S(2)}) collective-permute-start(bf16[2,384,1024]{2,1,0:T(8,128)(2,1)} %pad_maximum_fusion), channel_id=1, source_target_pairs={{1,0},{0,1},{3,2},{2,3},{5,4},{4,5},{7,6},{6,7},{9,8},{8,9},{11,10... | collective-permute-start | bytes 4718600 | tf_op jit(solution)/shard_map/while/body/eval_jaxpr/ppermute | solution.py:18
  84.1 0.8 broadcast_reduce_fusion.1
  85.8 0.8 broadcast_reduce_fusion
  87.7 12.7 %conditional.2 = (f32[16,384]{1,0:T(8,128)}, f32[16,384]{1,0:T(8,128)S(1)}, f32[384,1024]{0,1:T(8,128)S(1)}) conditional(s32[]{:T(128)} %convert_element_type.49, () %tuple.30, (pred[3,128,384]{2,1,0:T(8,128)(4,1)S(1)}, bf16[384,1024]{1,0:T(8,128)(2,1)S(1)}, bf16[384,16,64]{0,2,1:T(8,128)(2,1)S(1)}, bf16[384,1024]{1,0:T(8,128)(2,1)S(1)}) %tuple.59), branch_computations={%region_4.5_spmd, %region_5.0_spmd} | conditional | flops 630349824 | bytes 74145848 | solution.py:74
  88.3 1.6 %select_reduce_fusion = (f32[16,384]{1,0:T(8,128)S(1)}, f32[16,384,384]{1,2,0:T(8,128)S(1)}) fusion(pred[384,384]{0,1:T(8,128)(4,1)S(1)} %copy.21, bf16[384,16,64]{0,2,1:T(8,128)(2,1)S(1)} %get-tuple-element.71, bf16[384,16,64]{0,2,1:T(8,128)(2,1)S(1)} %bitcast.79), kind=kOutput, calls=%fused_computation.1 | convolution fusion | flops 309061632 | bytes 11182080 | tf_op jit(solution)/shard_map/cond/branch_1_fun/qhd,khd->hqk/dot_general | solution.py:54
  90.6 2.7 %fusion.1 = f32[16,384]{1,0:T(8,128)S(1)} fusion(f32[16,384,384]{1,2,0:T(8,128)S(1)} %get-tuple-element.123, f32[16,384]{1,0:T(8,128)} %get-tuple-element.132, pred[384,384]{0,1:T(8,128)(4,1)S(1)} %copy.21), kind=kLoop, calls=%fused_computation.3 | loop fusion | flops 9431040 | bytes 9633792 | tf_op jit(solution)/shard_map/cond/branch_1_fun/reduce_sum | solution.py:61
  93.6 0.7 fusion.8
  94.7 5.7 %bitcast_add_fusion = f32[384,16,64]{0,2,1:T(8,128)S(1)} fusion(bf16[384,16,64]{0,2,1:T(8,128)(2,1)S(1)} %bitcast.81, f32[16,384,384]{1,2,0:T(8,128)} %copy-done, f32[16,384]{1,0:T(8,128)} %get-tuple-element.132, pred[384,384]{0,1:T(8,128)(4,1)S(1)} %copy.21, f32[384,16]{0,1:T(8,128)S(1)} %get-tuple-element.114), kind=kOutput, calls=%fused_computation.6 | convolution fusion | flops 311820288 | bytes 11993088 | tf_op jit(solution)/shard_map/cond/branch_1_fun/hqk,khd->qhd/dot_general | solution.py:62
  100.4 18.9 %collective-permute-done = bf16[2,384,1024]{2,1,0:T(8,128)(2,1)} collective-permute-done((bf16[2,384,1024]{2,1,0:T(8,128)(2,1)}, bf16[2,384,1024]{2,1,0:T(8,128)(2,1)}, u32[]{:S(2)}, u32[]{:S(2)}) %collective-permute-start) | collective-permute-done | bytes 1572896 | tf_op jit(solution)/shard_map/while/body/eval_jaxpr/ppermute | solution.py:18
  119.3 11.9 %conditional.3 = ((f32[16,384]{1,0:T(8,128)S(1)}, f32[384,1024]{0,1:T(8,128)S(1)})) conditional(s32[]{:T(128)} %convert_element_type.48, (f32[16,384]{1,0:T(8,128)S(1)}, f32[384,1024]{0,1:T(8,128)S(1)}) %tuple.32, (pred[3,128,384]{2,1,0:T(8,128)(4,1)S(1)}, bf16[2,384,1024]{2,1,0:T(8,128)(2,1)}, bf16[384,16,64]{0,2,1:T(8,128)(2,1)S(1)}, ...), branch_computations={%region_8.9_spmd, %region_9.12_spmd} | conditional | flops 630736896 | bytes 41189400 | solution.py:74
  119.8 2.6 %copy.28 = bf16[2,384,1024]{1,2,0:T(8,128)(2,1)} copy(bf16[2,384,1024]{2,1,0:T(8,128)(2,1)} %get-tuple-element.107) | data formatting | bytes 3145728 | tf_op jit(solution)/shard_map
  122.4 1.5 %fusion.52 = (bf16[1,384,1024]{1,2,0:T(8,128)(2,1)S(1)}, bf16[1,384,1024]{1,2,0:T(8,128)(2,1)S(1)}) fusion(bf16[2,384,1024]{1,2,0:T(8,128)(2,1)} %copy.28), kind=kLoop, calls=%fused_computation.82 | loop fusion | bytes 3145728 | tf_op jit(solution)/shard_map/while/body/eval_jaxpr/slice | solution.py:104
  124.0 1.6 %select_reduce_fusion.1 = (f32[16,384]{1,0:T(8,128)S(1)}, f32[16,384,384]{1,2,0:T(8,128)S(1)}) fusion(pred[384,384]{0,1:T(8,128)(4,1)S(1)} %copy.23, bf16[384,16,64]{0,2,1:T(8,128)(2,1)S(1)} %get-tuple-element.77, bf16[384,16,64]{0,2,1:T(8,128)(2,1)S(1)} %bitcast.80), kind=kOutput, calls=%fused_computation.14 | convolution fusion | flops 309061632 | bytes 11182080 | tf_op jit(solution)/shard_map/while/body/eval_jaxpr/cond/branch_1_fun/qhd,khd->hqk/dot_general | solution.py:54
  125.5 0.8 fusion.18
  126.3 1.9 %fusion.12 = f32[16,384]{1,0:T(8,128)S(1)} fusion(f32[16,384,384]{1,2,0:T(8,128)S(1)} %get-tuple-element.121, f32[16,384]{1,0:T(8,128)S(1)} %get-tuple-element.117, pred[384,384]{0,1:T(8,128)(4,1)S(1)} %copy.23), kind=kLoop, calls=%fused_computation.16 | loop fusion | flops 9431040 | bytes 9633792 | tf_op jit(solution)/shard_map/while/body/eval_jaxpr/cond/branch_1_fun/reduce_sum | solution.py:61
  128.2 0.8 multiply_add_fusion
  129.0 2.3 %bitcast_add_fusion.1 = f32[384,16,64]{0,2,1:T(8,128)S(1)} fusion(f32[384,16,64]{0,2,1:T(8,128)S(1)} %bitcast.77, bf16[384,16,64]{0,2,1:T(8,128)(2,1)S(1)} %bitcast.82, f32[16,384,384]{1,2,0:T(8,128)S(1)} %get-tuple-element.121, f32[16,384]{1,0:T(8,128)S(1)} %get-tuple-element.117, pred[384,384]{0,1:T(8,128)(4,1)S(1)} %copy.23, ...), kind=kOutput, calls=%fused_computation.19 | convolution fusion | flops 312213504 | bytes 13565952 | tf_op jit(solution)/shard_map/while/body/eval_jaxpr/cond/branch_1_fun/hqk,khd->qhd/dot_general | solution.py:62
  131.4 1.2 copy.29
  132.6 3.5 %fusion.32 = bf16[1,384,1024]{2,1,0:T(8,128)(2,1)} fusion(bf16[384,1024]{0,1:T(8,128)(2,1)S(1)} %fusion.31, bf16[1024,1024]{1,0:T(8,128)(2,1)} %all-gather.5.cloned.1.call-done, bf16[1,384,1024]{2,1,0:T(8,128)(2,1)S(1)} %copy-done.1, f32[1024]{0:T(1024)S(1)} %copy-done.2), kind=kOutput, calls=%fused_computation.41 | convolution fusion | flops 806879232 | bytes 4460544 | tf_op jit(solution)/shard_map/dot_general | solution.py:30
  (30 shorter events, 5.3 us)
Async XLA Ops:
  7.2 67.7 %all-gather.3.cloned.1.call-start = ((), (), s32[]{:S(2)}) async-start(), calls=%async_computation | async-start | bytes 6684672 | tf_op jit(solution)/shard_map/all_gather | solution.py:84
  7.9 124.7 %all-gather.5.cloned.1.call-start = ((), (), s32[]{:S(2)}) async-start(), calls=%async_computation.1 | async-start | bytes 2228224 | tf_op jit(solution)/shard_map/all_gather | solution.py:116
  80.6 3.3 %copy-start.3 = (s32[1,3,6]{2,0,1:T(1,128)S(1)}, s32[1,3,6]{2,0,1:T(1,128)}, u32[]{:S(2)}) copy-start(s32[1,3,6]{2,0,1:T(1,128)} %param.13) | copy-start | bytes 220
  82.4 36.9 %collective-permute-start = (bf16[2,384,1024]{2,1,0:T(8,128)(2,1)}, bf16[2,384,1024]{2,1,0:T(8,128)(2,1)}, u32[]{:S(2)}, u32[]{:S(2)}) collective-permute-start(bf16[2,384,1024]{2,1,0:T(8,128)(2,1)} %pad_maximum_fusion), channel_id=1, source_target_pairs={{1,0},{0,1},{3,2},{2,3},{5,4},{4,5},{7,6},{6,7},{9,8},{8,9},{11,10... | collective-permute-start | bytes 4718600 | tf_op jit(solution)/shard_map/while/body/eval_jaxpr/ppermute | solution.py:18
  89.9 3.6 %copy-start = (f32[16,384,384]{1,2,0:T(8,128)}, f32[16,384,384]{1,2,0:T(8,128)S(1)}, u32[]{:S(2)}) copy-start(f32[16,384,384]{1,2,0:T(8,128)S(1)} %get-tuple-element.123) | copy-start | bytes 28311556 | tf_op jit(solution)/shard_map/cond
  119.3 13.3 %copy-start.1 = (bf16[1,384,1024]{2,1,0:T(8,128)(2,1)S(1)}, bf16[1,384,1024]{2,1,0:T(8,128)(2,1)}, u32[]{:S(2)}) copy-start(bf16[1,384,1024]{2,1,0:T(8,128)(2,1)} %param.12) | copy-start | bytes 2359300
  119.3 13.3 %copy-start.2 = (f32[1024]{0:T(1024)S(1)}, f32[1024]{0:T(1024)}, u32[]{:S(2)}) copy-start(f32[1024]{0:T(1024)} %param.19) | copy-start | bytes 12292
Sparse Core Ops, SparseCore 0:
  10.3 64.5 all-gather.2
  77.0 39.8 all-gather.4
where the time goes:
time: 143 us
  waiting for transfers between devices  83.7 us (59%)
  matrix products  20.8 us (15%)
  between operations  15.4 us (11%)
  other arithmetic  13.3 us (9%)
  local copies, waits for them, and re-layouts  7.86 us (5%)
  starting transfers between devices  1.55 us (1%)
    all_gather x1, waiting for transfers between devices, on_device(): lax.all_gather(w_qkv, 'dp', axis=0, tiled=True)  63.4 us
    ppermute x1, waiting for transfers between devices, from_behind(): return lax.ppermute(block, axis, route)  18.9 us
    dot_general x2, matrix products, row_adder(): jnp.dot(left_operand, shard_piece, preferred_element_type=jnp.float32)  9.17 us
    dot_general x2, matrix products, update(): jnp.einsum('hqk,khd->qhd', weights.astype(jnp.bfloat16), value_heads, pre...  7.98 us
    reduce_sum x2, other arithmetic, update(): new_sum = run_sum * factor + jnp.sum(weights, axis=2)  4.59 us
    another operation x3, local copies, waits for them, and re-layouts  3.31 us
    dot_general x2, matrix products, update(): jnp.einsum('qhd,khd->hqk', queries, key_heads, preferred_element_type=jnp...  3.14 us
  transfers between devices with their start and end apart: 3, of which 2 were waited for; matrix products, arithmetic and copies ran while one was open for 27% of the time, Pallas kernels for 0%

commit v1 on v0

v1 whole, which is shorter than its diff:
```python
import functools

import jax
import jax.numpy as jnp
from jax import lax
from jax.experimental import pallas as pl
from jax.experimental.pallas import tpu as pltpu
from jax.sharding import PartitionSpec as P

D = 1024
HEADS = 16
BLOCK = 128
HEAD_DIM = D // HEADS
PAIR = 2 * HEAD_DIM

NEG_FILL = -1e30
EPSILON = 1e-06
VMEM_LIMIT = 56 * 1024 * 1024

VMEM = pl.BlockSpec(memory_space=pltpu.VMEM)
SMEM = pl.BlockSpec(memory_space=pltpu.SMEM)


def swap(block, axis, distance):
    if distance == 0:
        return block
    size = lax.axis_size(axis)
    return lax.ppermute(block, axis, [(i, i ^ distance) for i in range(size)])


def call(kernel, out_shape, in_specs, scratch=(), flops=0, nbytes=0, name=None):
    many = isinstance(out_shape, (list, tuple))
    return pl.pallas_call(
        kernel,
        out_shape=out_shape,
        in_specs=in_specs,
        out_specs=[VMEM] * len(out_shape) if many else VMEM,
        scratch_shapes=scratch,
        compiler_params=pltpu.CompilerParams(vmem_limit_bytes=VMEM_LIMIT),
        cost_estimate=pl.CostEstimate(
            flops=flops, bytes_accessed=nbytes, transcendentals=0
        ),
        name=name,
    )


def norm_kernel(sheet_ref, gain_ref, bias_ref, out_ref):
    step = 64

    @pl.loop(0, sheet_ref.shape[0] // step)
    def _(index):
        rows = pl.ds(pl.multiple_of(index * step, step), step)
        values = sheet_ref[rows, :].astype(jnp.float32)
        center = jnp.mean(values, axis=-1, keepdims=True)
        moved = values - center
        spread = jnp.mean(jnp.square(moved), axis=-1, keepdims=True)
        normed = moved * lax.rsqrt(spread + EPSILON)
        out_ref[rows, :] = (normed * gain_ref[...] + bias_ref[...]).astype(jnp.bfloat16)


def gather_rows(pieces, here, target):
    rows = pieces[0][1].shape[0]
    for slot, piece in pieces:
        first = pl.multiple_of((here ^ slot) * rows, rows)
        target[pl.ds(first, rows), :] = piece[...]


def attend_block(query, row_mask, blocks, key_ref, value_ref, scores, tops, sums, store):
    pairs = key_ref.shape[1] // PAIR
    lane = lax.broadcasted_iota(jnp.int32, (BLOCK, PAIR), 1)
    low = lane < HEAD_DIM
    tops[...] = jnp.full(tops.shape, NEG_FILL, jnp.float32)
    sums[...] = jnp.zeros(sums.shape, jnp.float32)
    ones = jnp.ones((BLOCK, PAIR), jnp.bfloat16)

    @pl.loop(0, blocks)
    def _(block):
        @pl.when(row_mask(block) == 1)
        def _():
            rows = pl.ds(pl.multiple_of(block * BLOCK, BLOCK), BLOCK)
            for pair in range(pairs):
                lanes = pl.ds(pair * PAIR, PAIR)
                both = query(lanes)
                zero = jnp.zeros_like(both)
                stacked = jnp.concatenate(
                    [jnp.where(low, both, zero), jnp.where(low, zero, both)], axis=0
                )
                found = lax.dot_general(
                    stacked,
                    key_ref[rows, lanes],
                    (((1,), (1,)), ((), ())),
                    preferred_element_type=jnp.float32,
                )
                scores[block, pair] = found
                tops[pair] = jnp.maximum(tops[pair], found)

    for pair in range(pairs):
        top = jnp.max(tops[pair], axis=1, keepdims=True)
        tops[pair] = jnp.broadcast_to(top, tops.shape[1:])

    @pl.loop(0, blocks)
    def _(block):
        @pl.when(row_mask(block) == 1)
        def _():
            rows = pl.ds(pl.multiple_of(block * BLOCK, BLOCK), BLOCK)
            for pair in range(pairs):
                lanes = pl.ds(pair * PAIR, PAIR)
                weights = jnp.exp(scores[block, pair] - tops[pair]).astype(jnp.bfloat16)
                widened = jnp.concatenate([value_ref[rows, lanes], ones], axis=1)
                sums[pair] += jnp.dot(
                    weights, widened, preferred_element_type=jnp.float32
                )

    for pair in range(pairs):
        mixed = sums[pair, :, :PAIR] / sums[pair, :, PAIR:]
        store(
            pl.ds(pair * PAIR, PAIR),
            jnp.where(low, mixed[:BLOCK], mixed[BLOCK:]).astype(jnp.bfloat16),
        )


def attend_strip(query_ref, first_row, mask_row, out_ref, seat, strips, key_ref, value_ref, scores, tops, sums):
    per_strip = out_ref.shape[0] // BLOCK

    @pl.loop(0, per_strip)
    def _(index):
        rows = pl.ds(pl.multiple_of(index * BLOCK, BLOCK), BLOCK)
        source = pl.ds(pl.multiple_of(first_row + index * BLOCK, BLOCK), BLOCK)

        def allowed(block):
            strip = block // per_strip
            column = (seat ^ strip) * per_strip + block % per_strip
            return mask_row(index, column)

        def store(lanes, value):
            out_ref[rows, lanes] = value

        attend_block(
            lambda lanes: query_ref[source, lanes],
            allowed,
            strips * per_strip,
            key_ref,
            value_ref,
            scores,
            tops,
            sums,
            store,
        )


def project_kernel(strips, slots, *refs):
    ids_ref, masks_ref = refs[:2]
    normed = refs[2 : 2 + strips]
    pieces = refs[2 + strips : 2 + strips + len(slots)]
    bias_ref = refs[2 + strips + len(slots)]
    rest = refs[3 + strips + len(slots) :]
    away, (query_ref, key_ref, value_ref), (weight, queries, scores, tops, sums) = (
        rest[: strips - 1],
        rest[strips - 1 : strips + 2],
        rest[strips + 2 :],
    )
    here, seat = ids_ref[0], ids_ref[1]
    gather_rows(list(zip(slots, pieces)), here, weight)
    length = normed[0].shape[0]
    width = key_ref.shape[1]
    step = PAIR * 2 if width % (PAIR * 2) == 0 else PAIR
    for kind in range(3):

        @pl.loop(0, width // step)
        def _(index):
            first = pl.multiple_of(index * step, step)
            lanes = pl.ds(pl.multiple_of(kind * width + first, step), step)
            for strip in range(strips):
                found = jnp.dot(
                    normed[strip][...],
                    weight[:, lanes],
                    preferred_element_type=jnp.float32,
                )
                found = found + bias_ref[:, lanes]
                rows = pl.ds(strip * length, length)
                out = pl.ds(first, step)
                if kind == 0:
                    found = (found * HEAD_DIM**-0.5).astype(jnp.bfloat16)
                    if strip == 0:
                        query_ref[:, out] = found
                    else:
                        queries[pl.ds((strip - 1) * length, length), out] = found
                elif kind == 1:
                    key_ref[rows, out] = found.astype(jnp.bfloat16)
                else:
                    value_ref[rows, out] = found.astype(jnp.bfloat16)

    for strip in range(1, strips):
        attend_strip(
            queries,
            (strip - 1) * length,
            lambda index, column: masks_ref[strip, index, column],
            away[strip - 1],
            seat,
            strips,
            key_ref,
            value_ref,
            scores,
            tops,
            sums,
        )


def own_kernel(strips, ids_ref, masks_ref, query_ref, key_ref, value_ref, out_ref, scores, tops, sums):
    attend_strip(
        query_ref,
        0,
        lambda index, column: masks_ref[0, index, column],
        out_ref,
        ids_ref[1],
        strips,
        key_ref,
        value_ref,
        scores,
        tops,
        sums,
    )


def output_kernel(strips, slots, *refs):
    ids_ref = refs[0]
    parts = refs[1 : 1 + strips]
    pieces = refs[1 + strips : 1 + strips + len(slots)]
    sheet_ref, bias_ref, updated_ref, context_ref, weight = refs[1 + strips + len(slots) :]
    here, seat = ids_ref[0], ids_ref[1]
    gather_rows(list(zip(slots, pieces)), here, weight)
    width = parts[0].shape[1]
    for strip, part in enumerate(parts):
        first = pl.multiple_of((seat ^ strip) * width, width)
        context_ref[:, pl.ds(first, width)] = part[...]
    step = 256

    @pl.loop(0, updated_ref.shape[1] // step)
    def _(index):
        lanes = pl.ds(pl.multiple_of(index * step, step), step)
        found = jnp.dot(
            context_ref[...], weight[:, lanes], preferred_element_type=jnp.float32
        )
        found = sheet_ref[:, lanes].astype(jnp.float32) + found + bias_ref[:, lanes]
        updated_ref[:, lanes] = found.astype(jnp.bfloat16)


def spread_rows(own, size):
    along_x = size // 8
    pieces = {0: own}
    for z in range(1, 4):
        pieces[2 * along_x * z] = swap(own, "dp", 2 * along_x * z)
    for z in range(4):
        far = 2 * along_x * z
        for x in range(1, along_x):
            pieces[far + 2 * x] = swap(pieces[far], "dp", 2 * x)
    return pieces


def on_device(tokens, masks, ln_gain, ln_bias, w_qkv, qkv_bias, w_out, out_bias):
    size, strips = lax.axis_size("dp"), lax.axis_size("seq")
    here, seat = lax.axis_index("dp"), lax.axis_index("seq")
    ids = jnp.stack([here, seat]).astype(jnp.int32)
    sheet = tokens[0]
    length, features = sheet.shape
    width = D // strips
    total = length * strips
    blocks = total // BLOCK
    pairs = width // PAIR
    rows = w_qkv.shape[0]

    own = lax.dynamic_index_in_dim(
        w_qkv.reshape(rows, 3, strips, width), seat, 2, keepdims=False
    ).reshape(rows, 3 * width)
    bias = lax.dynamic_index_in_dim(
        qkv_bias.reshape(3, strips, width), seat, 1, keepdims=False
    ).reshape(1, 3 * width)

    sheets = [swap(sheet, "seq", k) for k in range(strips)]
    mask_rows = jnp.stack([swap(masks[0], "seq", k) for k in range(strips)])

    pieces = spread_rows(own, size)
    for slot in sorted(pieces):
        pieces[slot + 1] = swap(pieces[slot], "dp", 1)
    slots = sorted(pieces)

    out_pieces = spread_rows(w_out, size)
    out_slots = sorted(out_pieces)
    packed = jnp.concatenate([out_pieces[slot] for slot in out_slots], axis=0)
    other = swap(packed, "dp", 1)
    for index, slot in enumerate(out_slots):
        out_pieces[slot + 1] = other[index * rows : (index + 1) * rows]

    normed = [
        call(
            norm_kernel,
            jax.ShapeDtypeStruct((length, features), jnp.bfloat16),
            [VMEM] * 3,
            flops=10 * length * features,
            nbytes=4 * length * features,
            name="norm",
        )(block, ln_gain[None], ln_bias[None])
        for block in sheets
    ]

    work = [
        pltpu.VMEM((blocks, pairs, 2 * BLOCK, BLOCK), jnp.float32),
        pltpu.VMEM((pairs, 2 * BLOCK, BLOCK), jnp.float32),
        pltpu.VMEM((pairs, 2 * BLOCK, 2 * PAIR), jnp.float32),
    ]
    strip_out = jax.ShapeDtypeStruct((length, width), jnp.bfloat16)
    whole_out = jax.ShapeDtypeStruct((total, width), jnp.bfloat16)
    *away, query, key, value = call(
        functools.partial(project_kernel, strips, slots),
        [strip_out] * (strips - 1) + [strip_out, whole_out, whole_out],
        [SMEM, SMEM] + [VMEM] * (strips + len(slots) + 1),
        [
            pltpu.VMEM((D, 3 * width), jnp.bfloat16),
            pltpu.VMEM((total - length, width), jnp.bfloat16),
        ]
        + work,
        flops=2 * total * D * 3 * width,
        nbytes=2 * (total * D + D * 3 * width),
        name="project",
    )(ids, mask_rows, *normed, *[pieces[slot] for slot in slots], bias)

    returned = [swap(block, "seq", k + 1) for k, block in enumerate(away)]

    mine = call(
        functools.partial(own_kernel, strips),
        strip_out,
        [SMEM, SMEM] + [VMEM] * 3,
        work,
        flops=4 * length * total * width,
        nbytes=4 * total * width,
        name="own_strip",
    )(ids, mask_rows, query, key, value)

    out_slots = sorted(out_pieces)
    updated, context = call(
        functools.partial(output_kernel, strips, out_slots),
        [jax.ShapeDtypeStruct((length, D), jnp.bfloat16)] * 2,
        [SMEM] + [VMEM] * (strips + len(out_slots) + 2),
        [pltpu.VMEM((D, D), jnp.bfloat16)],
        flops=2 * length * D * D,
        nbytes=2 * D * D,
        name="output",
    )(
        ids,
        mine,
        *returned,
        *[out_pieces[slot] for slot in out_slots],
        sheet,
        out_bias[None],
    )
    return (updated[None], context[None])


def solution(mesh):
    placed = (
        P("dp", "seq", None),
        P("dp", "seq", None),
        P(),
        P(),
        P("dp", None),
        P(),
        P("dp", None),
        P(),
    )
    return jax.shard_map(
        on_device,
        mesh=mesh,
        in_specs=placed,
        out_specs=(P("dp", "seq", None), P("dp", "seq", None)),
        check_vma=False,
    )
```

time: 143 us -> 115 us (0.80)
  waiting for transfers between devices: 83.7 us -> 49.3 us
  Pallas kernels: 0 us -> 29.4 us
  matrix products: 20.8 us -> 0 us
  starting transfers between devices: 1.55 us -> 22 us
  between operations: 15.4 us -> 0.83 us
  other arithmetic: 13.3 us -> 1.19 us
  local copies, waits for them, and re-layouts: 7.86 us -> 11.9 us
    all_gather x2 -> x0, waiting for transfers between devices: 63.4 us -> none  [the longest x1 63.4 us: on_device(): lax.all_gather(w_qkv, 'dp', axis=0, tiled=True)]
    ppermute x1 -> x26, waiting for transfers between devices: 18.9 us -> 49.3 us  [swap(): return lax.ppermute(block, axis, [(i, i ^ distance) for i in range(size)])]
    pallas_call x0 -> x5, Pallas kernels: none -> 29.4 us  [the longest x1 11.6 us: on_device(): call(functools.partial(project_kernel, strips, slots), [strip_out] * (str...]
    dot_general x8 -> x0, matrix products: 20.8 us -> none  [the longest x2 9.17 us: row_adder(): jnp.dot(left_operand, shard_piece, preferred_element_type=jnp.float32)]
    ppermute x1 -> x26, starting transfers between devices: 1.47 us -> 22 us  [swap(): return lax.ppermute(block, axis, [(i, i ^ distance) for i in range(size)])]
    reduce_sum x4 -> x0, other arithmetic: 7.38 us -> none  [the longest x2 4.59 us: update(): new_sum = run_sum * factor + jnp.sum(weights, axis=2)]
    unnamed x7 -> x63, local copies, waits for them, and re-layouts: 1.19 us -> 7.02 us
    another operation x4 -> x0, local copies, waits for them, and re-layouts: 3.83 us -> none
  transfers between devices with their start and end apart: 3 -> 26, of which waited for: 2 -> 8; matrix products, arithmetic and copies ran while one was open for 27% -> 9% of each run, Pallas kernels for 0% -> 22%
where the time goes in v1:
time: 115 us
  waiting for transfers between devices  49.3 us (43%)
  Pallas kernels  29.4 us (26%)
  starting transfers between devices  22 us (19%)
  local copies, waits for them, and re-layouts  11.9 us (10%)
  other arithmetic  1.19 us (1%)
    ppermute x26, waiting for transfers between devices, swap(): return lax.ppermute(block, axis, [(i, i ^ distance) for i in range(size)])  49.3 us
    ppermute x26, starting transfers between devices, swap(): return lax.ppermute(block, axis, [(i, i ^ distance) for i in range(size)])  22 us
    pallas_call x1, Pallas kernels, on_device(): call(functools.partial(project_kernel, strips, slots), [strip_out] * (str...  11.6 us
    unnamed x63, local copies, waits for them, and re-layouts  7.02 us
    pallas_call x2, Pallas kernels, on_device(): call(norm_kernel, jax.ShapeDtypeStruct((length, features), jnp.bfloat16),...  6.75 us
    pallas_call x1, Pallas kernels, on_device(): call(functools.partial(own_kernel, strips), strip_out, [SMEM, SMEM] + [VM...  6.44 us
    pallas_call x1, Pallas kernels, on_device(): call(functools.partial(output_kernel, strips, out_slots), [jax.ShapeDtype...  4.69 us
  transfers between devices with their start and end apart: 26, of which 8 were waited for; matrix products, arithmetic and copies ran while one was open for 9% of the time, Pallas kernels for 22%

profile of v1, /device:TPU:0, one launch (start us, length us, event | category | flops | bytes accessed | tf_op | source)
XLA Modules:
  0.0 114.7 jit_solution(9259124136911884154)
XLA Ops:
  0.6 3.1 %collective-permute-start.19 = (bf16[64,1024]{1,0:T(8,128)(2,1)}, bf16[64,1024]{1,0:T(8,128)(2,1)S(1)}, u32[]{:S(2)}, u32[]{:S(2)}) collective-permute-start(bf16[64,1024]{1,0:T(8,128)(2,1)} %refs_3_.1), channel_id=1, source_target_pairs={{0,8},{2,10},{4,12},{6,14},{8,0},{10,2},{12,4},{14,6},{16,24},{18,... | collective-permute-start | bytes 393224 | tf_op jit(solution)/shard_map/ppermute | solution.py:28
  3.7 1.5 %collective-permute-start.18 = (bf16[64,1024]{1,0:T(8,128)(2,1)}, bf16[64,1024]{1,0:T(8,128)(2,1)S(1)}, u32[]{:S(2)}, u32[]{:S(2)}) collective-permute-start(bf16[64,1024]{1,0:T(8,128)(2,1)} %refs_3_.1), channel_id=1, source_target_pairs={{0,4},{2,6},{4,0},{6,2},{8,12},{10,14},{12,8},{14,10},{16,20},{18,... | collective-permute-start | bytes 393224 | tf_op jit(solution)/shard_map/ppermute | solution.py:28
  5.2 1.3 %reshape.18 = bf16[64,3,2,512]{3,2,1,0:T(2,128)(2,1)S(1)} reshape(bf16[64,3072]{1,0:T(8,128)(2,1)} %param.12) | data formatting | bytes 786432 | tf_op jit(solution)/shard_map/reshape | solution.py:273
  6.5 1.3 %dynamic-slice_reduce_fusion = bf16[64,3,512]{2,1,0:T(4,128)(2,1)S(1)} fusion(bf16[64,3,2,512]{3,2,1,0:T(2,128)(2,1)S(1)} %reshape.18, s32[]{:T(128)S(6)} %select_n.6), kind=kLoop, calls=%fused_computation | loop fusion | bytes 393220 | tf_op jit(solution)/shard_map/jit(dynamic_index_in_dim)/dynamic_slice | solution.py:272
  7.9 2.7 %collective-permute-start.9 = (bf16[64,1536]{1,0:T(8,128)(2,1)S(1)}, bf16[64,1536]{1,0:T(8,128)(2,1)}, u32[]{:S(2)}, u32[]{:S(2)}) collective-permute-start(bf16[64,1536]{1,0:T(8,128)(2,1)S(1)} %bitcast.18), channel_id=1, source_target_pairs={{0,16},{2,18},{4,20},{6,22},{8,24},{10,26},{12,28},{14,30},{16,0},... | collective-permute-start | bytes 589832 | tf_op jit(solution)/shard_map/ppermute | solution.py:28
  10.8 1.7 %collective-permute-start.21 = (bf16[64,1024]{1,0:T(8,128)(2,1)S(1)}, bf16[64,1024]{1,0:T(8,128)(2,1)S(1)}, u32[]{:S(2)}, u32[]{:S(2)}) collective-permute-start(bf16[64,1024]{1,0:T(8,128)(2,1)S(1)} %copy-done.2), channel_id=1, source_target_pairs={{0,16},{2,18},{4,20},{6,22},{8,24},{10,26},{12,28},{14,30},{16,0},... | collective-permute-start | bytes 393224 | tf_op jit(solution)/shard_map/ppermute | solution.py:28
  13.1 1.9 %collective-permute-start.23 = (bf16[64,1024]{1,0:T(8,128)(2,1)S(1)}, bf16[64,1024]{1,0:T(8,128)(2,1)S(1)}, u32[]{:S(2)}, u32[]{:S(2)}) collective-permute-start(bf16[64,1024]{1,0:T(8,128)(2,1)S(1)} %copy-done.2), channel_id=1, source_target_pairs={{0,24},{2,26},{4,28},{6,30},{8,16},{10,18},{12,20},{14,22},{16,8},... | collective-permute-start | bytes 393224 | tf_op jit(solution)/shard_map/ppermute | solution.py:28
  16.9 19.1 %collective-permute-done.21.refs_11_ = bf16[64,1024]{1,0:T(8,128)(2,1)S(1)} collective-permute-done((bf16[64,1024]{1,0:T(8,128)(2,1)S(1)}, bf16[64,1024]{1,0:T(8,128)(2,1)S(1)}, u32[]{:S(2)}, u32[]{:S(2)}) %collective-permute-start.21) | collective-permute-done | bytes 131104 | tf_op jit(solution)/shard_map/ppermute | solution.py:28
  36.0 1.5 %collective-permute-start.1 = (bf16[384,1024]{1,0:T(8,128)(2,1)S(1)}, bf16[384,1024]{1,0:T(8,128)(2,1)S(1)}, u32[]{:S(2)}, u32[]{:S(2)}) collective-permute-start(bf16[384,1024]{1,0:T(8,128)(2,1)S(1)} %bitcast.16), channel_id=1, source_target_pairs={{0,1},{1,0},{2,3},{3,2},{4,5},{5,4},{6,7},{7,6},{8,9},{9,8},{10,11... | collective-permute-start | bytes 2359304 | tf_op jit(solution)/shard_map/ppermute | solution.py:28
  38.1 1.5 %collective-permute-start.24 = (bf16[64,1024]{1,0:T(8,128)(2,1)S(1)}, bf16[64,1024]{1,0:T(8,128)(2,1)S(1)}, u32[]{:S(2)}, u32[]{:S(2)}) collective-permute-start(bf16[64,1024]{1,0:T(8,128)(2,1)S(1)} %collective-permute-done.23.refs_15_), channel_id=1, source_target_pairs={{0,4},{2,6},{4,0},{6,2},{8,12},{10,14},{12,8},{14,10},{16,20},{18,... | collective-permute-start | bytes 393224 | tf_op jit(solution)/shard_map/ppermute | solution.py:28
  40.9 3.1 %collective-permute-done.22.refs_13_ = bf16[64,1024]{1,0:T(8,128)(2,1)S(1)} collective-permute-done((bf16[64,1024]{1,0:T(8,128)(2,1)S(1)}, bf16[64,1024]{1,0:T(8,128)(2,1)S(1)}, u32[]{:S(2)}, u32[]{:S(2)}) %collective-permute-start.22) | collective-permute-done | bytes 131104 | tf_op jit(solution)/shard_map/ppermute | solution.py:28
  45.1 10.3 %collective-permute-done = s32[3,6]{1,0:T(4,128)S(1)} collective-permute-done((s32[3,6]{1,0:T(4,128)S(1)}, s32[3,6]{1,0:T(4,128)S(1)}, u32[]{:S(2)}, u32[]{:S(2)}) %collective-permute-start) | collective-permute-done | bytes 104 | tf_op jit(solution)/shard_map/ppermute | solution.py:28
  57.8 3.5 %collective-permute-done.5.refs_8_ = bf16[64,1536]{1,0:T(8,128)(2,1)S(1)} collective-permute-done((bf16[64,1536]{1,0:T(8,128)(2,1)S(1)}, bf16[64,1536]{1,0:T(8,128)(2,1)S(1)}, u32[]{:S(2)}, u32[]{:S(2)}) %collective-permute-start.5) | collective-permute-done | bytes 196640 | tf_op jit(solution)/shard_map/ppermute | solution.py:28
  61.8 1.5 %collective-permute-start.15 = (bf16[64,1536]{1,0:T(8,128)(2,1)}, bf16[64,1536]{1,0:T(8,128)(2,1)S(1)}, u32[]{:S(2)}, u32[]{:S(2)}) collective-permute-start(bf16[64,1536]{1,0:T(8,128)(2,1)} %collective-permute-done.13.refs_16_), channel_id=1, source_target_pairs={{0,4},{2,6},{4,0},{6,2},{8,12},{10,14},{12,8},{14,10},{16,20},{18,... | collective-permute-start | bytes 589832 | tf_op jit(solution)/shard_map/ppermute | solution.py:28
  63.8 5.5 %collective-permute-done.11.refs_14_ = bf16[64,1536]{1,0:T(8,128)(2,1)S(1)} collective-permute-done((bf16[64,1536]{1,0:T(8,128)(2,1)}, bf16[64,1536]{1,0:T(8,128)(2,1)S(1)}, u32[]{:S(2)}, u32[]{:S(2)}) %collective-permute-start.11) | collective-permute-done | bytes 196640 | tf_op jit(solution)/shard_map/ppermute | solution.py:28
  69.3 3.4 %collective-permute-done.15.refs_18_ = bf16[64,1536]{1,0:T(8,128)(2,1)S(1)} collective-permute-done((bf16[64,1536]{1,0:T(8,128)(2,1)}, bf16[64,1536]{1,0:T(8,128)(2,1)S(1)}, u32[]{:S(2)}, u32[]{:S(2)}) %collective-permute-start.15) | collective-permute-done | bytes 196640 | tf_op jit(solution)/shard_map/ppermute | solution.py:28
  72.8 2.1 %collective-permute-done.7.refs_10_ = bf16[64,1536]{1,0:T(8,128)(2,1)S(1)} collective-permute-done((bf16[64,1536]{1,0:T(8,128)(2,1)S(1)}, bf16[64,1536]{1,0:T(8,128)(2,1)S(1)}, u32[]{:S(2)}, u32[]{:S(2)}) %collective-permute-start.7) | collective-permute-done | bytes 196640 | tf_op jit(solution)/shard_map/ppermute | solution.py:28
  75.6 3.4 %norm.2.refs_2_ = bf16[384,1024]{1,0:T(8,128)(2,1)} custom-call(bf16[384,1024]{1,0:T(8,128)(2,1)} %bitcast.14, f32[1,1024]{1,0:T(1,128)} %bitcast.24, f32[1,1024]{1,0:T(1,128)} %bitcast.26), custom_call_target="tpu_custom_call" | custom-call | flops 3932160 | bytes 1572864 | tf_op jit(solution)/shard_map/norm/pallas_call | solution.py:295
  82.0 3.3 %norm.3.refs_3_ = bf16[384,1024]{1,0:T(8,128)(2,1)} custom-call(bf16[384,1024]{1,0:T(8,128)(2,1)} %copy-done.1, f32[1,1024]{1,0:T(1,128)} %bitcast.25, f32[1,1024]{1,0:T(1,128)} %bitcast.27), custom_call_target="tpu_custom_call" | custom-call | flops 3932160 | bytes 1572864 | tf_op jit(solution)/shard_map/norm/pallas_call | solution.py:295
  86.2 11.6 %project.1 = (bf16[384,512]{1,0:T(8,128)(2,1)}, bf16[384,512]{1,0:T(8,128)(2,1)}, bf16[768,512]{1,0:T(8,128)(2,1)}, bf16[768,512]{1,0:T(8,128)(2,1)}) custom-call(s32[2]{0:T(128)} %pad_add_fusion.1.refs_0_.ids_ref, s32[2,3,6]{2,1,0:T(4,128)} %pad_add_fusion.refs_1_.masks_ref, bf16[384,1024]{1,0:T(8,128)(2,1)} %norm.2.refs_2_, ...), custom_call_target="tpu_custom_call" | custom-call | flops 2415919104 | bytes 4718592 | tf_op jit(solution)/shard_map/project/pallas_call | solution.py:313
  97.8 1.6 %collective-permute-start.17 = (bf16[384,512]{1,0:T(8,128)(2,1)}, bf16[384,512]{1,0:T(8,128)(2,1)S(1)}, u32[]{:S(2)}, u32[]{:S(2)}) collective-permute-start(bf16[384,512]{1,0:T(8,128)(2,1)} %get-tuple-element.11), channel_id=1, source_target_pairs={{0,1},{1,0},{2,3},{3,2},{4,5},{5,4},{6,7},{7,6},{8,9},{9,8},{10,11... | collective-permute-start | bytes 1179656 | tf_op jit(solution)/shard_map/ppermute | solution.py:28
  99.4 6.4 %own_strip.1.refs_1_ = bf16[384,512]{1,0:T(8,128)(2,1)} custom-call(s32[2]{0:T(128)} %pad_add_fusion.1.refs_0_.ids_ref, s32[2,3,6]{2,1,0:T(4,128)} %pad_add_fusion.refs_1_.masks_ref, bf16[384,512]{1,0:T(8,128)(2,1)} %get-tuple-element.8.query_ref, bf16[768,512]{1,0:T(8,128)(2,1)} %get-tuple-element.9.key_ref, bf16[768,512]{1,0:T(8,128)(2,1)} %get-tuple-element.10.value_ref), custom_call_target="tpu_custom_call" | custom-call | flops 603979776 | bytes 1572864 | tf_op jit(solution)/shard_map/own_strip/pallas_call | solution.py:329
  106.9 2.4 %collective-permute-done.17.refs_2_ = bf16[384,512]{1,0:T(8,128)(2,1)S(1)} collective-permute-done((bf16[384,512]{1,0:T(8,128)(2,1)}, bf16[384,512]{1,0:T(8,128)(2,1)S(1)}, u32[]{:S(2)}, u32[]{:S(2)}) %collective-permute-start.17) | collective-permute-done | bytes 393248 | tf_op jit(solution)/shard_map/ppermute | solution.py:28
  110.0 4.7 %output.1 = (bf16[384,1024]{1,0:T(8,128)(2,1)}, bf16[384,1024]{1,0:T(8,128)(2,1)}) custom-call(s32[2]{0:T(128)} %pad_add_fusion.1.refs_0_.ids_ref, bf16[384,512]{1,0:T(8,128)(2,1)} %own_strip.1.refs_1_, bf16[384,512]{1,0:T(8,128)(2,1)} %copy-done.10, bf16[64,1024]{1,0:T(8,128)(2,1)} %refs_3_.1, bf16[64,1024]{1,0:T(8,128)(2,1)} %get-tuple-element.21.refs_4_, ...), custom_call_target="tpu_custom_call" | custom-call | flops 805306368 | bytes 2097152 | tf_op jit(solution)/shard_map/output/pallas_call | solution.py:340
  (104 shorter events, 15.6 us)
Async XLA Ops:
  0.6 12.5 %collective-permute-start.19 = (bf16[64,1024]{1,0:T(8,128)(2,1)}, bf16[64,1024]{1,0:T(8,128)(2,1)S(1)}, u32[]{:S(2)}, u32[]{:S(2)}) collective-permute-start(bf16[64,1024]{1,0:T(8,128)(2,1)} %refs_3_.1), channel_id=1, source_target_pairs={{0,8},{2,10},{4,12},{6,14},{8,0},{10,2},{12,4},{14,6},{16,24},{18,... | collective-permute-start | bytes 393224 | tf_op jit(solution)/shard_map/ppermute | solution.py:28
  3.7 11.3 %collective-permute-start.18 = (bf16[64,1024]{1,0:T(8,128)(2,1)}, bf16[64,1024]{1,0:T(8,128)(2,1)S(1)}, u32[]{:S(2)}, u32[]{:S(2)}) collective-permute-start(bf16[64,1024]{1,0:T(8,128)(2,1)} %refs_3_.1), channel_id=1, source_target_pairs={{0,4},{2,6},{4,0},{6,2},{8,12},{10,14},{12,8},{14,10},{16,20},{18,... | collective-permute-start | bytes 393224 | tf_op jit(solution)/shard_map/ppermute | solution.py:28
  7.9 47.5 %collective-permute-start.9 = (bf16[64,1536]{1,0:T(8,128)(2,1)S(1)}, bf16[64,1536]{1,0:T(8,128)(2,1)}, u32[]{:S(2)}, u32[]{:S(2)}) collective-permute-start(bf16[64,1536]{1,0:T(8,128)(2,1)S(1)} %bitcast.18), channel_id=1, source_target_pairs={{0,16},{2,18},{4,20},{6,22},{8,24},{10,26},{12,28},{14,30},{16,0},... | collective-permute-start | bytes 589832 | tf_op jit(solution)/shard_map/ppermute | solution.py:28
  10.5 46.8 %collective-permute-start.13 = (bf16[64,1536]{1,0:T(8,128)(2,1)S(1)}, bf16[64,1536]{1,0:T(8,128)(2,1)}, u32[]{:S(2)}, u32[]{:S(2)}) collective-permute-start(bf16[64,1536]{1,0:T(8,128)(2,1)S(1)} %bitcast.19), channel_id=1, source_target_pairs={{0,24},{2,26},{4,28},{6,30},{8,16},{10,18},{12,20},{14,22},{16,8},... | collective-permute-start | bytes 589832 | tf_op jit(solution)/shard_map/ppermute | solution.py:28
  10.8 25.2 %collective-permute-start.21 = (bf16[64,1024]{1,0:T(8,128)(2,1)S(1)}, bf16[64,1024]{1,0:T(8,128)(2,1)S(1)}, u32[]{:S(2)}, u32[]{:S(2)}) collective-permute-start(bf16[64,1024]{1,0:T(8,128)(2,1)S(1)} %copy-done.2), channel_id=1, source_target_pairs={{0,16},{2,18},{4,20},{6,22},{8,24},{10,26},{12,28},{14,30},{16,0},... | collective-permute-start | bytes 393224 | tf_op jit(solution)/shard_map/ppermute | solution.py:28
  13.1 24.4 %collective-permute-start.23 = (bf16[64,1024]{1,0:T(8,128)(2,1)S(1)}, bf16[64,1024]{1,0:T(8,128)(2,1)S(1)}, u32[]{:S(2)}, u32[]{:S(2)}) collective-permute-start(bf16[64,1024]{1,0:T(8,128)(2,1)S(1)} %copy-done.2), channel_id=1, source_target_pairs={{0,24},{2,26},{4,28},{6,30},{8,16},{10,18},{12,20},{14,22},{16,8},... | collective-permute-start | bytes 393224 | tf_op jit(solution)/shard_map/ppermute | solution.py:28
  15.1 23.0 %collective-permute-start.20 = (bf16[64,1024]{1,0:T(8,128)(2,1)S(1)}, bf16[64,1024]{1,0:T(8,128)(2,1)S(1)}, u32[]{:S(2)}, u32[]{:S(2)}) collective-permute-start(bf16[64,1024]{1,0:T(8,128)(2,1)S(1)} %collective-permute-done.19.refs_7_), channel_id=1, source_target_pairs={{0,4},{2,6},{4,0},{6,2},{8,12},{10,14},{12,8},{14,10},{16,20},{18,... | collective-permute-start | bytes 393224 | tf_op jit(solution)/shard_map/ppermute | solution.py:28
  36.0 44.7 %collective-permute-start.1 = (bf16[384,1024]{1,0:T(8,128)(2,1)S(1)}, bf16[384,1024]{1,0:T(8,128)(2,1)S(1)}, u32[]{:S(2)}, u32[]{:S(2)}) collective-permute-start(bf16[384,1024]{1,0:T(8,128)(2,1)S(1)} %bitcast.16), channel_id=1, source_target_pairs={{0,1},{1,0},{2,3},{3,2},{4,5},{5,4},{6,7},{7,6},{8,9},{9,8},{10,11... | collective-permute-start | bytes 2359304 | tf_op jit(solution)/shard_map/ppermute | solution.py:28
  37.5 6.4 %collective-permute-start.22 = (bf16[64,1024]{1,0:T(8,128)(2,1)S(1)}, bf16[64,1024]{1,0:T(8,128)(2,1)S(1)}, u32[]{:S(2)}, u32[]{:S(2)}) collective-permute-start(bf16[64,1024]{1,0:T(8,128)(2,1)S(1)} %collective-permute-done.21.refs_11_), channel_id=1, source_target_pairs={{0,4},{2,6},{4,0},{6,2},{8,12},{10,14},{12,8},{14,10},{16,20},{18,... | collective-permute-start | bytes 393224 | tf_op jit(solution)/shard_map/ppermute | solution.py:28
  38.1 17.9 %collective-permute-start.24 = (bf16[64,1024]{1,0:T(8,128)(2,1)S(1)}, bf16[64,1024]{1,0:T(8,128)(2,1)S(1)}, u32[]{:S(2)}, u32[]{:S(2)}) collective-permute-start(bf16[64,1024]{1,0:T(8,128)(2,1)S(1)} %collective-permute-done.23.refs_15_), channel_id=1, source_target_pairs={{0,4},{2,6},{4,0},{6,2},{8,12},{10,14},{12,8},{14,10},{16,20},{18,... | collective-permute-start | bytes 393224 | tf_op jit(solution)/shard_map/ppermute | solution.py:28
  43.9 11.5 %collective-permute-start = (s32[3,6]{1,0:T(4,128)S(1)}, s32[3,6]{1,0:T(4,128)S(1)}, u32[]{:S(2)}, u32[]{:S(2)}) collective-permute-start(s32[3,6]{1,0:T(4,128)S(1)} %bitcast.28), channel_id=1, source_target_pairs={{0,1},{1,0},{2,3},{3,2},{4,5},{5,4},{6,7},{7,6},{8,9},{9,8},{10,11... | collective-permute-start | bytes 224 | tf_op jit(solution)/shard_map/ppermute | solution.py:28
  55.4 5.9 %collective-permute-start.5 = (bf16[64,1536]{1,0:T(8,128)(2,1)S(1)}, bf16[64,1536]{1,0:T(8,128)(2,1)S(1)}, u32[]{:S(2)}, u32[]{:S(2)}) collective-permute-start(bf16[64,1536]{1,0:T(8,128)(2,1)S(1)} %bitcast.20), channel_id=1, source_target_pairs={{0,8},{2,10},{4,12},{6,14},{8,0},{10,2},{12,4},{14,6},{16,24},{18,... | collective-permute-start | bytes 589832 | tf_op jit(solution)/shard_map/ppermute | solution.py:28
  55.4 6.4 %collective-permute-start.3 = (bf16[64,1536]{1,0:T(8,128)(2,1)S(1)}, bf16[64,1536]{1,0:T(8,128)(2,1)S(1)}, u32[]{:S(2)}, u32[]{:S(2)}) collective-permute-start(bf16[64,1536]{1,0:T(8,128)(2,1)S(1)} %bitcast.21), channel_id=1, source_target_pairs={{0,4},{2,6},{4,0},{6,2},{8,12},{10,14},{12,8},{14,10},{16,20},{18,... | collective-permute-start | bytes 589832 | tf_op jit(solution)/shard_map/ppermute | solution.py:28
  55.9 7.4 %collective-permute-start.2 = (bf16[64,1536]{1,0:T(8,128)(2,1)S(1)}, bf16[64,1536]{1,0:T(8,128)(2,1)S(1)}, u32[]{:S(2)}, u32[]{:S(2)}) collective-permute-start(bf16[64,1536]{1,0:T(8,128)(2,1)S(1)} %bitcast.22), channel_id=1, source_target_pairs={{0,2},{2,0},{4,6},{6,4},{8,10},{10,8},{12,14},{14,12},{16,18},{18,... | collective-permute-start | bytes 589832 | tf_op jit(solution)/shard_map/ppermute | solution.py:28
  57.3 48.5 %collective-permute-start.25 = (bf16[512,1024]{1,0:T(8,128)(2,1)}, bf16[512,1024]{1,0:T(8,128)(2,1)S(1)}, u32[]{:S(2)}, u32[]{:S(2)}) collective-permute-start(bf16[512,1024]{1,0:T(8,128)(2,1)} %constant_dynamic-update-slice_fusion), channel_id=1, source_target_pairs={{0,2},{2,0},{4,6},{6,4},{8,10},{10,8},{12,14},{14,12},{16,18},{18,... | collective-permute-start | bytes 3145736 | tf_op jit(solution)/shard_map/ppermute | solution.py:28
  61.3 8.0 %collective-permute-start.11 = (bf16[64,1536]{1,0:T(8,128)(2,1)}, bf16[64,1536]{1,0:T(8,128)(2,1)S(1)}, u32[]{:S(2)}, u32[]{:S(2)}) collective-permute-start(bf16[64,1536]{1,0:T(8,128)(2,1)} %collective-permute-done.9.refs_12_), channel_id=1, source_target_pairs={{0,4},{2,6},{4,0},{6,2},{8,12},{10,14},{12,8},{14,10},{16,20},{18,... | collective-permute-start | bytes 589832 | tf_op jit(solution)/shard_map/ppermute | solution.py:28
  61.8 11.0 %collective-permute-start.15 = (bf16[64,1536]{1,0:T(8,128)(2,1)}, bf16[64,1536]{1,0:T(8,128)(2,1)S(1)}, u32[]{:S(2)}, u32[]{:S(2)}) collective-permute-start(bf16[64,1536]{1,0:T(8,128)(2,1)} %collective-permute-done.13.refs_16_), channel_id=1, source_target_pairs={{0,4},{2,6},{4,0},{6,2},{8,12},{10,14},{12,8},{14,10},{16,20},{18,... | collective-permute-start | bytes 589832 | tf_op jit(solution)/shard_map/ppermute | solution.py:28
  63.3 11.5 %collective-permute-start.7 = (bf16[64,1536]{1,0:T(8,128)(2,1)S(1)}, bf16[64,1536]{1,0:T(8,128)(2,1)S(1)}, u32[]{:S(2)}, u32[]{:S(2)}) collective-permute-start(bf16[64,1536]{1,0:T(8,128)(2,1)S(1)} %collective-permute-done.5.refs_8_), channel_id=1, source_target_pairs={{0,4},{2,6},{4,0},{6,2},{8,12},{10,14},{12,8},{14,10},{16,20},{18,... | collective-permute-start | bytes 589832 | tf_op jit(solution)/shard_map/ppermute | solution.py:28
  69.3 10.3 %collective-permute-start.10 = (bf16[64,1536]{1,0:T(8,128)(2,1)}, bf16[64,1536]{1,0:T(8,128)(2,1)}, u32[]{:S(2)}, u32[]{:S(2)}) collective-permute-start(bf16[64,1536]{1,0:T(8,128)(2,1)} %collective-permute-done.9.refs_12_), channel_id=1, source_target_pairs={{0,2},{2,0},{4,6},{6,4},{8,10},{10,8},{12,14},{14,12},{16,18},{18,... | collective-permute-start | bytes 589832 | tf_op jit(solution)/shard_map/ppermute | solution.py:28
  72.8 7.4 %collective-permute-start.14 = (bf16[64,1536]{1,0:T(8,128)(2,1)}, bf16[64,1536]{1,0:T(8,128)(2,1)}, u32[]{:S(2)}, u32[]{:S(2)}) collective-permute-start(bf16[64,1536]{1,0:T(8,128)(2,1)} %collective-permute-done.13.refs_16_), channel_id=1, source_target_pairs={{0,2},{2,0},{4,6},{6,4},{8,10},{10,8},{12,14},{14,12},{16,18},{18,... | collective-permute-start | bytes 589832 | tf_op jit(solution)/shard_map/ppermute | solution.py:28
  79.6 5.7 %collective-permute-start.4 = (bf16[64,1536]{1,0:T(8,128)(2,1)S(1)}, bf16[64,1536]{1,0:T(8,128)(2,1)S(1)}, u32[]{:S(2)}, u32[]{:S(2)}) collective-permute-start(bf16[64,1536]{1,0:T(8,128)(2,1)S(1)} %copy-done.16), channel_id=1, source_target_pairs={{0,2},{2,0},{4,6},{6,4},{8,10},{10,8},{12,14},{14,12},{16,18},{18,... | collective-permute-start | bytes 589832 | tf_op jit(solution)/shard_map/ppermute | solution.py:28
  80.1 5.2 %collective-permute-start.12 = (bf16[64,1536]{1,0:T(8,128)(2,1)S(1)}, bf16[64,1536]{1,0:T(8,128)(2,1)S(1)}, u32[]{:S(2)}, u32[]{:S(2)}) collective-permute-start(bf16[64,1536]{1,0:T(8,128)(2,1)S(1)} %collective-permute-done.11.refs_14_), channel_id=1, source_target_pairs={{0,2},{2,0},{4,6},{6,4},{8,10},{10,8},{12,14},{14,12},{16,18},{18,... | collective-permute-start | bytes 589832 | tf_op jit(solution)/shard_map/ppermute | solution.py:28
  80.2 5.1 %collective-permute-start.16 = (bf16[64,1536]{1,0:T(8,128)(2,1)S(1)}, bf16[64,1536]{1,0:T(8,128)(2,1)S(1)}, u32[]{:S(2)}, u32[]{:S(2)}) collective-permute-start(bf16[64,1536]{1,0:T(8,128)(2,1)S(1)} %copy-done.20), channel_id=1, source_target_pairs={{0,2},{2,0},{4,6},{6,4},{8,10},{10,8},{12,14},{14,12},{16,18},{18,... | collective-permute-start | bytes 589832 | tf_op jit(solution)/shard_map/ppermute | solution.py:28
  97.8 11.5 %collective-permute-start.17 = (bf16[384,512]{1,0:T(8,128)(2,1)}, bf16[384,512]{1,0:T(8,128)(2,1)S(1)}, u32[]{:S(2)}, u32[]{:S(2)}) collective-permute-start(bf16[384,512]{1,0:T(8,128)(2,1)} %get-tuple-element.11), channel_id=1, source_target_pairs={{0,1},{1,0},{2,3},{3,2},{4,5},{5,4},{6,7},{7,6},{8,9},{9,8},{10,11... | collective-permute-start | bytes 1179656 | tf_op jit(solution)/shard_map/ppermute | solution.py:28
  (29 other events, 226.3 us)

commit v2 on v1

v2 whole, which is shorter than its diff:
```python
import functools

import jax
import jax.numpy as jnp
from jax import lax
from jax.experimental import pallas as pl
from jax.experimental.pallas import tpu as pltpu
from jax.sharding import PartitionSpec as P

D = 1024
HEADS = 16
BLOCK = 128
HEAD_DIM = D // HEADS
PAIR = 2 * HEAD_DIM

NEG_FILL = -1e30
EPSILON = 1e-06
VMEM_LIMIT = 24 * 1024 * 1024

VMEM = pl.BlockSpec(memory_space=pltpu.VMEM)
SMEM = pl.BlockSpec(memory_space=pltpu.SMEM)


def swap(block, axis, distance):
    if distance == 0:
        return block
    size = lax.axis_size(axis)
    return lax.ppermute(block, axis, [(i, i ^ distance) for i in range(size)])


def call(kernel, out_shape, in_specs, scratch=(), flops=0, nbytes=0, name=None):
    many = isinstance(out_shape, (list, tuple))
    return pl.pallas_call(
        kernel,
        out_shape=out_shape,
        in_specs=in_specs,
        out_specs=[VMEM] * len(out_shape) if many else VMEM,
        scratch_shapes=scratch,
        compiler_params=pltpu.CompilerParams(vmem_limit_bytes=VMEM_LIMIT),
        cost_estimate=pl.CostEstimate(
            flops=flops, bytes_accessed=nbytes, transcendentals=0
        ),
        name=name,
    )


def norm_kernel(sheet_ref, gain_ref, bias_ref, out_ref):
    step = 32

    @pl.loop(0, sheet_ref.shape[0] // step, unroll=4)
    def _(index):
        rows = pl.ds(pl.multiple_of(index * step, step), step)
        values = sheet_ref[rows, :].astype(jnp.float32)
        center = jnp.mean(values, axis=-1, keepdims=True)
        moved = values - center
        spread = jnp.mean(jnp.square(moved), axis=-1, keepdims=True)
        normed = moved * lax.rsqrt(spread + EPSILON)
        out_ref[rows, :] = (normed * gain_ref[...] + bias_ref[...]).astype(jnp.bfloat16)


def gather_rows(pieces, target):
    here = lax.axis_index("dp")
    for slots, piece in pieces:
        rows = piece.shape[0] // len(slots)
        for index, slot in enumerate(slots):
            first = pl.multiple_of((here ^ slot) * rows, rows)
            target[pl.ds(first, rows), :] = piece[pl.ds(index * rows, rows), :]


def attend_strip(query_ref, first_row, mask_ref, out_ref, strips, key_ref, value_ref, scores, weights):
    seat = lax.axis_index("seq")
    per_strip = out_ref.shape[0] // BLOCK
    blocks = strips * per_strip
    pairs = key_ref.shape[1] // PAIR
    low = lax.broadcasted_iota(jnp.int32, (BLOCK, PAIR), 1) < HEAD_DIM

    @pl.loop(0, per_strip)
    def _(index):
        rows = pl.ds(pl.multiple_of(index * BLOCK, BLOCK), BLOCK)
        source = pl.ds(pl.multiple_of(first_row + index * BLOCK, BLOCK), BLOCK)

        def allowed(block):
            column = (seat ^ (block // per_strip)) * per_strip + block % per_strip
            return mask_ref[index, column] == 1

        stacked = []
        for pair in range(pairs):
            both = query_ref[source, pl.ds(pair * PAIR, PAIR)]
            zero = jnp.zeros_like(both)
            stacked.append(
                jnp.concatenate(
                    [jnp.where(low, both, zero), jnp.where(low, zero, both)], axis=0
                )
            )

        def score(block, tops):
            keys = pl.ds(pl.multiple_of(block * BLOCK, BLOCK), BLOCK)

            def found():
                risen = []
                for pair in range(pairs):
                    result = lax.dot_general(
                        key_ref[keys, pl.ds(pair * PAIR, PAIR)],
                        stacked[pair],
                        (((1,), (1,)), ((), ())),
                        preferred_element_type=jnp.float32,
                    )
                    scores[pair, keys, :] = result
                    folded = jnp.max(result.reshape(BLOCK // 8, 8, 2 * BLOCK), axis=0)
                    risen.append(jnp.maximum(tops[pair], folded))
                return tuple(risen)

            return lax.cond(allowed(block), found, lambda: tops)

        start = tuple(jnp.full((8, 2 * BLOCK), NEG_FILL, jnp.float32) for _ in range(pairs))
        tops = lax.fori_loop(0, blocks, score, start)
        tops = [jnp.max(top, axis=0, keepdims=True) for top in tops]

        @pl.loop(0, blocks)
        def _(block):
            keys = pl.ds(pl.multiple_of(block * BLOCK, BLOCK), BLOCK)
            active = allowed(block)

            @pl.when(active)
            def _():
                for pair in range(pairs):
                    weights[pair, keys, :] = jnp.exp(
                        scores[pair, keys, :] - tops[pair]
                    ).astype(jnp.bfloat16)

            @pl.when(jnp.logical_not(active))
            def _():
                for pair in range(pairs):
                    weights[pair, keys, :] = jnp.zeros((BLOCK, 2 * BLOCK), jnp.bfloat16)

        for pair in range(pairs):
            mixed = jnp.dot(
                value_ref[pair], weights[pair], preferred_element_type=jnp.float32
            )
            mixed = mixed[:PAIR] / mixed[PAIR : PAIR + 1]
            both = jnp.concatenate(
                [mixed[:HEAD_DIM, :BLOCK], mixed[HEAD_DIM:, BLOCK:]], axis=0
            )
            out_ref[rows, pl.ds(pair * PAIR, PAIR)] = both.T.astype(jnp.bfloat16)


def project_kernel(strips, slots, *refs):
    masks = refs[: strips - 1]
    normed = refs[strips - 1 : 2 * strips - 1]
    pieces = refs[2 * strips - 1 : 2 * strips - 1 + len(slots)]
    bias_ref, *rest = refs[2 * strips - 1 + len(slots) :]
    away, rest = rest[: strips - 1], rest[strips - 1 :]
    query_ref, key_ref, value_ref, weight, queries, scores, weights = rest
    seat = lax.axis_index("seq")
    gather_rows(list(zip(slots, pieces)), weight)
    length = normed[0].shape[0]
    width = key_ref.shape[1]
    step = PAIR * 2 if width % (PAIR * 2) == 0 else PAIR
    value_ref[:, PAIR:, :] = jnp.ones((width // PAIR, 16, length * strips), jnp.bfloat16)
    for kind in range(3):
        for first in range(0, width, step):
            lanes = pl.ds(kind * width + first, step)
            bias = bias_ref[:, pl.ds(pl.multiple_of(kind * D + seat * width + first, PAIR), step)]
            for strip in range(strips):
                found = jnp.dot(
                    normed[strip][...],
                    weight[:, lanes],
                    preferred_element_type=jnp.float32,
                )
                found = found + bias
                rows = pl.ds(strip * length, length)
                out = pl.ds(first, step)
                if kind == 0:
                    found = (found * HEAD_DIM**-0.5).astype(jnp.bfloat16)
                    if strip == 0:
                        query_ref[:, out] = found
                    else:
                        queries[pl.ds((strip - 1) * length, length), out] = found
                elif kind == 1:
                    key_ref[rows, out] = found.astype(jnp.bfloat16)
                else:
                    turned = found.T.astype(jnp.bfloat16)
                    for offset in range(0, step, PAIR):
                        value_ref[(first + offset) // PAIR, :PAIR, rows] = turned[
                            offset : offset + PAIR
                        ]

    for strip in range(1, strips):
        attend_strip(
            queries,
            (strip - 1) * length,
            masks[strip - 1],
            away[strip - 1],
            strips,
            key_ref,
            value_ref,
            scores,
            weights,
        )


def own_kernel(strips, mask_ref, query_ref, key_ref, value_ref, out_ref, scores, weights):
    attend_strip(
        query_ref, 0, mask_ref, out_ref, strips, key_ref, value_ref, scores, weights
    )


def output_kernel(strips, slots, *refs):
    parts = refs[:strips]
    pieces = refs[strips : strips + len(slots)]
    sheet_ref, bias_ref, updated_ref, context_ref, weight = refs[strips + len(slots) :]
    seat = lax.axis_index("seq")
    gather_rows(list(zip(slots, pieces)), weight)
    width = parts[0].shape[1]
    for strip, part in enumerate(parts):
        first = pl.multiple_of((seat ^ strip) * width, width)
        context_ref[:, pl.ds(first, width)] = part[...]
    step = 256
    for first in range(0, updated_ref.shape[1], step):
        lanes = pl.ds(first, step)
        found = jnp.dot(
            context_ref[...], weight[:, lanes], preferred_element_type=jnp.float32
        )
        found = sheet_ref[:, lanes].astype(jnp.float32) + found + bias_ref[:, lanes]
        updated_ref[:, lanes] = found.astype(jnp.bfloat16)


def after(block, *others):
    return lax.optimization_barrier((block, *others))[0]


def after_all(blocks, *others):
    return lax.optimization_barrier((*blocks, *others))[: len(blocks)]


def spread_far(own, size):
    along_x = size // 8
    pieces = {0: own}
    for x in range(1, along_x):
        pieces[2 * x] = swap(own, "dp", 2 * x)
    for z in (1, 3):
        pieces[2 * along_x * z] = swap(own, "dp", 2 * along_x * z)
    pieces[4 * along_x] = swap(pieces[6 * along_x], "dp", 2 * along_x)
    return pieces


def spread_near(pieces, size, awaited=()):
    along_x = size // 8
    pieces = dict(pieces)
    for z in (1, 3, 2):
        far = 2 * along_x * z
        piece = pieces[far]
        if z == 2 and awaited:
            piece = after(piece, *awaited)
        for x in range(1, along_x):
            pieces[far + 2 * x] = swap(piece, "dp", 2 * x)
    return pieces


def on_device(tokens, masks, ln_gain, ln_bias, w_qkv, qkv_bias, w_out, out_bias):
    size, strips = lax.axis_size("dp"), lax.axis_size("seq")
    seat = lax.axis_index("seq")
    sheet = tokens[0]
    length, features = sheet.shape
    width = D // strips
    total = length * strips
    blocks = total // BLOCK
    pairs = width // PAIR
    rows = w_qkv.shape[0]

    def mine_of(array):
        starts = [kind * D + seat * width for kind in range(3)]
        return jnp.concatenate(
            [lax.dynamic_slice_in_dim(array, start, width, 1) for start in starts], axis=1
        )

    own = mine_of(w_qkv)

    sheets = [swap(sheet, "seq", k) for k in range(strips)]
    normed = [
        call(
            norm_kernel,
            jax.ShapeDtypeStruct((length, features), jnp.bfloat16),
            [VMEM] * 3,
            flops=10 * length * features,
            nbytes=4 * length * features,
            name="norm",
        )(block, ln_gain[None], ln_bias[None])
        for block in sheets
    ]

    along_x = size // 8
    first, second, third = 2 * along_x, 6 * along_x, 4 * along_x
    pieces = spread_near(spread_far(own, size), size)
    for slot in sorted(pieces):
        pieces[slot + 1] = swap(pieces[slot], "dp", 1)
    slots = sorted(pieces)
    mask_rows = [
        swap(after(masks[0], pieces[first]) if k else masks[0], "seq", k)
        for k in range(strips)
    ]

    beside = [after(w_out, pieces[first])]
    for x in range(1, along_x):
        beside.append(swap(beside[0], "dp", 2 * x))
    early = [0, 2, first, second, first + 2]
    early = early + [slot + 1 for slot in early] + [third, second + 2]
    out_own = jnp.concatenate(beside, axis=0)
    out_ready = after(out_own, *sheets[1:], *[pieces[slot] for slot in early])
    out_first, out_second = swap(out_ready, "dp", first), swap(out_ready, "dp", second)

    work = [
        pltpu.VMEM((pairs, total, 2 * BLOCK), jnp.float32),
        pltpu.VMEM((pairs, total, 2 * BLOCK), jnp.bfloat16),
    ]
    strip_out = jax.ShapeDtypeStruct((length, width), jnp.bfloat16)
    *away, query, key, value = call(
        functools.partial(project_kernel, strips, [[slot] for slot in slots]),
        [strip_out] * (strips - 1)
        + [
            strip_out,
            jax.ShapeDtypeStruct((total, width), jnp.bfloat16),
            jax.ShapeDtypeStruct((pairs, PAIR + 16, total), jnp.bfloat16),
        ],
        [SMEM] * (strips - 1) + [VMEM] * (strips + len(slots) + 1),
        [
            pltpu.VMEM((D, 3 * width), jnp.bfloat16),
            pltpu.VMEM((total - length, width), jnp.bfloat16),
        ]
        + work,
        name="project",
    )(*mask_rows[1:], *normed, *[pieces[slot] for slot in slots], qkv_bias[None])

    returned = [swap(block, "seq", k + 1) for k, block in enumerate(away)]
    mine = call(
        functools.partial(own_kernel, strips),
        strip_out,
        [SMEM] + [VMEM] * 3,
        work,
        flops=10**10,
        name="own_strip",
    )(mask_rows[0], query, key, value)

    out_third = swap(after(out_second, *away), "dp", first)
    out_slots, out_pieces = [], []
    for far, piece in ((0, out_own), (first, out_first), (second, out_second), (third, out_third)):
        for core in range(2):
            if core:
                piece = swap(after(piece, mine) if far == third else piece, "dp", 1)
            out_slots.append([far + core + 2 * x for x in range(along_x)])
            out_pieces.append(piece)

    updated, context = call(
        functools.partial(output_kernel, strips, out_slots),
        [jax.ShapeDtypeStruct((length, D), jnp.bfloat16)] * 2,
        [VMEM] * (strips + len(out_slots) + 2),
        [pltpu.VMEM((D, D), jnp.bfloat16)],
        flops=2 * length * D * D,
        nbytes=2 * D * D,
        name="output",
    )(
        mine,
        *returned,
        *out_pieces,
        sheet,
        out_bias[None],
    )
    return (updated[None], context[None])


def solution(mesh):
    placed = (
        P("dp", "seq", None),
        P("dp", "seq", None),
        P(),
        P(),
        P("dp", None),
        P(),
        P("dp", None),
        P(),
    )
    return jax.shard_map(
        on_device,
        mesh=mesh,
        in_specs=placed,
        out_specs=(P("dp", "seq", None), P("dp", "seq", None)),
        check_vma=False,
    )
```

time: 115 us -> 60.4 us (0.53)
  waiting for transfers between devices: 49.3 us -> 19.2 us
  Pallas kernels: 29.4 us -> 15.4 us
  local copies, waits for them, and re-layouts: 11.9 us -> 1.87 us
  other arithmetic: 1.19 us -> 0.02 us
    ppermute x26, waiting for transfers between devices: 49.3 us -> 19.2 us  [swap(): return lax.ppermute(block, axis, [(i, i ^ distance) for i in range(size)])]
    pallas_call x2, Pallas kernels: 18 us -> 11.8 us  [the longest x1 7.35 us: on_device(): call(functools.partial(project_kernel, strips, [[slot] for slot in slots]...]
    unnamed x63 -> x14, local copies, waits for them, and re-layouts: 7.02 us -> 0.95 us
    pallas_call x2, Pallas kernels: 6.75 us -> 1.6 us  [on_device(): call(norm_kernel, jax.ShapeDtypeStruct((length, features), jnp.bfloat16),...]
    pallas_call x1, Pallas kernels: 4.69 us -> 2.06 us  [on_device(): call(functools.partial(output_kernel, strips, out_slots), [jax.ShapeDtype...]
    reshape x2 -> x0, local copies, waits for them, and re-layouts: 1.3 us -> none  [the longest x1 1.29 us: on_device(): w_qkv.reshape(rows, 3, strips, width)]
    another operation x2 -> x0, other arithmetic: 1.19 us -> none  [the longest x1 0.6 us: on_device(): ids = jnp.stack([here, seat]).astype(jnp.int32)]
  transfers between devices with their start and end apart: 26 -> 26, of which waited for: 8 -> 9; matrix products, arithmetic and copies ran while one was open for 9% -> 3% of each run, Pallas kernels for 22% -> 22%
where the time goes in v2:
time: 60.4 us; the launch traced here: 60 us
  starting transfers between devices  22.6 us (37%)
  waiting for transfers between devices  19.2 us (32%)
  Pallas kernels  15.4 us (25%)
  local copies, waits for them, and re-layouts  1.87 us (3%)
  between operations  0.81 us (1%)
    ppermute x26, starting transfers between devices, swap(): return lax.ppermute(block, axis, [(i, i ^ distance) for i in range(size)])  22.6 us
    ppermute x26, waiting for transfers between devices, swap(): return lax.ppermute(block, axis, [(i, i ^ distance) for i in range(size)])  19.2 us
    pallas_call x1, Pallas kernels, on_device(): call(functools.partial(project_kernel, strips, [[slot] for slot in slots]...  7.35 us
    pallas_call x1, Pallas kernels, on_device(): call(functools.partial(own_kernel, strips), strip_out, [SMEM] + [VMEM] *...  4.41 us
    pallas_call x1, Pallas kernels, on_device(): call(functools.partial(output_kernel, strips, out_slots), [jax.ShapeDtype...  2.06 us
    pallas_call x2, Pallas kernels, on_device(): call(norm_kernel, jax.ShapeDtypeStruct((length, features), jnp.bfloat16),...  1.6 us
  transfers between devices with their start and end apart: 26, of which 9 were waited for; matrix products, arithmetic and copies ran while one was open for 3% of the time, Pallas kernels for 22%

profile of v2, /device:TPU:0, one launch (start us, length us, event | category | flops | bytes accessed | tf_op | source)
XLA Modules:
  0.0 60.0 jit_solution(1124957694486203348)
XLA Ops:
  0.6 3.0 %collective-permute-start.2 = (bf16[384,1024]{1,0:T(8,128)(2,1)}, bf16[384,1024]{1,0:T(8,128)(2,1)S(1)}, u32[]{:S(2)}, u32[]{:S(2)}) collective-permute-start(bf16[384,1024]{1,0:T(8,128)(2,1)} %bitcast.10), channel_id=1, source_target_pairs={{0,1},{1,0},{2,3},{3,2},{4,5},{5,4},{6,7},{7,6},{8,9},{9,8},{10,11... | collective-permute-start | bytes 2359304 | tf_op jit(solution)/shard_map/ppermute | solution.py:28
  3.7 0.9 %constant_dynamic-slice_fusion.2 = (bf16[64,512]{1,0:T(8,128)(2,1)S(1)}, bf16[64,512]{1,0:T(8,128)(2,1)S(1)}, bf16[64,512]{1,0:T(8,128)(2,1)S(1)}) fusion(bf16[64,3072]{1,0:T(8,128)(2,1)} %param.12, s32[]{:T(128)S(6)} %select_n.9, s32[]{:T(128)S(6)} %select_n.11, s32[]{:T(128)S(6)} %select_n.10), kind=kLoop, calls=%fused_computation.6 | loop fusion | bytes 393228 | tf_op jit(solution)/shard_map/dynamic_slice | solution.py:274
  4.6 1.6 %collective-permute-start = (bf16[64,1536]{1,0:T(8,128)(2,1)S(1)}, bf16[64,1536]{1,0:T(8,128)(2,1)S(1)}, u32[]{:S(2)}, u32[]{:S(2)}) collective-permute-start(bf16[64,1536]{1,0:T(8,128)(2,1)S(1)} %pad_maximum_fusion.refs_3_), channel_id=1, source_target_pairs={{0,8},{2,10},{4,12},{6,14},{8,0},{10,2},{12,4},{14,6},{16,24},{18,... | collective-permute-start | bytes 589832 | tf_op jit(solution)/shard_map/ppermute | solution.py:28
  6.3 2.5 %collective-permute-start.9 = (bf16[64,1536]{1,0:T(8,128)(2,1)S(1)}, bf16[64,1536]{1,0:T(8,128)(2,1)S(1)}, u32[]{:S(2)}, u32[]{:S(2)}) collective-permute-start(bf16[64,1536]{1,0:T(8,128)(2,1)S(1)} %pad_maximum_fusion.refs_3_), channel_id=1, source_target_pairs={{0,24},{2,26},{4,28},{6,30},{8,16},{10,18},{12,20},{14,22},{16,8},... | collective-permute-start | bytes 589832 | tf_op jit(solution)/shard_map/ppermute | solution.py:28
  8.7 1.5 %collective-permute-start.4 = (bf16[64,1536]{1,0:T(8,128)(2,1)S(1)}, bf16[64,1536]{1,0:T(8,128)(2,1)S(1)}, u32[]{:S(2)}, u32[]{:S(2)}) collective-permute-start(bf16[64,1536]{1,0:T(8,128)(2,1)S(1)} %pad_maximum_fusion.refs_3_), channel_id=1, source_target_pairs={{0,4},{2,6},{4,0},{6,2},{8,12},{10,14},{12,8},{14,10},{16,20},{18,... | collective-permute-start | bytes 589832 | tf_op jit(solution)/shard_map/ppermute | solution.py:28
  10.2 1.4 %collective-permute-done.refs_7_ = bf16[64,1536]{1,0:T(8,128)(2,1)S(1)} collective-permute-done((bf16[64,1536]{1,0:T(8,128)(2,1)S(1)}, bf16[64,1536]{1,0:T(8,128)(2,1)S(1)}, u32[]{:S(2)}, u32[]{:S(2)}) %collective-permute-start) | collective-permute-done | bytes 196640 | tf_op jit(solution)/shard_map/ppermute | solution.py:28
  11.6 1.5 %collective-permute-start.18 = (bf16[64,1024]{1,0:T(8,128)(2,1)}, bf16[64,1024]{1,0:T(8,128)(2,1)S(1)}, u32[]{:S(2)}, u32[]{:S(2)}) collective-permute-start(bf16[64,1024]{1,0:T(8,128)(2,1)} %param.14), channel_id=1, source_target_pairs={{0,4},{2,6},{4,0},{6,2},{8,12},{10,14},{12,8},{14,10},{16,20},{18,... | collective-permute-start | bytes 393224 | tf_op jit(solution)/shard_map/ppermute | solution.py:28
  13.1 4.3 %collective-permute-done.9.refs_15_ = bf16[64,1536]{1,0:T(8,128)(2,1)S(1)} collective-permute-done((bf16[64,1536]{1,0:T(8,128)(2,1)S(1)}, bf16[64,1536]{1,0:T(8,128)(2,1)S(1)}, u32[]{:S(2)}, u32[]{:S(2)}) %collective-permute-start.9) | collective-permute-done | bytes 196640 | tf_op jit(solution)/shard_map/ppermute | solution.py:28
  17.4 1.5 %collective-permute-start.7 = (bf16[64,1536]{1,0:T(8,128)(2,1)S(1)}, bf16[64,1536]{1,0:T(8,128)(2,1)S(1)}, u32[]{:S(2)}, u32[]{:S(2)}) collective-permute-start(bf16[64,1536]{1,0:T(8,128)(2,1)S(1)} %collective-permute-done.refs_7_), channel_id=1, source_target_pairs={{0,4},{2,6},{4,0},{6,2},{8,12},{10,14},{12,8},{14,10},{16,20},{18,... | collective-permute-start | bytes 589832 | tf_op jit(solution)/shard_map/ppermute | solution.py:28
  20.1 3.5 %collective-permute-done.7.refs_9_ = bf16[64,1536]{1,0:T(8,128)(2,1)S(1)} collective-permute-done((bf16[64,1536]{1,0:T(8,128)(2,1)S(1)}, bf16[64,1536]{1,0:T(8,128)(2,1)S(1)}, u32[]{:S(2)}, u32[]{:S(2)}) %collective-permute-start.7) | collective-permute-done | bytes 196640 | tf_op jit(solution)/shard_map/ppermute | solution.py:28
  23.6 1.0 %collective-permute-done.10.refs_11_ = bf16[64,1536]{1,0:T(8,128)(2,1)S(1)} collective-permute-done((bf16[64,1536]{1,0:T(8,128)(2,1)S(1)}, bf16[64,1536]{1,0:T(8,128)(2,1)S(1)}, u32[]{:S(2)}, u32[]{:S(2)}) %collective-permute-start.10) | collective-permute-done | bytes 196640 | tf_op jit(solution)/shard_map/ppermute | solution.py:28
  25.1 2.2 %collective-permute-done.15.refs_17_ = bf16[64,1536]{1,0:T(8,128)(2,1)S(1)} collective-permute-done((bf16[64,1536]{1,0:T(8,128)(2,1)S(1)}, bf16[64,1536]{1,0:T(8,128)(2,1)S(1)}, u32[]{:S(2)}, u32[]{:S(2)}) %collective-permute-start.15) | collective-permute-done | bytes 196640 | tf_op jit(solution)/shard_map/ppermute | solution.py:28
  27.3 1.5 %collective-permute-start.12 = (bf16[64,1536]{1,0:T(8,128)(2,1)S(1)}, bf16[64,1536]{1,0:T(8,128)(2,1)S(1)}, u32[]{:S(2)}, u32[]{:S(2)}) collective-permute-start(bf16[64,1536]{1,0:T(8,128)(2,1)S(1)} %collective-permute-done.10.refs_11_), channel_id=1, source_target_pairs={{0,4},{2,6},{4,0},{6,2},{8,12},{10,14},{12,8},{14,10},{16,20},{18,... | collective-permute-start | bytes 589832 | tf_op jit(solution)/shard_map/ppermute | solution.py:28
  28.8 0.9 %constant_dynamic-update-slice_fusion.1 = bf16[128,1024]{1,0:T(8,128)(2,1)S(1)} fusion(bf16[64,1024]{1,0:T(8,128)(2,1)} %param.14), kind=kLoop, calls=%fused_computation.2 | loop fusion | bytes 262144
  29.8 3.2 %collective-permute-start.22 = (bf16[128,1024]{1,0:T(8,128)(2,1)S(1)}, bf16[128,1024]{1,0:T(8,128)(2,1)S(1)}, u32[]{:S(2)}, u32[]{:S(2)}) collective-permute-start(bf16[128,1024]{1,0:T(8,128)(2,1)S(1)} %constant_dynamic-update-slice_fusion.refs_2_), channel_id=1, source_target_pairs={{0,24},{2,26},{4,28},{6,30},{8,16},{10,18},{12,20},{14,22},{16,8},... | collective-permute-start | bytes 786440 | tf_op jit(solution)/shard_map/ppermute | solution.py:28
  33.8 0.8 %norm.2.refs_1_ = bf16[384,1024]{1,0:T(8,128)(2,1)S(1)} custom-call(bf16[384,1024]{1,0:T(8,128)(2,1)S(1)} %bitcast.11, f32[1,1024]{1,0:T(1,128)S(1)} %bitcast.13, f32[1,1024]{1,0:T(1,128)S(1)} %bitcast.15), custom_call_target="tpu_custom_call" | custom-call | flops 3932160 | bytes 1572864 | tf_op jit(solution)/shard_map/norm/pallas_call | solution.py:281
  36.0 2.3 %collective-permute-done.1.refs_0_ = s32[3,6]{1,0:T(4,128)S(1)} collective-permute-done((s32[3,6]{1,0:T(4,128)S(1)}, s32[3,6]{1,0:T(4,128)S(1)}, u32[]{:S(2)}, u32[]{:S(2)}) %collective-permute-start.1) | collective-permute-done | bytes 104 | tf_op jit(solution)/shard_map/ppermute | solution.py:28
  38.3 0.9 %collective-permute-start.20 = (bf16[128,1024]{1,0:T(8,128)(2,1)S(1)}, bf16[128,1024]{1,0:T(8,128)(2,1)S(1)}, u32[]{:S(2)}, u32[]{:S(2)}) collective-permute-start(bf16[128,1024]{1,0:T(8,128)(2,1)S(1)} %constant_dynamic-update-slice_fusion.refs_2_), channel_id=1, source_target_pairs={{0,8},{2,10},{4,12},{6,14},{8,0},{10,2},{12,4},{14,6},{16,24},{18,... | collective-permute-start | bytes 786440 | tf_op jit(solution)/shard_map/ppermute | solution.py:28
  39.2 7.4 %project.1 = (bf16[384,512]{1,0:T(8,128)(2,1)S(1)}, bf16[384,512]{1,0:T(8,128)(2,1)S(1)}, bf16[768,512]{1,0:T(8,128)(2,1)S(1)}, bf16[4,144,768]{2,1,0:T(8,128)(2,1)S(1)}) custom-call(s32[3,6]{1,0:T(4,128)S(1)} %collective-permute-done.1.refs_0_, bf16[384,1024]{1,0:T(8,128)(2,1)S(1)} %norm.2.refs_1_, bf16[384,1024]{1,0:T(8,128)(2,1)S(1)} %norm.3.refs_2_, ...), custom_call_target="tpu_custom_call" | custom-call | tf_op jit(solution)/shard_map/project/pallas_call | solution.py:317
  47.2 1.4 %collective-permute-start.24 = (bf16[128,1024]{1,0:T(8,128)(2,1)S(1)}, bf16[128,1024]{1,0:T(8,128)(2,1)S(1)}, u32[]{:S(2)}, u32[]{:S(2)}) collective-permute-start(bf16[128,1024]{1,0:T(8,128)(2,1)S(1)} %collective-permute-done.22.refs_6_), channel_id=1, source_target_pairs={{0,8},{2,10},{4,12},{6,14},{8,0},{10,2},{12,4},{14,6},{16,24},{18,... | collective-permute-start | bytes 786440 | tf_op jit(solution)/shard_map/ppermute | solution.py:28
  48.5 4.4 %own_strip.1.refs_0_ = bf16[384,512]{1,0:T(8,128)(2,1)S(1)} custom-call(s32[3,6]{1,0:T(4,128)S(1)} %bitcast.20, bf16[384,512]{1,0:T(8,128)(2,1)S(1)} %get-tuple-element.14.query_ref, bf16[768,512]{1,0:T(8,128)(2,1)S(1)} %get-tuple-element.15.key_ref, bf16[4,144,768]{2,1,0:T(8,128)(2,1)S(1)} %get-tuple-element.16.value_ref), custom_call_target="tpu_custom_call" | custom-call | flops 10000000000 | tf_op jit(solution)/shard_map/own_strip/pallas_call | solution.py:335
  53.7 2.2 %collective-permute-done.24.refs_8_ = bf16[128,1024]{1,0:T(8,128)(2,1)S(1)} collective-permute-done((bf16[128,1024]{1,0:T(8,128)(2,1)S(1)}, bf16[128,1024]{1,0:T(8,128)(2,1)S(1)}, u32[]{:S(2)}, u32[]{:S(2)}) %collective-permute-start.24) | collective-permute-done | bytes 262176 | tf_op jit(solution)/shard_map/ppermute | solution.py:28
  55.8 2.1 %collective-permute-done.17.refs_1_ = bf16[384,512]{1,0:T(8,128)(2,1)S(1)} collective-permute-done((bf16[384,512]{1,0:T(8,128)(2,1)S(1)}, bf16[384,512]{1,0:T(8,128)(2,1)S(1)}, u32[]{:S(2)}, u32[]{:S(2)}) %collective-permute-start.17) | collective-permute-done | bytes 393248 | tf_op jit(solution)/shard_map/ppermute | solution.py:28
  57.9 2.1 %output.1 = (bf16[384,1024]{1,0:T(8,128)(2,1)}, bf16[384,1024]{1,0:T(8,128)(2,1)}) custom-call(bf16[384,512]{1,0:T(8,128)(2,1)S(1)} %own_strip.1.refs_0_, bf16[384,512]{1,0:T(8,128)(2,1)S(1)} %collective-permute-done.17.refs_1_, bf16[128,1024]{1,0:T(8,128)(2,1)S(1)} %constant_dynamic-update-slice_fusion.refs_2_, ...), custom_call_target="tpu_custom_call" | custom-call | flops 805306368 | bytes 2097152 | tf_op jit(solution)/shard_map/output/pallas_call | solution.py:353
  (50 shorter events, 5.3 us)
Async XLA Ops:
  0.6 29.1 %collective-permute-start.2 = (bf16[384,1024]{1,0:T(8,128)(2,1)}, bf16[384,1024]{1,0:T(8,128)(2,1)S(1)}, u32[]{:S(2)}, u32[]{:S(2)}) collective-permute-start(bf16[384,1024]{1,0:T(8,128)(2,1)} %bitcast.10), channel_id=1, source_target_pairs={{0,1},{1,0},{2,3},{3,2},{4,5},{5,4},{6,7},{7,6},{8,9},{9,8},{10,11... | collective-permute-start | bytes 2359304 | tf_op jit(solution)/shard_map/ppermute | solution.py:28
  4.6 7.0 %collective-permute-start = (bf16[64,1536]{1,0:T(8,128)(2,1)S(1)}, bf16[64,1536]{1,0:T(8,128)(2,1)S(1)}, u32[]{:S(2)}, u32[]{:S(2)}) collective-permute-start(bf16[64,1536]{1,0:T(8,128)(2,1)S(1)} %pad_maximum_fusion.refs_3_), channel_id=1, source_target_pairs={{0,8},{2,10},{4,12},{6,14},{8,0},{10,2},{12,4},{14,6},{16,24},{18,... | collective-permute-start | bytes 589832 | tf_op jit(solution)/shard_map/ppermute | solution.py:28
  6.3 11.1 %collective-permute-start.9 = (bf16[64,1536]{1,0:T(8,128)(2,1)S(1)}, bf16[64,1536]{1,0:T(8,128)(2,1)S(1)}, u32[]{:S(2)}, u32[]{:S(2)}) collective-permute-start(bf16[64,1536]{1,0:T(8,128)(2,1)S(1)} %pad_maximum_fusion.refs_3_), channel_id=1, source_target_pairs={{0,24},{2,26},{4,28},{6,30},{8,16},{10,18},{12,20},{14,22},{16,8},... | collective-permute-start | bytes 589832 | tf_op jit(solution)/shard_map/ppermute | solution.py:28
  8.7 10.1 %collective-permute-start.4 = (bf16[64,1536]{1,0:T(8,128)(2,1)S(1)}, bf16[64,1536]{1,0:T(8,128)(2,1)S(1)}, u32[]{:S(2)}, u32[]{:S(2)}) collective-permute-start(bf16[64,1536]{1,0:T(8,128)(2,1)S(1)} %pad_maximum_fusion.refs_3_), channel_id=1, source_target_pairs={{0,4},{2,6},{4,0},{6,2},{8,12},{10,14},{12,8},{14,10},{16,20},{18,... | collective-permute-start | bytes 589832 | tf_op jit(solution)/shard_map/ppermute | solution.py:28
  10.2 9.2 %collective-permute-start.3 = (bf16[64,1536]{1,0:T(8,128)(2,1)S(1)}, bf16[64,1536]{1,0:T(8,128)(2,1)S(1)}, u32[]{:S(2)}, u32[]{:S(2)}) collective-permute-start(bf16[64,1536]{1,0:T(8,128)(2,1)S(1)} %pad_maximum_fusion.refs_3_), channel_id=1, source_target_pairs={{0,2},{2,0},{4,6},{6,4},{8,10},{10,8},{12,14},{14,12},{16,18},{18,... | collective-permute-start | bytes 589832 | tf_op jit(solution)/shard_map/ppermute | solution.py:28
  11.6 7.9 %collective-permute-start.18 = (bf16[64,1024]{1,0:T(8,128)(2,1)}, bf16[64,1024]{1,0:T(8,128)(2,1)S(1)}, u32[]{:S(2)}, u32[]{:S(2)}) collective-permute-start(bf16[64,1024]{1,0:T(8,128)(2,1)} %param.14), channel_id=1, source_target_pairs={{0,4},{2,6},{4,0},{6,2},{8,12},{10,14},{12,8},{14,10},{16,20},{18,... | collective-permute-start | bytes 393224 | tf_op jit(solution)/shard_map/ppermute | solution.py:28
  17.4 6.2 %collective-permute-start.7 = (bf16[64,1536]{1,0:T(8,128)(2,1)S(1)}, bf16[64,1536]{1,0:T(8,128)(2,1)S(1)}, u32[]{:S(2)}, u32[]{:S(2)}) collective-permute-start(bf16[64,1536]{1,0:T(8,128)(2,1)S(1)} %collective-permute-done.refs_7_), channel_id=1, source_target_pairs={{0,4},{2,6},{4,0},{6,2},{8,12},{10,14},{12,8},{14,10},{16,20},{18,... | collective-permute-start | bytes 589832 | tf_op jit(solution)/shard_map/ppermute | solution.py:28
  18.9 5.7 %collective-permute-start.10 = (bf16[64,1536]{1,0:T(8,128)(2,1)S(1)}, bf16[64,1536]{1,0:T(8,128)(2,1)S(1)}, u32[]{:S(2)}, u32[]{:S(2)}) collective-permute-start(bf16[64,1536]{1,0:T(8,128)(2,1)S(1)} %collective-permute-done.9.refs_15_), channel_id=1, source_target_pairs={{0,8},{2,10},{4,12},{6,14},{8,0},{10,2},{12,4},{14,6},{16,24},{18,... | collective-permute-start | bytes 589832 | tf_op jit(solution)/shard_map/ppermute | solution.py:28
  19.5 5.1 %collective-permute-start.14 = (bf16[64,1536]{1,0:T(8,128)(2,1)S(1)}, bf16[64,1536]{1,0:T(8,128)(2,1)S(1)}, u32[]{:S(2)}, u32[]{:S(2)}) collective-permute-start(bf16[64,1536]{1,0:T(8,128)(2,1)S(1)} %collective-permute-done.9.refs_15_), channel_id=1, source_target_pairs={{0,2},{2,0},{4,6},{6,4},{8,10},{10,8},{12,14},{14,12},{16,18},{18,... | collective-permute-start | bytes 589832 | tf_op jit(solution)/shard_map/ppermute | solution.py:28
  19.5 7.8 %collective-permute-start.15 = (bf16[64,1536]{1,0:T(8,128)(2,1)S(1)}, bf16[64,1536]{1,0:T(8,128)(2,1)S(1)}, u32[]{:S(2)}, u32[]{:S(2)}) collective-permute-start(bf16[64,1536]{1,0:T(8,128)(2,1)S(1)} %collective-permute-done.9.refs_15_), channel_id=1, source_target_pairs={{0,4},{2,6},{4,0},{6,2},{8,12},{10,14},{12,8},{14,10},{16,20},{18,... | collective-permute-start | bytes 589832 | tf_op jit(solution)/shard_map/ppermute | solution.py:28
  23.6 6.2 %collective-permute-start.6 = (bf16[64,1536]{1,0:T(8,128)(2,1)S(1)}, bf16[64,1536]{1,0:T(8,128)(2,1)S(1)}, u32[]{:S(2)}, u32[]{:S(2)}) collective-permute-start(bf16[64,1536]{1,0:T(8,128)(2,1)S(1)} %collective-permute-done.refs_7_), channel_id=1, source_target_pairs={{0,2},{2,0},{4,6},{6,4},{8,10},{10,8},{12,14},{14,12},{16,18},{18,... | collective-permute-start | bytes 589832 | tf_op jit(solution)/shard_map/ppermute | solution.py:28
  24.6 5.2 %collective-permute-start.5 = (bf16[64,1536]{1,0:T(8,128)(2,1)S(1)}, bf16[64,1536]{1,0:T(8,128)(2,1)S(1)}, u32[]{:S(2)}, u32[]{:S(2)}) collective-permute-start(bf16[64,1536]{1,0:T(8,128)(2,1)S(1)} %collective-permute-done.4.refs_5_), channel_id=1, source_target_pairs={{0,2},{2,0},{4,6},{6,4},{8,10},{10,8},{12,14},{14,12},{16,18},{18,... | collective-permute-start | bytes 589832 | tf_op jit(solution)/shard_map/ppermute | solution.py:28
  24.6 5.2 %collective-permute-start.8 = (bf16[64,1536]{1,0:T(8,128)(2,1)S(1)}, bf16[64,1536]{1,0:T(8,128)(2,1)S(1)}, u32[]{:S(2)}, u32[]{:S(2)}) collective-permute-start(bf16[64,1536]{1,0:T(8,128)(2,1)S(1)} %collective-permute-done.7.refs_9_), channel_id=1, source_target_pairs={{0,2},{2,0},{4,6},{6,4},{8,10},{10,8},{12,14},{14,12},{16,18},{18,... | collective-permute-start | bytes 589832 | tf_op jit(solution)/shard_map/ppermute | solution.py:28
  27.3 6.5 %collective-permute-start.12 = (bf16[64,1536]{1,0:T(8,128)(2,1)S(1)}, bf16[64,1536]{1,0:T(8,128)(2,1)S(1)}, u32[]{:S(2)}, u32[]{:S(2)}) collective-permute-start(bf16[64,1536]{1,0:T(8,128)(2,1)S(1)} %collective-permute-done.10.refs_11_), channel_id=1, source_target_pairs={{0,4},{2,6},{4,0},{6,2},{8,12},{10,14},{12,8},{14,10},{16,20},{18,... | collective-permute-start | bytes 589832 | tf_op jit(solution)/shard_map/ppermute | solution.py:28
  29.8 17.4 %collective-permute-start.22 = (bf16[128,1024]{1,0:T(8,128)(2,1)S(1)}, bf16[128,1024]{1,0:T(8,128)(2,1)S(1)}, u32[]{:S(2)}, u32[]{:S(2)}) collective-permute-start(bf16[128,1024]{1,0:T(8,128)(2,1)S(1)} %constant_dynamic-update-slice_fusion.refs_2_), channel_id=1, source_target_pairs={{0,24},{2,26},{4,28},{6,30},{8,16},{10,18},{12,20},{14,22},{16,8},... | collective-permute-start | bytes 786440 | tf_op jit(solution)/shard_map/ppermute | solution.py:28
  32.9 5.4 %collective-permute-start.11 = (bf16[64,1536]{1,0:T(8,128)(2,1)S(1)}, bf16[64,1536]{1,0:T(8,128)(2,1)S(1)}, u32[]{:S(2)}, u32[]{:S(2)}) collective-permute-start(bf16[64,1536]{1,0:T(8,128)(2,1)S(1)} %collective-permute-done.10.refs_11_), channel_id=1, source_target_pairs={{0,2},{2,0},{4,6},{6,4},{8,10},{10,8},{12,14},{14,12},{16,18},{18,... | collective-permute-start | bytes 589832 | tf_op jit(solution)/shard_map/ppermute | solution.py:28
  32.9 6.3 %collective-permute-start.16 = (bf16[64,1536]{1,0:T(8,128)(2,1)S(1)}, bf16[64,1536]{1,0:T(8,128)(2,1)S(1)}, u32[]{:S(2)}, u32[]{:S(2)}) collective-permute-start(bf16[64,1536]{1,0:T(8,128)(2,1)S(1)} %collective-permute-done.15.refs_17_), channel_id=1, source_target_pairs={{0,2},{2,0},{4,6},{6,4},{8,10},{10,8},{12,14},{14,12},{16,18},{18,... | collective-permute-start | bytes 589832 | tf_op jit(solution)/shard_map/ppermute | solution.py:28
  33.8 5.4 %collective-permute-start.13 = (bf16[64,1536]{1,0:T(8,128)(2,1)S(1)}, bf16[64,1536]{1,0:T(8,128)(2,1)S(1)}, u32[]{:S(2)}, u32[]{:S(2)}) collective-permute-start(bf16[64,1536]{1,0:T(8,128)(2,1)S(1)} %collective-permute-done.12.refs_13_), channel_id=1, source_target_pairs={{0,2},{2,0},{4,6},{6,4},{8,10},{10,8},{12,14},{14,12},{16,18},{18,... | collective-permute-start | bytes 589832 | tf_op jit(solution)/shard_map/ppermute | solution.py:28
  38.3 17.5 %collective-permute-start.19 = (bf16[128,1024]{1,0:T(8,128)(2,1)S(1)}, bf16[128,1024]{1,0:T(8,128)(2,1)S(1)}, u32[]{:S(2)}, u32[]{:S(2)}) collective-permute-start(bf16[128,1024]{1,0:T(8,128)(2,1)S(1)} %constant_dynamic-update-slice_fusion.refs_2_), channel_id=1, source_target_pairs={{0,2},{2,0},{4,6},{6,4},{8,10},{10,8},{12,14},{14,12},{16,18},{18,... | collective-permute-start | bytes 786440 | tf_op jit(solution)/shard_map/ppermute | solution.py:28
  38.3 15.3 %collective-permute-start.20 = (bf16[128,1024]{1,0:T(8,128)(2,1)S(1)}, bf16[128,1024]{1,0:T(8,128)(2,1)S(1)}, u32[]{:S(2)}, u32[]{:S(2)}) collective-permute-start(bf16[128,1024]{1,0:T(8,128)(2,1)S(1)} %constant_dynamic-update-slice_fusion.refs_2_), channel_id=1, source_target_pairs={{0,8},{2,10},{4,12},{6,14},{8,0},{10,2},{12,4},{14,6},{16,24},{18,... | collective-permute-start | bytes 786440 | tf_op jit(solution)/shard_map/ppermute | solution.py:28
  46.6 11.3 %collective-permute-start.17 = (bf16[384,512]{1,0:T(8,128)(2,1)S(1)}, bf16[384,512]{1,0:T(8,128)(2,1)S(1)}, u32[]{:S(2)}, u32[]{:S(2)}) collective-permute-start(bf16[384,512]{1,0:T(8,128)(2,1)S(1)} %get-tuple-element.17), channel_id=1, source_target_pairs={{0,1},{1,0},{2,3},{3,2},{4,5},{5,4},{6,7},{7,6},{8,9},{9,8},{10,11... | collective-permute-start | bytes 1179656 | tf_op jit(solution)/shard_map/ppermute | solution.py:28
  47.2 8.7 %collective-permute-start.24 = (bf16[128,1024]{1,0:T(8,128)(2,1)S(1)}, bf16[128,1024]{1,0:T(8,128)(2,1)S(1)}, u32[]{:S(2)}, u32[]{:S(2)}) collective-permute-start(bf16[128,1024]{1,0:T(8,128)(2,1)S(1)} %collective-permute-done.22.refs_6_), channel_id=1, source_target_pairs={{0,8},{2,10},{4,12},{6,14},{8,0},{10,2},{12,4},{14,6},{16,24},{18,... | collective-permute-start | bytes 786440 | tf_op jit(solution)/shard_map/ppermute | solution.py:28
  53.0 4.9 %collective-permute-start.23 = (bf16[128,1024]{1,0:T(8,128)(2,1)S(1)}, bf16[128,1024]{1,0:T(8,128)(2,1)S(1)}, u32[]{:S(2)}, u32[]{:S(2)}) collective-permute-start(bf16[128,1024]{1,0:T(8,128)(2,1)S(1)} %collective-permute-done.22.refs_6_), channel_id=1, source_target_pairs={{0,2},{2,0},{4,6},{6,4},{8,10},{10,8},{12,14},{14,12},{16,18},{18,... | collective-permute-start | bytes 786440 | tf_op jit(solution)/shard_map/ppermute | solution.py:28
  53.6 4.3 %collective-permute-start.21 = (bf16[128,1024]{1,0:T(8,128)(2,1)S(1)}, bf16[128,1024]{1,0:T(8,128)(2,1)S(1)}, u32[]{:S(2)}, u32[]{:S(2)}) collective-permute-start(bf16[128,1024]{1,0:T(8,128)(2,1)S(1)} %collective-permute-done.20.refs_4_), channel_id=1, source_target_pairs={{0,2},{2,0},{4,6},{6,4},{8,10},{10,8},{12,14},{14,12},{16,18},{18,... | collective-permute-start | bytes 786440 | tf_op jit(solution)/shard_map/ppermute | solution.py:28
  (8 other events, 65.1 us)

commit v3 on v2

v3 whole, which is shorter than its diff:
```python
import functools

import jax
import jax.numpy as jnp
from jax import lax
from jax.experimental import pallas as pl
from jax.experimental.pallas import tpu as pltpu
from jax.sharding import PartitionSpec as P

D = 1024
HEADS = 16
BLOCK = 128
HEAD_DIM = D // HEADS
PAIR = 2 * HEAD_DIM

ROUND = 3
LONG = 10**11

NEG_FILL = -1e30
EPSILON = 1e-06
VMEM_LIMIT = 28 * 1024 * 1024

VMEM = pl.BlockSpec(memory_space=pltpu.VMEM)
SMEM = pl.BlockSpec(memory_space=pltpu.SMEM)


def swap(block, axis, distance):
    if distance == 0:
        return block
    size = lax.axis_size(axis)
    return lax.ppermute(block, axis, [(i, i ^ distance) for i in range(size)])


def call(kernel, out_shape, in_specs, scratch=(), flops=0, nbytes=0, name=None):
    many = isinstance(out_shape, (list, tuple))
    return pl.pallas_call(
        kernel,
        out_shape=out_shape,
        in_specs=in_specs,
        out_specs=[VMEM] * len(out_shape) if many else VMEM,
        scratch_shapes=scratch,
        compiler_params=pltpu.CompilerParams(vmem_limit_bytes=VMEM_LIMIT),
        cost_estimate=pl.CostEstimate(
            flops=flops, bytes_accessed=nbytes, transcendentals=0
        ),
        name=name,
    )


def norm_kernel(sheet_ref, gain_ref, bias_ref, out_ref):
    step = 32

    @pl.loop(0, sheet_ref.shape[0] // step, unroll=4)
    def _(index):
        rows = pl.ds(pl.multiple_of(index * step, step), step)
        values = sheet_ref[rows, :].astype(jnp.float32)
        center = jnp.mean(values, axis=-1, keepdims=True)
        moved = values - center
        spread = jnp.mean(jnp.square(moved), axis=-1, keepdims=True)
        normed = moved * lax.rsqrt(spread + EPSILON)
        out_ref[rows, :] = (normed * gain_ref[...] + bias_ref[...]).astype(jnp.bfloat16)


def gather_rows(pieces, target):
    here = lax.axis_index("dp")
    for slots, piece in pieces:
        rows = piece.shape[0] // len(slots)
        for index, slot in enumerate(slots):
            first = pl.multiple_of((here ^ slot) * rows, rows)
            columns = pl.ds(0, target.shape[1])
            target[pl.ds(first, rows), :] = piece[pl.ds(index * rows, rows), columns]


def attend_strip(query_ref, first_row, mask_ref, out_ref, strips, key_ref, value_ref, work):
    scores, tops, sums, listed = work
    seat = lax.axis_index("seq")
    per_strip = out_ref.shape[0] // BLOCK
    blocks = strips * per_strip
    pairs = key_ref.shape[1] // PAIR
    low = lax.broadcasted_iota(jnp.int32, (BLOCK, PAIR), 1) < HEAD_DIM

    def enlist(number, count):
        index, block = number // blocks, number % blocks
        column = (seat ^ (block // per_strip)) * per_strip + block % per_strip
        listed[count] = number
        return count + mask_ref[index, column]

    count = lax.fori_loop(0, per_strip * blocks, enlist, 0)
    for extra in range(ROUND):
        listed[count + extra] = per_strip * blocks
    rounds = (count + ROUND - 1) // ROUND

    tops[...] = jnp.full(tops.shape, NEG_FILL, jnp.float32)
    sums[...] = jnp.zeros(sums.shape, jnp.float32)

    def entries(turn):
        for lane in range(ROUND):
            number = listed[turn * ROUND + lane]
            yield number // blocks, pl.multiple_of(number % blocks * BLOCK, BLOCK)

    @pl.loop(0, rounds)
    def _(turn):
        for index, key in entries(turn):
            inside = jnp.minimum(index, per_strip - 1)
            source = pl.ds(pl.multiple_of(first_row + inside * BLOCK, BLOCK), BLOCK)
            for pair in range(pairs):
                lanes = pl.ds(pair * PAIR, PAIR)
                both = query_ref[source, lanes]
                zero = jnp.zeros_like(both)
                stacked = jnp.concatenate(
                    [jnp.where(low, both, zero), jnp.where(low, zero, both)], axis=0
                )
                result = lax.dot_general(
                    key_ref[pl.ds(key, BLOCK), lanes],
                    stacked,
                    (((1,), (1,)), ((), ())),
                    preferred_element_type=jnp.float32,
                )
                scores[index, pair, pl.ds(key, BLOCK), :] = result
                folded = jnp.max(result.reshape(BLOCK // 8, 8, 2 * BLOCK), axis=0)
                tops[index, pair] = jnp.maximum(tops[index, pair], folded)

    for index in range(per_strip):
        for pair in range(pairs):
            top = jnp.max(tops[index, pair], axis=0, keepdims=True)
            tops[index, pair] = jnp.broadcast_to(top, tops.shape[2:])

    @pl.loop(0, rounds)
    def _(turn):
        for index, key in entries(turn):
            for pair in range(pairs):
                found = scores[index, pair, pl.ds(key, BLOCK), :]
                weights = jnp.exp(found - tops[index, pair, :1]).astype(jnp.bfloat16)
                sums[index, pair] += jnp.dot(
                    value_ref[pair, :, pl.ds(key, BLOCK)],
                    weights,
                    preferred_element_type=jnp.float32,
                )

    for index in range(per_strip):
        for pair in range(pairs):
            share = 1.0 / sums[index, pair, PAIR : PAIR + 1]
            both = jnp.concatenate(
                [
                    sums[index, pair, :HEAD_DIM, :BLOCK] * share[:, :BLOCK],
                    sums[index, pair, HEAD_DIM:PAIR, BLOCK:] * share[:, BLOCK:],
                ],
                axis=0,
            )
            out_ref[pl.ds(index * BLOCK, BLOCK), pl.ds(pair * PAIR, PAIR)] = both.T.astype(
                jnp.bfloat16
            )


def project_kernel(strips, parts, slots, *refs):
    masks, refs = refs[: strips - 1], refs[strips - 1 :]
    normed, refs = refs[:parts], refs[parts:]
    pieces, refs = refs[: len(slots)], refs[len(slots) :]
    bias_ref, *rest = refs
    away, rest = rest[: strips - 1], rest[strips - 1 :]
    query_ref, key_ref, value_ref, weight, tokens, queries, *work = rest
    seat = lax.axis_index("seq")
    gather_rows(list(zip(slots, pieces)), weight)
    filled = 0
    for part in normed:
        tokens[pl.ds(filled, part.shape[0]), :] = part[...]
        filled += part.shape[0]
    length = filled // strips
    width = key_ref.shape[1]
    step = PAIR * 2 if width % (PAIR * 2) == 0 else PAIR
    value_ref[:, PAIR:, :] = jnp.ones((width // PAIR, 16, length * strips), jnp.bfloat16)
    for kind in range(3):
        for first in range(0, width, step):
            lanes = pl.ds(kind * width + first, step)
            bias = bias_ref[:, pl.ds(pl.multiple_of(kind * D + seat * width + first, PAIR), step)]
            for strip in range(strips):
                found = jnp.dot(
                    tokens[pl.ds(strip * length, length), :],
                    weight[:, lanes],
                    preferred_element_type=jnp.float32,
                )
                found = found + bias
                rows = pl.ds(strip * length, length)
                out = pl.ds(first, step)
                if kind == 0:
                    found = (found * HEAD_DIM**-0.5).astype(jnp.bfloat16)
                    if strip == 0:
                        query_ref[:, out] = found
                    else:
                        queries[pl.ds((strip - 1) * length, length), out] = found
                elif kind == 1:
                    key_ref[rows, out] = found.astype(jnp.bfloat16)
                else:
                    turned = found.T.astype(jnp.bfloat16)
                    for offset in range(0, step, PAIR):
                        value_ref[(first + offset) // PAIR, :PAIR, rows] = turned[
                            offset : offset + PAIR
                        ]

    for strip in range(1, strips):
        attend_strip(
            queries,
            (strip - 1) * length,
            masks[strip - 1],
            away[strip - 1],
            strips,
            key_ref,
            value_ref,
            work,
        )


def own_kernel(strips, mask_ref, query_ref, key_ref, value_ref, out_ref, *work):
    attend_strip(query_ref, 0, mask_ref, out_ref, strips, key_ref, value_ref, work)


def output_kernel(strips, slots, *refs):
    parts = refs[:strips]
    pieces = refs[strips : strips + len(slots)]
    sheet_ref, bias_ref, updated_ref, context_ref, weight = refs[strips + len(slots) :]
    seat = lax.axis_index("seq")
    gather_rows(list(zip(slots, pieces)), weight)
    width = parts[0].shape[1]
    for strip, part in enumerate(parts):
        first = pl.multiple_of((seat ^ strip) * width, width)
        context_ref[:, pl.ds(first, width)] = part[...]
    step = 256
    for first in range(0, updated_ref.shape[1], step):
        lanes = pl.ds(first, step)
        found = jnp.dot(
            context_ref[...], weight[:, lanes], preferred_element_type=jnp.float32
        )
        found = sheet_ref[:, lanes].astype(jnp.float32) + found + bias_ref[:, lanes]
        updated_ref[:, lanes] = found.astype(jnp.bfloat16)


def after(block, *others):
    return lax.optimization_barrier((block, *others))[0]


def on_device(tokens, masks, ln_gain, ln_bias, w_qkv, qkv_bias, w_out, out_bias):
    size, strips = lax.axis_size("dp"), lax.axis_size("seq")
    seat = lax.axis_index("seq")
    sheet = tokens[0]
    length, features = sheet.shape
    width = D // strips
    total = length * strips
    per_strip, blocks = length // BLOCK, total // BLOCK
    pairs = width // PAIR
    rows = w_qkv.shape[0]

    def mine_of(array):
        starts = [kind * D + seat * width for kind in range(3)]
        return jnp.concatenate(
            [lax.dynamic_slice_in_dim(array, start, width, 1) for start in starts], axis=1
        )

    own = mine_of(w_qkv)
    masks_of = [swap(masks[0], "seq", k) for k in range(strips)]
    sheets = [swap(after(sheet, *masks_of[1:]) if k else sheet, "seq", k) for k in range(strips)]

    def norm(block, flops=0):
        return call(
            norm_kernel,
            jax.ShapeDtypeStruct(block.shape, jnp.bfloat16),
            [VMEM] * 3,
            flops=flops,
            name="norm",
        )(block, ln_gain[None], ln_bias[None])

    along_x = size // 8
    across = [2 * x for x in range(1, along_x)]
    first, second, third = (2 * along_x * z for z in (1, 3, 2))

    pieces = {0: own}
    both = jnp.concatenate([own, w_out], axis=1)
    for x in across:
        pieces[x] = swap(both, "dp", x)
    pieces[second] = swap(own, "dp", second)
    pieces[first] = swap(own, "dp", first)
    normed = [norm(sheet[:BLOCK], LONG)]

    one = after(pieces[first], pieces[across[0]], normed[0])
    for x in across:
        pieces[first + x] = swap(one, "dp", x)
    out_near = [w_out, *(pieces[x][:, 3 * width :] for x in across)]
    out_own = jnp.concatenate(out_near, axis=0)

    pieces[third] = swap(pieces[second], "dp", first)
    for x in across:
        pieces[second + x] = swap(pieces[second], "dp", x)

    for x in across:
        pieces[third + x] = swap(pieces[third], "dp", x)
    out_ready = after(out_own, pieces[third])
    out_second = swap(out_ready, "dp", second)
    out_first = swap(out_ready, "dp", first)
    before = [pieces[slot] for slot in (third, first + across[0], second + across[0])]
    normed.append(norm(after(sheet[BLOCK:], normed[0], *before), LONG))
    normed.extend(norm(sheets[k]) for k in range(1, strips))

    for slot in sorted(pieces):
        pieces[slot + 1] = swap(pieces[slot], "dp", 1)
    slots = sorted(pieces)

    work = [
        pltpu.VMEM((per_strip + 1, pairs, total, 2 * BLOCK), jnp.float32),
        pltpu.VMEM((per_strip + 1, pairs, 8, 2 * BLOCK), jnp.float32),
        pltpu.VMEM((per_strip + 1, pairs, PAIR + 16, 2 * BLOCK), jnp.float32),
        pltpu.SMEM((per_strip * blocks + ROUND,), jnp.int32),
    ]
    strip_out = jax.ShapeDtypeStruct((length, width), jnp.bfloat16)
    *away, query, key, value = call(
        functools.partial(project_kernel, strips, len(normed), [[slot] for slot in slots]),
        [strip_out] * (strips - 1)
        + [
            strip_out,
            jax.ShapeDtypeStruct((total, width), jnp.bfloat16),
            jax.ShapeDtypeStruct((pairs, PAIR + 16, total), jnp.bfloat16),
        ],
        [SMEM] * (strips - 1) + [VMEM] * (len(normed) + len(slots) + 1),
        [
            pltpu.VMEM((D, 3 * width), jnp.bfloat16),
            pltpu.VMEM((total, D), jnp.bfloat16),
            pltpu.VMEM((total - length, width), jnp.bfloat16),
        ]
        + work,
        name="project",
    )(
        *masks_of[1:],
        *normed,
        *[pieces[slot] for slot in slots],
        qkv_bias[None],
    )

    returned = [swap(block, "seq", k + 1) for k, block in enumerate(away)]
    mine = call(
        functools.partial(own_kernel, strips),
        strip_out,
        [SMEM] + [VMEM] * 3,
        work,
        flops=LONG,
        name="own_strip",
    )(masks_of[0], query, key, value)

    out_third = swap(after(out_second, *away), "dp", first)
    out_slots, out_pieces = [], []
    for far, piece in ((0, out_own), (first, out_first), (second, out_second), (third, out_third)):
        out_slots.append([far + x for x in (0, *across)])
        out_pieces.append(piece)
        out_slots.append([far + x + 1 for x in (0, *across)])
        out_pieces.append(swap(after(piece, mine), "dp", 1))

    updated, context = call(
        functools.partial(output_kernel, strips, out_slots),
        [jax.ShapeDtypeStruct((length, D), jnp.bfloat16)] * 2,
        [VMEM] * (strips + len(out_slots) + 2),
        [pltpu.VMEM((D, D), jnp.bfloat16)],
        flops=2 * length * D * D,
        nbytes=2 * D * D,
        name="output",
    )(
        mine,
        *returned,
        *out_pieces,
        sheet,
        out_bias[None],
    )
    return (updated[None], context[None])


def solution(mesh):
    placed = (
        P("dp", "seq", None),
        P("dp", "seq", None),
        P(),
        P(),
        P("dp", None),
        P(),
        P("dp", None),
        P(),
    )
    return jax.shard_map(
        on_device,
        mesh=mesh,
        in_specs=placed,
        out_specs=(P("dp", "seq", None), P("dp", "seq", None)),
        check_vma=False,
    )
```

time: 60.4 us -> 55.3 us (0.916)
  waiting for transfers between devices: 19.2 us -> 14.4 us
  Pallas kernels: 15.4 us -> 11.1 us
  starting transfers between devices: 22.6 us -> 25.2 us
  other arithmetic: 0.02 us -> 0.96 us
  local copies, waits for them, and re-layouts: 1.87 us -> 2.67 us
    ppermute x26 -> x25, waiting for transfers between devices: 19.2 us -> 14.4 us  [swap(): return lax.ppermute(block, axis, [(i, i ^ distance) for i in range(size)])]
    ppermute x26 -> x25, starting transfers between devices: 22.6 us -> 25.2 us  [swap(): return lax.ppermute(block, axis, [(i, i ^ distance) for i in range(size)])]
    pallas_call x1, Pallas kernels: 4.41 us -> 2.25 us  [on_device(): call(functools.partial(own_kernel, strips), strip_out, [SMEM] + [VMEM] *...]
    pallas_call x3 -> x4, Pallas kernels: 8.95 us -> 6.81 us  [the longest x1 5.2 us: on_device(): call(functools.partial(project_kernel, strips, len(normed), [[slot] for s...]
    concatenate x0 -> x2, other arithmetic: none -> 0.94 us  [the longest x1 0.93 us: on_device(): both = jnp.concatenate([own, w_out], axis=1)]
    unnamed x14 -> x23, local copies, waits for them, and re-layouts: 0.95 us -> 1.61 us
  transfers between devices with their start and end apart: 26 -> 25, of which waited for: 9 -> 8; matrix products, arithmetic and copies ran while one was open for 3% -> 2% of each run, Pallas kernels for 22% -> 16%
where the time goes in v3:
time: 55.3 us; the launch traced here: 55.1 us
  starting transfers between devices  25.2 us (46%)
  waiting for transfers between devices  14.4 us (26%)
  Pallas kernels  11.1 us (20%)
  local copies, waits for them, and re-layouts  2.67 us (5%)
  other arithmetic  0.96 us (2%)
  between operations  0.85 us (2%)
    ppermute x25, starting transfers between devices, swap(): return lax.ppermute(block, axis, [(i, i ^ distance) for i in range(size)])  25.2 us
    ppermute x25, waiting for transfers between devices, swap(): return lax.ppermute(block, axis, [(i, i ^ distance) for i in range(size)])  14.4 us
    pallas_call x1, Pallas kernels, on_device(): call(functools.partial(project_kernel, strips, len(normed), [[slot] for s...  5.2 us
    pallas_call x1, Pallas kernels, on_device(): call(functools.partial(own_kernel, strips), strip_out, [SMEM] + [VMEM] *...  2.25 us
    pallas_call x1, Pallas kernels, on_device(): call(functools.partial(output_kernel, strips, out_slots), [jax.ShapeDtype...  2.05 us
    unnamed x23, local copies, waits for them, and re-layouts  1.61 us
    pallas_call x3, Pallas kernels, norm(): call(norm_kernel, jax.ShapeDtypeStruct(block.shape, jnp.bfloat16), [VMEM]...  1.6 us
  transfers between devices with their start and end apart: 25, of which 8 were waited for; matrix products, arithmetic and copies ran while one was open for 2% of the time, Pallas kernels for 16%

profile of v3, /device:TPU:0, one launch (start us, length us, event | category | flops | bytes accessed | tf_op | source)
XLA Modules:
  0.0 55.1 jit_solution(3613309474342208317)
XLA Ops:
  0.6 1.0 %constant_dynamic-slice_fusion.2 = (bf16[64,512]{1,0:T(8,128)(2,1)S(1)}, bf16[64,512]{1,0:T(8,128)(2,1)S(1)}, bf16[64,512]{1,0:T(8,128)(2,1)S(1)}) fusion(bf16[64,3072]{1,0:T(8,128)(2,1)} %param.12, s32[]{:T(128)S(6)} %select_n.9, s32[]{:T(128)S(6)} %select_n.11, s32[]{:T(128)S(6)} %select_n.10), kind=kLoop, calls=%fused_computation.8 | loop fusion | bytes 393228 | tf_op jit(solution)/shard_map/dynamic_slice | solution.py:255
  1.7 3.1 %collective-permute-start.3 = (bf16[64,1536]{1,0:T(8,128)(2,1)S(1)}, bf16[64,1536]{1,0:T(8,128)(2,1)S(1)}, u32[]{:S(2)}, u32[]{:S(2)}) collective-permute-start(bf16[64,1536]{1,0:T(8,128)(2,1)S(1)} %pad_maximum_fusion.2.refs_4_), channel_id=1, source_target_pairs={{0,8},{2,10},{4,12},{6,14},{8,0},{10,2},{12,4},{14,6},{16,24},{18,... | collective-permute-start | bytes 589832 | tf_op jit(solution)/shard_map/ppermute | solution.py:31
  4.8 2.5 %collective-permute-start.1 = (bf16[64,1536]{1,0:T(8,128)(2,1)S(1)}, bf16[64,1536]{1,0:T(8,128)(2,1)S(1)}, u32[]{:S(2)}, u32[]{:S(2)}) collective-permute-start(bf16[64,1536]{1,0:T(8,128)(2,1)S(1)} %pad_maximum_fusion.2.refs_4_), channel_id=1, source_target_pairs={{0,24},{2,26},{4,28},{6,30},{8,16},{10,18},{12,20},{14,22},{16,8},... | collective-permute-start | bytes 589832 | tf_op jit(solution)/shard_map/ppermute | solution.py:31
  7.2 0.9 %pad_maximum_fusion = bf16[64,2560]{1,0:T(8,128)(2,1)S(1)} fusion(bf16[64,1024]{1,0:T(8,128)(2,1)} %param.14, bf16[64,512]{1,0:T(8,128)(2,1)S(1)} %get-tuple-element.33, bf16[64,512]{1,0:T(8,128)(2,1)S(1)} %get-tuple-element.34, bf16[64,512]{1,0:T(8,128)(2,1)S(1)} %get-tuple-element.32), kind=kLoop, calls=%fused_computation.1 | loop fusion | flops 1310720 | bytes 655360 | tf_op jit(solution)/shard_map/concatenate | solution.py:276
  8.2 1.6 %collective-permute-start.4 = (bf16[64,2560]{1,0:T(8,128)(2,1)S(1)}, bf16[64,2560]{1,0:T(8,128)(2,1)S(1)}, u32[]{:S(2)}, u32[]{:S(2)}) collective-permute-start(bf16[64,2560]{1,0:T(8,128)(2,1)S(1)} %pad_maximum_fusion), channel_id=1, source_target_pairs={{0,4},{2,6},{4,0},{6,2},{8,12},{10,14},{12,8},{14,10},{16,20},{18,... | collective-permute-start | bytes 983048 | tf_op jit(solution)/shard_map/ppermute | solution.py:31
  9.7 1.5 %collective-permute-start = (s32[3,6]{1,0:T(4,128)S(1)}, s32[3,6]{1,0:T(4,128)S(1)}, u32[]{:S(2)}, u32[]{:S(2)}) collective-permute-start(s32[3,6]{1,0:T(4,128)S(1)} %bitcast.24), channel_id=1, source_target_pairs={{0,1},{1,0},{2,3},{3,2},{4,5},{5,4},{6,7},{7,6},{8,9},{9,8},{10,11... | collective-permute-start | bytes 224 | tf_op jit(solution)/shard_map/ppermute | solution.py:31
  11.3 2.0 %collective-permute-done.refs_0_ = s32[3,6]{1,0:T(4,128)S(1)} collective-permute-done((s32[3,6]{1,0:T(4,128)S(1)}, s32[3,6]{1,0:T(4,128)S(1)}, u32[]{:S(2)}, u32[]{:S(2)}) %collective-permute-start) | collective-permute-done | bytes 104 | tf_op jit(solution)/shard_map/ppermute | solution.py:31
  13.3 1.5 %collective-permute-start.7 = (bf16[384,1024]{1,0:T(8,128)(2,1)S(1)}, bf16[384,1024]{1,0:T(8,128)(2,1)S(1)}, u32[]{:S(2)}, u32[]{:S(2)}) collective-permute-start(bf16[384,1024]{1,0:T(8,128)(2,1)S(1)} %bitcast.14), channel_id=1, source_target_pairs={{0,1},{1,0},{2,3},{3,2},{4,5},{5,4},{6,7},{7,6},{8,9},{9,8},{10,11... | collective-permute-start | bytes 2359304 | tf_op jit(solution)/shard_map/ppermute | solution.py:31
  15.1 1.1 %collective-permute-done.1.refs_16_ = bf16[64,1536]{1,0:T(8,128)(2,1)S(1)} collective-permute-done((bf16[64,1536]{1,0:T(8,128)(2,1)S(1)}, bf16[64,1536]{1,0:T(8,128)(2,1)S(1)}, u32[]{:S(2)}, u32[]{:S(2)}) %collective-permute-start.1) | collective-permute-done | bytes 196640 | tf_op jit(solution)/shard_map/ppermute | solution.py:31
  16.8 1.5 %collective-permute-start.6 = (bf16[64,1536]{1,0:T(8,128)(2,1)S(1)}, bf16[64,1536]{1,0:T(8,128)(2,1)S(1)}, u32[]{:S(2)}, u32[]{:S(2)}) collective-permute-start(bf16[64,1536]{1,0:T(8,128)(2,1)S(1)} %collective-permute-done.1.refs_16_), channel_id=1, source_target_pairs={{0,4},{2,6},{4,0},{6,2},{8,12},{10,14},{12,8},{14,10},{16,20},{18,... | collective-permute-start | bytes 589832 | tf_op jit(solution)/shard_map/ppermute | solution.py:31
  18.7 1.5 %collective-permute-start.5 = (bf16[64,1536]{1,0:T(8,128)(2,1)S(1)}, bf16[64,1536]{1,0:T(8,128)(2,1)S(1)}, u32[]{:S(2)}, u32[]{:S(2)}) collective-permute-start(bf16[64,1536]{1,0:T(8,128)(2,1)S(1)} %collective-permute-done.3.refs_8_), channel_id=1, source_target_pairs={{0,4},{2,6},{4,0},{6,2},{8,12},{10,14},{12,8},{14,10},{16,20},{18,... | collective-permute-start | bytes 589832 | tf_op jit(solution)/shard_map/ppermute | solution.py:31
  20.2 1.6 %collective-permute-done.2.refs_12_ = bf16[64,1536]{1,0:T(8,128)(2,1)S(1)} collective-permute-done((bf16[64,1536]{1,0:T(8,128)(2,1)S(1)}, bf16[64,1536]{1,0:T(8,128)(2,1)S(1)}, u32[]{:S(2)}, u32[]{:S(2)}) %collective-permute-start.2) | collective-permute-done | bytes 196640 | tf_op jit(solution)/shard_map/ppermute | solution.py:31
  21.9 2.6 %collective-permute-done.6.refs_18_ = bf16[64,1536]{1,0:T(8,128)(2,1)S(1)} collective-permute-done((bf16[64,1536]{1,0:T(8,128)(2,1)S(1)}, bf16[64,1536]{1,0:T(8,128)(2,1)S(1)}, u32[]{:S(2)}, u32[]{:S(2)}) %collective-permute-start.6) | collective-permute-done | bytes 196640 | tf_op jit(solution)/shard_map/ppermute | solution.py:31
  24.5 1.5 %collective-permute-start.13 = (bf16[64,1536]{1,0:T(8,128)(2,1)S(1)}, bf16[64,1536]{1,0:T(8,128)(2,1)S(1)}, u32[]{:S(2)}, u32[]{:S(2)}) collective-permute-start(bf16[64,1536]{1,0:T(8,128)(2,1)S(1)} %collective-permute-done.2.refs_12_), channel_id=1, source_target_pairs={{0,4},{2,6},{4,0},{6,2},{8,12},{10,14},{12,8},{14,10},{16,20},{18,... | collective-permute-start | bytes 589832 | tf_op jit(solution)/shard_map/ppermute | solution.py:31
  26.0 2.6 %collective-permute-done.5.refs_10_ = bf16[64,1536]{1,0:T(8,128)(2,1)S(1)} collective-permute-done((bf16[64,1536]{1,0:T(8,128)(2,1)S(1)}, bf16[64,1536]{1,0:T(8,128)(2,1)S(1)}, u32[]{:S(2)}, u32[]{:S(2)}) %collective-permute-start.5) | collective-permute-done | bytes 196640 | tf_op jit(solution)/shard_map/ppermute | solution.py:31
  28.6 0.9 %copy-done.9 = bf16[64,1024]{1,0:T(8,128)(2,1)S(1)} copy-done((bf16[64,1024]{1,0:T(8,128)(2,1)S(1)}, bf16[64,1024]{1,0:T(8,128)(2,1)}, u32[]{:S(2)}) %copy-start.9) | copy-done | bytes 131096
  30.1 1.8 %collective-permute-start.21 = (bf16[128,1024]{1,0:T(8,128)(2,1)S(1)}, bf16[128,1024]{1,0:T(8,128)(2,1)S(1)}, u32[]{:S(2)}, u32[]{:S(2)}) collective-permute-start(bf16[128,1024]{1,0:T(8,128)(2,1)S(1)} %pad_maximum_fusion.1.refs_2_), channel_id=1, source_target_pairs={{0,24},{2,26},{4,28},{6,30},{8,16},{10,18},{12,20},{14,22},{16,8},... | collective-permute-start | bytes 786440 | tf_op jit(solution)/shard_map/ppermute | solution.py:31
  34.3 5.2 %project.1 = (bf16[384,512]{1,0:T(8,128)(2,1)S(1)}, bf16[384,512]{1,0:T(8,128)(2,1)S(1)}, bf16[768,512]{1,0:T(8,128)(2,1)S(1)}, bf16[4,144,768]{2,1,0:T(8,128)(2,1)S(1)}) custom-call(s32[3,6]{1,0:T(4,128)S(1)} %copy-done.6, bf16[128,1024]{1,0:T(8,128)(2,1)S(1)} %norm.3.refs_1_, bf16[256,1024]{1,0:T(8,128)(2,1)S(1)} %norm.4.refs_2_, ...), custom_call_target="tpu_custom_call" | custom-call | tf_op jit(solution)/shard_map/project/pallas_call | solution.py:313
  39.5 1.6 %collective-permute-start.17 = (bf16[384,512]{1,0:T(8,128)(2,1)S(1)}, bf16[384,512]{1,0:T(8,128)(2,1)S(1)}, u32[]{:S(2)}, u32[]{:S(2)}) collective-permute-start(bf16[384,512]{1,0:T(8,128)(2,1)S(1)} %get-tuple-element.23), channel_id=1, source_target_pairs={{0,1},{1,0},{2,3},{3,2},{4,5},{5,4},{6,7},{7,6},{8,9},{9,8},{10,11... | collective-permute-start | bytes 1179656 | tf_op jit(solution)/shard_map/ppermute | solution.py:31
  41.1 4.3 %collective-permute-start.23 = (bf16[128,1024]{1,0:T(8,128)(2,1)S(1)}, bf16[128,1024]{1,0:T(8,128)(2,1)S(1)}, u32[]{:S(2)}, u32[]{:S(2)}) collective-permute-start(bf16[128,1024]{1,0:T(8,128)(2,1)S(1)} %collective-permute-done.21.refs_6_), channel_id=1, source_target_pairs={{0,8},{2,10},{4,12},{6,14},{8,0},{10,2},{12,4},{14,6},{16,24},{18,... | collective-permute-start | bytes 786440 | tf_op jit(solution)/shard_map/ppermute | solution.py:31
  46.1 2.3 %own_strip.1.refs_0_ = bf16[384,512]{1,0:T(8,128)(2,1)S(1)} custom-call(s32[3,6]{1,0:T(4,128)S(1)} %bitcast.25, bf16[384,512]{1,0:T(8,128)(2,1)S(1)} %get-tuple-element.20.query_ref, bf16[768,512]{1,0:T(8,128)(2,1)S(1)} %get-tuple-element.21.key_ref, bf16[4,144,768]{2,1,0:T(8,128)(2,1)S(1)} %get-tuple-element.22.value_ref), custom_call_target="tpu_custom_call" | custom-call | flops 99999997952 | tf_op jit(solution)/shard_map/own_strip/pallas_call | solution.py:337
  49.0 2.5 %collective-permute-done.23.refs_8_ = bf16[128,1024]{1,0:T(8,128)(2,1)S(1)} collective-permute-done((bf16[128,1024]{1,0:T(8,128)(2,1)S(1)}, bf16[128,1024]{1,0:T(8,128)(2,1)S(1)}, u32[]{:S(2)}, u32[]{:S(2)}) %collective-permute-start.23) | collective-permute-done | bytes 262176 | tf_op jit(solution)/shard_map/ppermute | solution.py:31
  51.5 1.5 %collective-permute-done.24.refs_9_ = bf16[128,1024]{1,0:T(8,128)(2,1)S(1)} collective-permute-done((bf16[128,1024]{1,0:T(8,128)(2,1)S(1)}, bf16[128,1024]{1,0:T(8,128)(2,1)S(1)}, u32[]{:S(2)}, u32[]{:S(2)}) %collective-permute-start.24) | collective-permute-done | bytes 262176 | tf_op jit(solution)/shard_map/ppermute | solution.py:31
  53.0 2.0 %output.1 = (bf16[384,1024]{1,0:T(8,128)(2,1)}, bf16[384,1024]{1,0:T(8,128)(2,1)}) custom-call(bf16[384,512]{1,0:T(8,128)(2,1)S(1)} %own_strip.1.refs_0_, bf16[384,512]{1,0:T(8,128)(2,1)S(1)} %collective-permute-done.17.refs_1_, bf16[128,1024]{1,0:T(8,128)(2,1)S(1)} %pad_maximum_fusion.1.refs_2_, bf16[128,1024]{1,0:T(8,128)(2,1)S(1)} %collective-permute-done.18.refs_3_, ...), custom_call_target="tpu_custom_call" | custom-call | flops 805306368 | bytes 2097152 | tf_op jit(solution)/shard_map/output/pallas_call | solution.py:354
  (62 shorter events, 5.8 us)
Async XLA Ops:
  1.7 15.1 %collective-permute-start.3 = (bf16[64,1536]{1,0:T(8,128)(2,1)S(1)}, bf16[64,1536]{1,0:T(8,128)(2,1)S(1)}, u32[]{:S(2)}, u32[]{:S(2)}) collective-permute-start(bf16[64,1536]{1,0:T(8,128)(2,1)S(1)} %pad_maximum_fusion.2.refs_4_), channel_id=1, source_target_pairs={{0,8},{2,10},{4,12},{6,14},{8,0},{10,2},{12,4},{14,6},{16,24},{18,... | collective-permute-start | bytes 589832 | tf_op jit(solution)/shard_map/ppermute | solution.py:31
  4.8 11.4 %collective-permute-start.1 = (bf16[64,1536]{1,0:T(8,128)(2,1)S(1)}, bf16[64,1536]{1,0:T(8,128)(2,1)S(1)}, u32[]{:S(2)}, u32[]{:S(2)}) collective-permute-start(bf16[64,1536]{1,0:T(8,128)(2,1)S(1)} %pad_maximum_fusion.2.refs_4_), channel_id=1, source_target_pairs={{0,24},{2,26},{4,28},{6,30},{8,16},{10,18},{12,20},{14,22},{16,8},... | collective-permute-start | bytes 589832 | tf_op jit(solution)/shard_map/ppermute | solution.py:31
  7.2 13.0 %collective-permute-start.8 = (bf16[64,1536]{1,0:T(8,128)(2,1)S(1)}, bf16[64,1536]{1,0:T(8,128)(2,1)S(1)}, u32[]{:S(2)}, u32[]{:S(2)}) collective-permute-start(bf16[64,1536]{1,0:T(8,128)(2,1)S(1)} %pad_maximum_fusion.2.refs_4_), channel_id=1, source_target_pairs={{0,2},{2,0},{4,6},{6,4},{8,10},{10,8},{12,14},{14,12},{16,18},{18,... | collective-permute-start | bytes 589832 | tf_op jit(solution)/shard_map/ppermute | solution.py:31
  8.2 10.6 %collective-permute-start.4 = (bf16[64,2560]{1,0:T(8,128)(2,1)S(1)}, bf16[64,2560]{1,0:T(8,128)(2,1)S(1)}, u32[]{:S(2)}, u32[]{:S(2)}) collective-permute-start(bf16[64,2560]{1,0:T(8,128)(2,1)S(1)} %pad_maximum_fusion), channel_id=1, source_target_pairs={{0,4},{2,6},{4,0},{6,2},{8,12},{10,14},{12,8},{14,10},{16,20},{18,... | collective-permute-start | bytes 983048 | tf_op jit(solution)/shard_map/ppermute | solution.py:31
  9.7 3.6 %collective-permute-start = (s32[3,6]{1,0:T(4,128)S(1)}, s32[3,6]{1,0:T(4,128)S(1)}, u32[]{:S(2)}, u32[]{:S(2)}) collective-permute-start(s32[3,6]{1,0:T(4,128)S(1)} %bitcast.24), channel_id=1, source_target_pairs={{0,1},{1,0},{2,3},{3,2},{4,5},{5,4},{6,7},{7,6},{8,9},{9,8},{10,11... | collective-permute-start | bytes 224 | tf_op jit(solution)/shard_map/ppermute | solution.py:31
  13.3 19.0 %collective-permute-start.7 = (bf16[384,1024]{1,0:T(8,128)(2,1)S(1)}, bf16[384,1024]{1,0:T(8,128)(2,1)S(1)}, u32[]{:S(2)}, u32[]{:S(2)}) collective-permute-start(bf16[384,1024]{1,0:T(8,128)(2,1)S(1)} %bitcast.14), channel_id=1, source_target_pairs={{0,1},{1,0},{2,3},{3,2},{4,5},{5,4},{6,7},{7,6},{8,9},{9,8},{10,11... | collective-permute-start | bytes 2359304 | tf_op jit(solution)/shard_map/ppermute | solution.py:31
  16.2 5.7 %collective-permute-start.2 = (bf16[64,1536]{1,0:T(8,128)(2,1)S(1)}, bf16[64,1536]{1,0:T(8,128)(2,1)S(1)}, u32[]{:S(2)}, u32[]{:S(2)}) collective-permute-start(bf16[64,1536]{1,0:T(8,128)(2,1)S(1)} %collective-permute-done.1.refs_16_), channel_id=1, source_target_pairs={{0,8},{2,10},{4,12},{6,14},{8,0},{10,2},{12,4},{14,6},{16,24},{18,... | collective-permute-start | bytes 589832 | tf_op jit(solution)/shard_map/ppermute | solution.py:31
  16.8 7.7 %collective-permute-start.6 = (bf16[64,1536]{1,0:T(8,128)(2,1)S(1)}, bf16[64,1536]{1,0:T(8,128)(2,1)S(1)}, u32[]{:S(2)}, u32[]{:S(2)}) collective-permute-start(bf16[64,1536]{1,0:T(8,128)(2,1)S(1)} %collective-permute-done.1.refs_16_), channel_id=1, source_target_pairs={{0,4},{2,6},{4,0},{6,2},{8,12},{10,14},{12,8},{14,10},{16,20},{18,... | collective-permute-start | bytes 589832 | tf_op jit(solution)/shard_map/ppermute | solution.py:31
  18.7 9.8 %collective-permute-start.5 = (bf16[64,1536]{1,0:T(8,128)(2,1)S(1)}, bf16[64,1536]{1,0:T(8,128)(2,1)S(1)}, u32[]{:S(2)}, u32[]{:S(2)}) collective-permute-start(bf16[64,1536]{1,0:T(8,128)(2,1)S(1)} %collective-permute-done.3.refs_8_), channel_id=1, source_target_pairs={{0,4},{2,6},{4,0},{6,2},{8,12},{10,14},{12,8},{14,10},{16,20},{18,... | collective-permute-start | bytes 589832 | tf_op jit(solution)/shard_map/ppermute | solution.py:31
  20.2 9.2 %collective-permute-start.10 = (bf16[64,1536]{1,0:T(8,128)(2,1)S(1)}, bf16[64,1536]{1,0:T(8,128)(2,1)S(1)}, u32[]{:S(2)}, u32[]{:S(2)}) collective-permute-start(bf16[64,1536]{1,0:T(8,128)(2,1)S(1)} %collective-permute-done.3.refs_8_), channel_id=1, source_target_pairs={{0,2},{2,0},{4,6},{6,4},{8,10},{10,8},{12,14},{14,12},{16,18},{18,... | collective-permute-start | bytes 589832 | tf_op jit(solution)/shard_map/ppermute | solution.py:31
  21.9 8.2 %collective-permute-start.15 = (bf16[64,1536]{1,0:T(8,128)(2,1)S(1)}, bf16[64,1536]{1,0:T(8,128)(2,1)S(1)}, u32[]{:S(2)}, u32[]{:S(2)}) collective-permute-start(bf16[64,1536]{1,0:T(8,128)(2,1)S(1)} %collective-permute-done.1.refs_16_), channel_id=1, source_target_pairs={{0,2},{2,0},{4,6},{6,4},{8,10},{10,8},{12,14},{14,12},{16,18},{18,... | collective-permute-start | bytes 589832 | tf_op jit(solution)/shard_map/ppermute | solution.py:31
  24.5 7.4 %collective-permute-start.13 = (bf16[64,1536]{1,0:T(8,128)(2,1)S(1)}, bf16[64,1536]{1,0:T(8,128)(2,1)S(1)}, u32[]{:S(2)}, u32[]{:S(2)}) collective-permute-start(bf16[64,1536]{1,0:T(8,128)(2,1)S(1)} %collective-permute-done.2.refs_12_), channel_id=1, source_target_pairs={{0,4},{2,6},{4,0},{6,2},{8,12},{10,14},{12,8},{14,10},{16,20},{18,... | collective-permute-start | bytes 589832 | tf_op jit(solution)/shard_map/ppermute | solution.py:31
  28.5 3.3 %collective-permute-start.12 = (bf16[64,1536]{1,0:T(8,128)(2,1)S(1)}, bf16[64,1536]{1,0:T(8,128)(2,1)S(1)}, u32[]{:S(2)}, u32[]{:S(2)}) collective-permute-start(bf16[64,1536]{1,0:T(8,128)(2,1)S(1)} %collective-permute-done.2.refs_12_), channel_id=1, source_target_pairs={{0,2},{2,0},{4,6},{6,4},{8,10},{10,8},{12,14},{14,12},{16,18},{18,... | collective-permute-start | bytes 589832 | tf_op jit(solution)/shard_map/ppermute | solution.py:31
  29.5 4.8 %collective-permute-start.9 = (bf16[64,2560]{1,0:T(8,128)(2,1)S(1)}, bf16[64,2560]{1,0:T(8,128)(2,1)S(1)}, u32[]{:S(2)}, u32[]{:S(2)}) collective-permute-start(bf16[64,2560]{1,0:T(8,128)(2,1)S(1)} %collective-permute-done.4.refs_6_), channel_id=1, source_target_pairs={{0,2},{2,0},{4,6},{6,4},{8,10},{10,8},{12,14},{14,12},{16,18},{18,... | collective-permute-start | bytes 983048 | tf_op jit(solution)/shard_map/ppermute | solution.py:31
  30.1 11.0 %collective-permute-start.21 = (bf16[128,1024]{1,0:T(8,128)(2,1)S(1)}, bf16[128,1024]{1,0:T(8,128)(2,1)S(1)}, u32[]{:S(2)}, u32[]{:S(2)}) collective-permute-start(bf16[128,1024]{1,0:T(8,128)(2,1)S(1)} %pad_maximum_fusion.1.refs_2_), channel_id=1, source_target_pairs={{0,24},{2,26},{4,28},{6,30},{8,16},{10,18},{12,20},{14,22},{16,8},... | collective-permute-start | bytes 786440 | tf_op jit(solution)/shard_map/ppermute | solution.py:31
  31.8 2.0 %collective-permute-start.16 = (bf16[64,1536]{1,0:T(8,128)(2,1)S(1)}, bf16[64,1536]{1,0:T(8,128)(2,1)S(1)}, u32[]{:S(2)}, u32[]{:S(2)}) collective-permute-start(bf16[64,1536]{1,0:T(8,128)(2,1)S(1)} %collective-permute-done.6.refs_18_), channel_id=1, source_target_pairs={{0,2},{2,0},{4,6},{6,4},{8,10},{10,8},{12,14},{14,12},{16,18},{18,... | collective-permute-start | bytes 589832 | tf_op jit(solution)/shard_map/ppermute | solution.py:31
  31.9 2.4 %collective-permute-start.11 = (bf16[64,1536]{1,0:T(8,128)(2,1)S(1)}, bf16[64,1536]{1,0:T(8,128)(2,1)S(1)}, u32[]{:S(2)}, u32[]{:S(2)}) collective-permute-start(bf16[64,1536]{1,0:T(8,128)(2,1)S(1)} %collective-permute-done.5.refs_10_), channel_id=1, source_target_pairs={{0,2},{2,0},{4,6},{6,4},{8,10},{10,8},{12,14},{14,12},{16,18},{18,... | collective-permute-start | bytes 589832 | tf_op jit(solution)/shard_map/ppermute | solution.py:31
  32.4 1.9 %collective-permute-start.14 = (bf16[64,1536]{1,0:T(8,128)(2,1)S(1)}, bf16[64,1536]{1,0:T(8,128)(2,1)S(1)}, u32[]{:S(2)}, u32[]{:S(2)}) collective-permute-start(bf16[64,1536]{1,0:T(8,128)(2,1)S(1)} %collective-permute-done.13.refs_14_), channel_id=1, source_target_pairs={{0,2},{2,0},{4,6},{6,4},{8,10},{10,8},{12,14},{14,12},{16,18},{18,... | collective-permute-start | bytes 589832 | tf_op jit(solution)/shard_map/ppermute | solution.py:31
  33.8 14.6 %collective-permute-start.19 = (bf16[128,1024]{1,0:T(8,128)(2,1)S(1)}, bf16[128,1024]{1,0:T(8,128)(2,1)S(1)}, u32[]{:S(2)}, u32[]{:S(2)}) collective-permute-start(bf16[128,1024]{1,0:T(8,128)(2,1)S(1)} %pad_maximum_fusion.1.refs_2_), channel_id=1, source_target_pairs={{0,8},{2,10},{4,12},{6,14},{8,0},{10,2},{12,4},{14,6},{16,24},{18,... | collective-permute-start | bytes 786440 | tf_op jit(solution)/shard_map/ppermute | solution.py:31
  39.5 12.0 %collective-permute-start.17 = (bf16[384,512]{1,0:T(8,128)(2,1)S(1)}, bf16[384,512]{1,0:T(8,128)(2,1)S(1)}, u32[]{:S(2)}, u32[]{:S(2)}) collective-permute-start(bf16[384,512]{1,0:T(8,128)(2,1)S(1)} %get-tuple-element.23), channel_id=1, source_target_pairs={{0,1},{1,0},{2,3},{3,2},{4,5},{5,4},{6,7},{7,6},{8,9},{9,8},{10,11... | collective-permute-start | bytes 1179656 | tf_op jit(solution)/shard_map/ppermute | solution.py:31
  41.1 10.4 %collective-permute-start.23 = (bf16[128,1024]{1,0:T(8,128)(2,1)S(1)}, bf16[128,1024]{1,0:T(8,128)(2,1)S(1)}, u32[]{:S(2)}, u32[]{:S(2)}) collective-permute-start(bf16[128,1024]{1,0:T(8,128)(2,1)S(1)} %collective-permute-done.21.refs_6_), channel_id=1, source_target_pairs={{0,8},{2,10},{4,12},{6,14},{8,0},{10,2},{12,4},{14,6},{16,24},{18,... | collective-permute-start | bytes 786440 | tf_op jit(solution)/shard_map/ppermute | solution.py:31
  48.4 3.1 %collective-permute-start.22 = (bf16[128,1024]{1,0:T(8,128)(2,1)S(1)}, bf16[128,1024]{1,0:T(8,128)(2,1)S(1)}, u32[]{:S(2)}, u32[]{:S(2)}) collective-permute-start(bf16[128,1024]{1,0:T(8,128)(2,1)S(1)} %collective-permute-done.21.refs_6_), channel_id=1, source_target_pairs={{0,2},{2,0},{4,6},{6,4},{8,10},{10,8},{12,14},{14,12},{16,18},{18,... | collective-permute-start | bytes 786440 | tf_op jit(solution)/shard_map/ppermute | solution.py:31
  48.5 3.1 %collective-permute-start.20 = (bf16[128,1024]{1,0:T(8,128)(2,1)S(1)}, bf16[128,1024]{1,0:T(8,128)(2,1)S(1)}, u32[]{:S(2)}, u32[]{:S(2)}) collective-permute-start(bf16[128,1024]{1,0:T(8,128)(2,1)S(1)} %collective-permute-done.19.refs_4_), channel_id=1, source_target_pairs={{0,2},{2,0},{4,6},{6,4},{8,10},{10,8},{12,14},{14,12},{16,18},{18,... | collective-permute-start | bytes 786440 | tf_op jit(solution)/shard_map/ppermute | solution.py:31
  49.0 2.6 %collective-permute-start.18 = (bf16[128,1024]{1,0:T(8,128)(2,1)S(1)}, bf16[128,1024]{1,0:T(8,128)(2,1)S(1)}, u32[]{:S(2)}, u32[]{:S(2)}) collective-permute-start(bf16[128,1024]{1,0:T(8,128)(2,1)S(1)} %pad_maximum_fusion.1.refs_2_), channel_id=1, source_target_pairs={{0,2},{2,0},{4,6},{6,4},{8,10},{10,8},{12,14},{14,12},{16,18},{18,... | collective-permute-start | bytes 786440 | tf_op jit(solution)/shard_map/ppermute | solution.py:31
  (12 other events, 41.6 us)

commit v4 on v3

--- a/solution.py
+++ b/solution.py
@@ -14,6 +14,7 @@
 PAIR = 2 * HEAD_DIM
 
 ROUND = 3
+ROWS = 16
 LONG = 10**11
 
 NEG_FILL = -1e30
@@ -24,11 +25,12 @@
 SMEM = pl.BlockSpec(memory_space=pltpu.SMEM)
 
 
-def swap(block, axis, distance):
+def swap(block, axis, distance, what="block"):
     if distance == 0:
         return block
     size = lax.axis_size(axis)
-    return lax.ppermute(block, axis, [(i, i ^ distance) for i in range(size)])
+    with jax.named_scope(what):
+        return lax.ppermute(block, axis, [(i, i ^ distance) for i in range(size)])
 
 
 def call(kernel, out_shape, in_specs, scratch=(), flops=0, nbytes=0, name=None):
@@ -50,7 +52,7 @@
 def norm_kernel(sheet_ref, gain_ref, bias_ref, out_ref):
     step = 32
 
-    @pl.loop(0, sheet_ref.shape[0] // step, unroll=4)
+    @pl.loop(0, out_ref.shape[0] // step, unroll=4)
     def _(index):
         rows = pl.ds(pl.multiple_of(index * step, step), step)
         values = sheet_ref[rows, :].astype(jnp.float32)
@@ -256,13 +258,18 @@
         )
 
     own = mine_of(w_qkv)
-    masks_of = [swap(masks[0], "seq", k) for k in range(strips)]
-    sheets = [swap(after(sheet, *masks_of[1:]) if k else sheet, "seq", k) for k in range(strips)]
+    wide = jnp.zeros((ROWS, features), jnp.bfloat16)
+    wide = lax.dynamic_update_slice(wide, masks[0].astype(jnp.bfloat16), (0, 0))
+    sent = jnp.concatenate([sheet, wide], axis=0)
+    sheets = [sheet] + [swap(sent, "seq", k, "tokens") for k in range(1, strips)]
+    masks_of = [masks[0]] + [
+        block[length : length + per_strip, :blocks].astype(jnp.int32) for block in sheets[1:]
+    ]
 
     def norm(block, flops=0):
         return call(
             norm_kernel,
-            jax.ShapeDtypeStruct(block.shape, jnp.bfloat16),
+            jax.ShapeDtypeStruct((length, features), jnp.bfloat16),
             [VMEM] * 3,
             flops=flops,
             name="norm",
@@ -275,32 +282,31 @@
     pieces = {0: own}
     both = jnp.concatenate([own, w_out], axis=1)
     for x in across:
-        pieces[x] = swap(both, "dp", x)
-    pieces[second] = swap(own, "dp", second)
-    pieces[first] = swap(own, "dp", first)
-    normed = [norm(sheet[:BLOCK], LONG)]
+        pieces[x] = swap(both, "dp", x, "in_x")
+    pieces[second] = swap(own, "dp", second, "in_z3")
+    pieces[first] = swap(own, "dp", first, "in_z1")
+    normed = [norm(sheet, LONG)]
 
     one = after(pieces[first], pieces[across[0]], normed[0])
     for x in across:
-        pieces[first + x] = swap(one, "dp", x)
+        pieces[first + x] = swap(one, "dp", x, "in_z1_x")
     out_near = [w_out, *(pieces[x][:, 3 * width :] for x in across)]
     out_own = jnp.concatenate(out_near, axis=0)
 
-    pieces[third] = swap(pieces[second], "dp", first)
+    pieces[third] = swap(pieces[second], "dp", first, "in_z2")
     for x in across:
-        pieces[second + x] = swap(pieces[second], "dp", x)
+        pieces[second + x] = swap(pieces[second], "dp", x, "in_z3_x")
 
     for x in across:
-        pieces[third + x] = swap(pieces[third], "dp", x)
+        pieces[third + x] = swap(pieces[third], "dp", x, "in_z2_x")
     out_ready = after(out_own, pieces[third])
-    out_second = swap(out_ready, "dp", second)
-    out_first = swap(out_ready, "dp", first)
+    out_second = swap(out_ready, "dp", second, "out_z3")
+    out_first = swap(out_ready, "dp", first, "out_z1")
     before = [pieces[slot] for slot in (third, first + across[0], second + across[0])]
-    normed.append(norm(after(sheet[BLOCK:], normed[0], *before), LONG))
-    normed.extend(norm(sheets[k]) for k in range(1, strips))
+    normed.extend(norm(after(sheets[k], normed[0], *before), 0) for k in range(1, strips))
 
     for slot in sorted(pieces):
-        pieces[slot + 1] = swap(pieces[slot], "dp", 1)
+        pieces[slot + 1] = swap(pieces[slot], "dp", 1, f"in_core_{slot}")
     slots = sorted(pieces)
 
     work = [
@@ -333,7 +339,7 @@
         qkv_bias[None],
     )
 
-    returned = [swap(block, "seq", k + 1) for k, block in enumerate(away)]
+    returned = [swap(block, "seq", k + 1, "context") for k, block in enumerate(away)]
     mine = call(
         functools.partial(own_kernel, strips),
         strip_out,
@@ -343,13 +349,13 @@
         name="own_strip",
     )(masks_of[0], query, key, value)
 
-    out_third = swap(after(out_second, *away), "dp", first)
+    out_third = swap(after(out_second, *away), "dp", first, "out_z2")
     out_slots, out_pieces = [], []
     for far, piece in ((0, out_own), (first, out_first), (second, out_second), (third, out_third)):
         out_slots.append([far + x for x in (0, *across)])
         out_pieces.append(piece)
         out_slots.append([far + x + 1 for x in (0, *across)])
-        out_pieces.append(swap(after(piece, mine), "dp", 1))
+        out_pieces.append(swap(after(piece, mine), "dp", 1, f"out_core_{far}"))
 
     updated, context = call(
         functools.partial(output_kernel, strips, out_slots),

time: 55.3 us -> 54 us (0.976)
  starting transfers between devices: 25.2 us -> 23.4 us
  Pallas kernels: 11.1 us -> 12.8 us
  local copies, waits for them, and re-layouts: 2.67 us -> 1.05 us
  waiting for transfers between devices: 14.4 us -> 15.7 us
  other arithmetic: 0.96 us -> 0.12 us
    ppermute x25 -> x24, starting transfers between devices: 25.2 us -> 23.4 us  [swap(): return lax.ppermute(block, axis, [(i, i ^ distance) for i in range(size)])]
    unnamed x23 -> x14, local copies, waits for them, and re-layouts: 1.61 us -> 0.04 us
    ppermute x25 -> x24, waiting for transfers between devices: 14.4 us -> 15.7 us  [swap(): return lax.ppermute(block, axis, [(i, i ^ distance) for i in range(size)])]
    concatenate x1, other arithmetic: 0.93 us -> 0.02 us  [on_device(): both = jnp.concatenate([own, w_out], axis=1)]
    pallas_call x1, Pallas kernels: 5.2 us -> 6.03 us  [on_device(): call(functools.partial(project_kernel, strips, len(normed), [[slot] for s...]
    pallas_call x1, Pallas kernels: 2.25 us -> 3.07 us  [on_device(): call(functools.partial(own_kernel, strips), strip_out, [SMEM] + [VMEM] *...]
    pallas_call x3 -> x2, Pallas kernels: 1.6 us -> 1.6 us  [norm(): call(norm_kernel, jax.ShapeDtypeStruct((length, features), jnp.bfloat16),...]
  transfers between devices with their start and end apart: 25 -> 24, of which waited for: 8 -> 9; matrix products, arithmetic and copies ran while one was open for 2% -> 0% of each run, Pallas kernels for 16% -> 20%
where the time goes in v4:
time: 54 us; the launch traced here: 53.9 us
  starting transfers between devices  23.4 us (43%)
  waiting for transfers between devices  15.7 us (29%)
  Pallas kernels  12.8 us (24%)
  local copies, waits for them, and re-layouts  1.05 us (2%)
  between operations  0.86 us (2%)
    ppermute x24, starting transfers between devices, swap(): return lax.ppermute(block, axis, [(i, i ^ distance) for i in range(size)])  23.4 us
    ppermute x24, waiting for transfers between devices, swap(): return lax.ppermute(block, axis, [(i, i ^ distance) for i in range(size)])  15.7 us
    pallas_call x1, Pallas kernels, on_device(): call(functools.partial(project_kernel, strips, len(normed), [[slot] for s...  6.03 us
    pallas_call x1, Pallas kernels, on_device(): call(functools.partial(own_kernel, strips), strip_out, [SMEM] + [VMEM] *...  3.07 us
    pallas_call x1, Pallas kernels, on_device(): call(functools.partial(output_kernel, strips, out_slots), [jax.ShapeDtype...  2.06 us
    pallas_call x2, Pallas kernels, norm(): call(norm_kernel, jax.ShapeDtypeStruct((length, features), jnp.bfloat16),...  1.6 us
  transfers between devices with their start and end apart: 24, of which 9 were waited for; matrix products, arithmetic and copies ran while one was open for 0% of the time, Pallas kernels for 20%

profile of v4, /device:TPU:0, one launch (start us, length us, event | category | flops | bytes accessed | tf_op | source)
XLA Modules:
  0.0 53.9 jit_solution(13094418755260880402)
XLA Ops:
  0.7 1.0 %constant_dynamic-slice_fusion.2 = (bf16[64,512]{1,0:T(8,128)(2,1)S(1)}, bf16[64,512]{1,0:T(8,128)(2,1)S(1)}, bf16[64,512]{1,0:T(8,128)(2,1)S(1)}) fusion(bf16[64,3072]{1,0:T(8,128)(2,1)} %param.12, s32[]{:T(128)S(6)} %select_n.9, s32[]{:T(128)S(6)} %select_n.11, s32[]{:T(128)S(6)} %select_n.10), kind=kLoop, calls=%fused_computation.10 | loop fusion | bytes 393228 | tf_op jit(solution)/shard_map/dynamic_slice | solution.py:257
  1.7 5.1 %collective-permute-start.1 = (bf16[64,1536]{1,0:T(8,128)(2,1)S(1)}, bf16[64,1536]{1,0:T(8,128)(2,1)S(1)}, u32[]{:S(2)}, u32[]{:S(2)}) collective-permute-start(bf16[64,1536]{1,0:T(8,128)(2,1)S(1)} %pad_maximum_fusion.2.refs_3_), channel_id=1, source_target_pairs={{0,24},{2,26},{4,28},{6,30},{8,16},{10,18},{12,20},{14,22},{16,8},... | collective-permute-start | bytes 589832 | tf_op jit(solution)/shard_map/in_z3/ppermute | solution.py:33
  6.9 1.6 %collective-permute-start.4 = (bf16[64,2560]{1,0:T(8,128)(2,1)S(1)}, bf16[64,2560]{1,0:T(8,128)(2,1)S(1)}, u32[]{:S(2)}, u32[]{:S(2)}) collective-permute-start(bf16[64,2560]{1,0:T(8,128)(2,1)S(1)} %pad_maximum_fusion), channel_id=1, source_target_pairs={{0,4},{2,6},{4,0},{6,2},{8,12},{10,14},{12,8},{14,10},{16,20},{18,... | collective-permute-start | bytes 983048 | tf_op jit(solution)/shard_map/in_x/ppermute | solution.py:33
  8.5 1.6 %collective-permute-start = (bf16[400,1024]{1,0:T(8,128)(2,1)S(1)}, bf16[400,1024]{1,0:T(8,128)(2,1)S(1)}, u32[]{:S(2)}, u32[]{:S(2)}) collective-permute-start(bf16[400,1024]{1,0:T(8,128)(2,1)S(1)} %fusion.1), channel_id=1, source_target_pairs={{0,1},{1,0},{2,3},{3,2},{4,5},{5,4},{6,7},{7,6},{8,9},{9,8},{10,11... | collective-permute-start | bytes 2457608 | tf_op jit(solution)/shard_map/tokens/ppermute | solution.py:33
  10.1 2.5 %collective-permute-done.1.refs_15_ = bf16[64,1536]{1,0:T(8,128)(2,1)S(1)} collective-permute-done((bf16[64,1536]{1,0:T(8,128)(2,1)S(1)}, bf16[64,1536]{1,0:T(8,128)(2,1)S(1)}, u32[]{:S(2)}, u32[]{:S(2)}) %collective-permute-start.1) | collective-permute-done | bytes 196640 | tf_op jit(solution)/shard_map/in_z3/ppermute | solution.py:33
  12.6 3.1 %collective-permute-start.2 = (bf16[64,1536]{1,0:T(8,128)(2,1)S(1)}, bf16[64,1536]{1,0:T(8,128)(2,1)S(1)}, u32[]{:S(2)}, u32[]{:S(2)}) collective-permute-start(bf16[64,1536]{1,0:T(8,128)(2,1)S(1)} %collective-permute-done.1.refs_15_), channel_id=1, source_target_pairs={{0,8},{2,10},{4,12},{6,14},{8,0},{10,2},{12,4},{14,6},{16,24},{18,... | collective-permute-start | bytes 589832 | tf_op jit(solution)/shard_map/in_z2/ppermute | solution.py:33
  16.1 1.5 %collective-permute-start.6 = (bf16[64,1536]{1,0:T(8,128)(2,1)S(1)}, bf16[64,1536]{1,0:T(8,128)(2,1)S(1)}, u32[]{:S(2)}, u32[]{:S(2)}) collective-permute-start(bf16[64,1536]{1,0:T(8,128)(2,1)S(1)} %collective-permute-done.1.refs_15_), channel_id=1, source_target_pairs={{0,4},{2,6},{4,0},{6,2},{8,12},{10,14},{12,8},{14,10},{16,20},{18,... | collective-permute-start | bytes 589832 | tf_op jit(solution)/shard_map/in_z3_x/ppermute | solution.py:33
  17.6 0.8 %norm.2.refs_1_ = bf16[384,1024]{1,0:T(8,128)(2,1)S(1)} custom-call(bf16[384,1024]{1,0:T(8,128)(2,1)S(1)} %bitcast.12, f32[1,1024]{1,0:T(1,128)S(1)} %bitcast.15, f32[1,1024]{1,0:T(1,128)S(1)} %bitcast.17), custom_call_target="tpu_custom_call" | custom-call | flops 99999997952 | tf_op jit(solution)/shard_map/norm/pallas_call | solution.py:270
  18.4 1.0 %collective-permute-start.5 = (bf16[64,1536]{1,0:T(8,128)(2,1)S(1)}, bf16[64,1536]{1,0:T(8,128)(2,1)S(1)}, u32[]{:S(2)}, u32[]{:S(2)}) collective-permute-start(bf16[64,1536]{1,0:T(8,128)(2,1)S(1)} %collective-permute-done.3.refs_7_), channel_id=1, source_target_pairs={{0,4},{2,6},{4,0},{6,2},{8,12},{10,14},{12,8},{14,10},{16,20},{18,... | collective-permute-start | bytes 589832 | tf_op jit(solution)/shard_map/in_z1_x/ppermute | solution.py:33
  20.2 3.7 %collective-permute-done.6.refs_17_ = bf16[64,1536]{1,0:T(8,128)(2,1)S(1)} collective-permute-done((bf16[64,1536]{1,0:T(8,128)(2,1)S(1)}, bf16[64,1536]{1,0:T(8,128)(2,1)S(1)}, u32[]{:S(2)}, u32[]{:S(2)}) %collective-permute-start.6) | collective-permute-done | bytes 196640 | tf_op jit(solution)/shard_map/in_z3_x/ppermute | solution.py:33
  23.9 1.5 %collective-permute-start.12 = (bf16[64,1536]{1,0:T(8,128)(2,1)S(1)}, bf16[64,1536]{1,0:T(8,128)(2,1)S(1)}, u32[]{:S(2)}, u32[]{:S(2)}) collective-permute-start(bf16[64,1536]{1,0:T(8,128)(2,1)S(1)} %collective-permute-done.2.refs_11_), channel_id=1, source_target_pairs={{0,4},{2,6},{4,0},{6,2},{8,12},{10,14},{12,8},{14,10},{16,20},{18,... | collective-permute-start | bytes 589832 | tf_op jit(solution)/shard_map/in_z2_x/ppermute | solution.py:33
  25.4 1.7 %collective-permute-done.5.refs_9_ = bf16[64,1536]{1,0:T(8,128)(2,1)S(1)} collective-permute-done((bf16[64,1536]{1,0:T(8,128)(2,1)S(1)}, bf16[64,1536]{1,0:T(8,128)(2,1)S(1)}, u32[]{:S(2)}, u32[]{:S(2)}) %collective-permute-start.5) | collective-permute-done | bytes 196640 | tf_op jit(solution)/shard_map/in_z1_x/ppermute | solution.py:33
  27.1 1.8 %collective-permute-done.sheet_ref = bf16[400,1024]{1,0:T(8,128)(2,1)S(1)} collective-permute-done((bf16[400,1024]{1,0:T(8,128)(2,1)S(1)}, bf16[400,1024]{1,0:T(8,128)(2,1)S(1)}, u32[]{:S(2)}, u32[]{:S(2)}) %collective-permute-start) | collective-permute-done | bytes 819232 | tf_op jit(solution)/shard_map/tokens/ppermute | solution.py:33
  28.9 0.9 %collective-permute-start.20 = (bf16[128,1024]{1,0:T(8,128)(2,1)S(1)}, bf16[128,1024]{1,0:T(8,128)(2,1)S(1)}, u32[]{:S(2)}, u32[]{:S(2)}) collective-permute-start(bf16[128,1024]{1,0:T(8,128)(2,1)S(1)} %pad_maximum_fusion.1.refs_2_), channel_id=1, source_target_pairs={{0,24},{2,26},{4,28},{6,30},{8,16},{10,18},{12,20},{14,22},{16,8},... | collective-permute-start | bytes 786440 | tf_op jit(solution)/shard_map/out_z3/ppermute | solution.py:33
  29.8 0.8 %norm.3.refs_2_ = bf16[384,1024]{1,0:T(8,128)(2,1)S(1)} custom-call(bf16[400,1024]{1,0:T(8,128)(2,1)S(1)} %collective-permute-done.sheet_ref, f32[1,1024]{1,0:T(1,128)S(1)} %bitcast.16, f32[1,1024]{1,0:T(1,128)S(1)} %bitcast.18), custom_call_target="tpu_custom_call" | custom-call | tf_op jit(solution)/shard_map/norm/pallas_call | solution.py:270
  31.3 0.8 %collective-permute-done.15.refs_18_ = bf16[64,1536]{1,0:T(8,128)(2,1)S(1)} collective-permute-done((bf16[64,1536]{1,0:T(8,128)(2,1)S(1)}, bf16[64,1536]{1,0:T(8,128)(2,1)S(1)}, u32[]{:S(2)}, u32[]{:S(2)}) %collective-permute-start.15) | collective-permute-done | bytes 196640 | tf_op jit(solution)/shard_map/in_core_14/ppermute | solution.py:33
  32.2 1.1 %collective-permute-start.18 = (bf16[128,1024]{1,0:T(8,128)(2,1)S(1)}, bf16[128,1024]{1,0:T(8,128)(2,1)S(1)}, u32[]{:S(2)}, u32[]{:S(2)}) collective-permute-start(bf16[128,1024]{1,0:T(8,128)(2,1)S(1)} %pad_maximum_fusion.1.refs_2_), channel_id=1, source_target_pairs={{0,8},{2,10},{4,12},{6,14},{8,0},{10,2},{12,4},{14,6},{16,24},{18,... | collective-permute-start | bytes 786440 | tf_op jit(solution)/shard_map/out_z1/ppermute | solution.py:33
  33.3 6.0 %project.1 = (bf16[384,512]{1,0:T(8,128)(2,1)S(1)}, bf16[384,512]{1,0:T(8,128)(2,1)S(1)}, bf16[768,512]{1,0:T(8,128)(2,1)S(1)}, bf16[4,144,768]{2,1,0:T(8,128)(2,1)S(1)}) custom-call(s32[3,6]{1,0:T(4,128)S(1)} %slice_convert_fusion.refs_0_, bf16[384,1024]{1,0:T(8,128)(2,1)S(1)} %norm.2.refs_1_, bf16[384,1024]{1,0:T(8,128)(2,1)S(1)} %norm.3.refs_2_, ...), custom_call_target="tpu_custom_call" | custom-call | tf_op jit(solution)/shard_map/project/pallas_call | solution.py:319
  39.3 1.6 %collective-permute-start.16 = (bf16[384,512]{1,0:T(8,128)(2,1)S(1)}, bf16[384,512]{1,0:T(8,128)(2,1)S(1)}, u32[]{:S(2)}, u32[]{:S(2)}) collective-permute-start(bf16[384,512]{1,0:T(8,128)(2,1)S(1)} %get-tuple-element.21), channel_id=1, source_target_pairs={{0,1},{1,0},{2,3},{3,2},{4,5},{5,4},{6,7},{7,6},{8,9},{9,8},{10,11... | collective-permute-start | bytes 1179656 | tf_op jit(solution)/shard_map/context/ppermute | solution.py:33
  40.9 3.3 %collective-permute-start.22 = (bf16[128,1024]{1,0:T(8,128)(2,1)S(1)}, bf16[128,1024]{1,0:T(8,128)(2,1)S(1)}, u32[]{:S(2)}, u32[]{:S(2)}) collective-permute-start(bf16[128,1024]{1,0:T(8,128)(2,1)S(1)} %collective-permute-done.20.refs_6_), channel_id=1, source_target_pairs={{0,8},{2,10},{4,12},{6,14},{8,0},{10,2},{12,4},{14,6},{16,24},{18,... | collective-permute-start | bytes 786440 | tf_op jit(solution)/shard_map/out_z2/ppermute | solution.py:33
  44.2 3.1 %own_strip.1.refs_0_ = bf16[384,512]{1,0:T(8,128)(2,1)S(1)} custom-call(s32[3,6]{1,0:T(4,128)S(1)} %get-tuple-element.34.mask_ref, bf16[384,512]{1,0:T(8,128)(2,1)S(1)} %get-tuple-element.18.query_ref, bf16[768,512]{1,0:T(8,128)(2,1)S(1)} %get-tuple-element.19.key_ref, bf16[4,144,768]{2,1,0:T(8,128)(2,1)S(1)} %get-tuple-element.20.value_ref), custom_call_target="tpu_custom_call" | custom-call | flops 99999997952 | tf_op jit(solution)/shard_map/own_strip/pallas_call | solution.py:343
  47.9 2.3 %collective-permute-done.22.refs_8_ = bf16[128,1024]{1,0:T(8,128)(2,1)S(1)} collective-permute-done((bf16[128,1024]{1,0:T(8,128)(2,1)S(1)}, bf16[128,1024]{1,0:T(8,128)(2,1)S(1)}, u32[]{:S(2)}, u32[]{:S(2)}) %collective-permute-start.22) | collective-permute-done | bytes 262176 | tf_op jit(solution)/shard_map/out_z2/ppermute | solution.py:33
  50.3 1.5 %collective-permute-done.23.refs_9_ = bf16[128,1024]{1,0:T(8,128)(2,1)S(1)} collective-permute-done((bf16[128,1024]{1,0:T(8,128)(2,1)S(1)}, bf16[128,1024]{1,0:T(8,128)(2,1)S(1)}, u32[]{:S(2)}, u32[]{:S(2)}) %collective-permute-start.23) | collective-permute-done | bytes 262176 | tf_op jit(solution)/shard_map/out_core_8/ppermute | solution.py:33
  51.8 2.1 %output.1 = (bf16[384,1024]{1,0:T(8,128)(2,1)}, bf16[384,1024]{1,0:T(8,128)(2,1)}) custom-call(bf16[384,512]{1,0:T(8,128)(2,1)S(1)} %own_strip.1.refs_0_, bf16[384,512]{1,0:T(8,128)(2,1)S(1)} %collective-permute-done.16.refs_1_, bf16[128,1024]{1,0:T(8,128)(2,1)S(1)} %pad_maximum_fusion.1.refs_2_, bf16[128,1024]{1,0:T(8,128)(2,1)S(1)} %collective-permute-done.17.refs_3_, ...), custom_call_target="tpu_custom_call" | custom-call | flops 805306368 | bytes 2097152 | tf_op jit(solution)/shard_map/output/pallas_call | solution.py:360
  (51 shorter events, 2.8 us)
Async XLA Ops:
  1.7 10.9 %collective-permute-start.1 = (bf16[64,1536]{1,0:T(8,128)(2,1)S(1)}, bf16[64,1536]{1,0:T(8,128)(2,1)S(1)}, u32[]{:S(2)}, u32[]{:S(2)}) collective-permute-start(bf16[64,1536]{1,0:T(8,128)(2,1)S(1)} %pad_maximum_fusion.2.refs_3_), channel_id=1, source_target_pairs={{0,24},{2,26},{4,28},{6,30},{8,16},{10,18},{12,20},{14,22},{16,8},... | collective-permute-start | bytes 589832 | tf_op jit(solution)/shard_map/in_z3/ppermute | solution.py:33
  6.8 9.3 %collective-permute-start.3 = (bf16[64,1536]{1,0:T(8,128)(2,1)S(1)}, bf16[64,1536]{1,0:T(8,128)(2,1)S(1)}, u32[]{:S(2)}, u32[]{:S(2)}) collective-permute-start(bf16[64,1536]{1,0:T(8,128)(2,1)S(1)} %pad_maximum_fusion.2.refs_3_), channel_id=1, source_target_pairs={{0,8},{2,10},{4,12},{6,14},{8,0},{10,2},{12,4},{14,6},{16,24},{18,... | collective-permute-start | bytes 589832 | tf_op jit(solution)/shard_map/in_z1/ppermute | solution.py:33
  6.8 11.6 %collective-permute-start.7 = (bf16[64,1536]{1,0:T(8,128)(2,1)S(1)}, bf16[64,1536]{1,0:T(8,128)(2,1)S(1)}, u32[]{:S(2)}, u32[]{:S(2)}) collective-permute-start(bf16[64,1536]{1,0:T(8,128)(2,1)S(1)} %pad_maximum_fusion.2.refs_3_), channel_id=1, source_target_pairs={{0,2},{2,0},{4,6},{6,4},{8,10},{10,8},{12,14},{14,12},{16,18},{18,... | collective-permute-start | bytes 589832 | tf_op jit(solution)/shard_map/in_core_0/ppermute | solution.py:33
  6.9 10.7 %collective-permute-start.4 = (bf16[64,2560]{1,0:T(8,128)(2,1)S(1)}, bf16[64,2560]{1,0:T(8,128)(2,1)S(1)}, u32[]{:S(2)}, u32[]{:S(2)}) collective-permute-start(bf16[64,2560]{1,0:T(8,128)(2,1)S(1)} %pad_maximum_fusion), channel_id=1, source_target_pairs={{0,4},{2,6},{4,0},{6,2},{8,12},{10,14},{12,8},{14,10},{16,20},{18,... | collective-permute-start | bytes 983048 | tf_op jit(solution)/shard_map/in_x/ppermute | solution.py:33
  8.5 20.4 %collective-permute-start = (bf16[400,1024]{1,0:T(8,128)(2,1)S(1)}, bf16[400,1024]{1,0:T(8,128)(2,1)S(1)}, u32[]{:S(2)}, u32[]{:S(2)}) collective-permute-start(bf16[400,1024]{1,0:T(8,128)(2,1)S(1)} %fusion.1), channel_id=1, source_target_pairs={{0,1},{1,0},{2,3},{3,2},{4,5},{5,4},{6,7},{7,6},{8,9},{9,8},{10,11... | collective-permute-start | bytes 2457608 | tf_op jit(solution)/shard_map/tokens/ppermute | solution.py:33
  12.6 7.7 %collective-permute-start.2 = (bf16[64,1536]{1,0:T(8,128)(2,1)S(1)}, bf16[64,1536]{1,0:T(8,128)(2,1)S(1)}, u32[]{:S(2)}, u32[]{:S(2)}) collective-permute-start(bf16[64,1536]{1,0:T(8,128)(2,1)S(1)} %collective-permute-done.1.refs_15_), channel_id=1, source_target_pairs={{0,8},{2,10},{4,12},{6,14},{8,0},{10,2},{12,4},{14,6},{16,24},{18,... | collective-permute-start | bytes 589832 | tf_op jit(solution)/shard_map/in_z2/ppermute | solution.py:33
  16.1 7.8 %collective-permute-start.6 = (bf16[64,1536]{1,0:T(8,128)(2,1)S(1)}, bf16[64,1536]{1,0:T(8,128)(2,1)S(1)}, u32[]{:S(2)}, u32[]{:S(2)}) collective-permute-start(bf16[64,1536]{1,0:T(8,128)(2,1)S(1)} %collective-permute-done.1.refs_15_), channel_id=1, source_target_pairs={{0,4},{2,6},{4,0},{6,2},{8,12},{10,14},{12,8},{14,10},{16,20},{18,... | collective-permute-start | bytes 589832 | tf_op jit(solution)/shard_map/in_z3_x/ppermute | solution.py:33
  17.6 6.3 %collective-permute-start.9 = (bf16[64,1536]{1,0:T(8,128)(2,1)S(1)}, bf16[64,1536]{1,0:T(8,128)(2,1)S(1)}, u32[]{:S(2)}, u32[]{:S(2)}) collective-permute-start(bf16[64,1536]{1,0:T(8,128)(2,1)S(1)} %collective-permute-done.3.refs_7_), channel_id=1, source_target_pairs={{0,2},{2,0},{4,6},{6,4},{8,10},{10,8},{12,14},{14,12},{16,18},{18,... | collective-permute-start | bytes 589832 | tf_op jit(solution)/shard_map/in_core_4/ppermute | solution.py:33
  18.4 8.6 %collective-permute-start.5 = (bf16[64,1536]{1,0:T(8,128)(2,1)S(1)}, bf16[64,1536]{1,0:T(8,128)(2,1)S(1)}, u32[]{:S(2)}, u32[]{:S(2)}) collective-permute-start(bf16[64,1536]{1,0:T(8,128)(2,1)S(1)} %collective-permute-done.3.refs_7_), channel_id=1, source_target_pairs={{0,4},{2,6},{4,0},{6,2},{8,12},{10,14},{12,8},{14,10},{16,20},{18,... | collective-permute-start | bytes 589832 | tf_op jit(solution)/shard_map/in_z1_x/ppermute | solution.py:33
  20.2 10.4 %collective-permute-start.14 = (bf16[64,1536]{1,0:T(8,128)(2,1)S(1)}, bf16[64,1536]{1,0:T(8,128)(2,1)S(1)}, u32[]{:S(2)}, u32[]{:S(2)}) collective-permute-start(bf16[64,1536]{1,0:T(8,128)(2,1)S(1)} %collective-permute-done.1.refs_15_), channel_id=1, source_target_pairs={{0,2},{2,0},{4,6},{6,4},{8,10},{10,8},{12,14},{14,12},{16,18},{18,... | collective-permute-start | bytes 589832 | tf_op jit(solution)/shard_map/in_core_12/ppermute | solution.py:33
  23.9 6.8 %collective-permute-start.11 = (bf16[64,1536]{1,0:T(8,128)(2,1)S(1)}, bf16[64,1536]{1,0:T(8,128)(2,1)S(1)}, u32[]{:S(2)}, u32[]{:S(2)}) collective-permute-start(bf16[64,1536]{1,0:T(8,128)(2,1)S(1)} %collective-permute-done.2.refs_11_), channel_id=1, source_target_pairs={{0,2},{2,0},{4,6},{6,4},{8,10},{10,8},{12,14},{14,12},{16,18},{18,... | collective-permute-start | bytes 589832 | tf_op jit(solution)/shard_map/in_core_8/ppermute | solution.py:33
  23.9 7.4 %collective-permute-start.12 = (bf16[64,1536]{1,0:T(8,128)(2,1)S(1)}, bf16[64,1536]{1,0:T(8,128)(2,1)S(1)}, u32[]{:S(2)}, u32[]{:S(2)}) collective-permute-start(bf16[64,1536]{1,0:T(8,128)(2,1)S(1)} %collective-permute-done.2.refs_11_), channel_id=1, source_target_pairs={{0,4},{2,6},{4,0},{6,2},{8,12},{10,14},{12,8},{14,10},{16,20},{18,... | collective-permute-start | bytes 589832 | tf_op jit(solution)/shard_map/in_z2_x/ppermute | solution.py:33
  27.1 6.2 %collective-permute-start.8 = (bf16[64,2560]{1,0:T(8,128)(2,1)S(1)}, bf16[64,2560]{1,0:T(8,128)(2,1)S(1)}, u32[]{:S(2)}, u32[]{:S(2)}) collective-permute-start(bf16[64,2560]{1,0:T(8,128)(2,1)S(1)} %collective-permute-done.4.refs_5_), channel_id=1, source_target_pairs={{0,2},{2,0},{4,6},{6,4},{8,10},{10,8},{12,14},{14,12},{16,18},{18,... | collective-permute-start | bytes 983048 | tf_op jit(solution)/shard_map/in_core_2/ppermute | solution.py:33
  28.9 12.0 %collective-permute-start.20 = (bf16[128,1024]{1,0:T(8,128)(2,1)S(1)}, bf16[128,1024]{1,0:T(8,128)(2,1)S(1)}, u32[]{:S(2)}, u32[]{:S(2)}) collective-permute-start(bf16[128,1024]{1,0:T(8,128)(2,1)S(1)} %pad_maximum_fusion.1.refs_2_), channel_id=1, source_target_pairs={{0,24},{2,26},{4,28},{6,30},{8,16},{10,18},{12,20},{14,22},{16,8},... | collective-permute-start | bytes 786440 | tf_op jit(solution)/shard_map/out_z3/ppermute | solution.py:33
  30.6 1.5 %collective-permute-start.15 = (bf16[64,1536]{1,0:T(8,128)(2,1)S(1)}, bf16[64,1536]{1,0:T(8,128)(2,1)S(1)}, u32[]{:S(2)}, u32[]{:S(2)}) collective-permute-start(bf16[64,1536]{1,0:T(8,128)(2,1)S(1)} %collective-permute-done.6.refs_17_), channel_id=1, source_target_pairs={{0,2},{2,0},{4,6},{6,4},{8,10},{10,8},{12,14},{14,12},{16,18},{18,... | collective-permute-start | bytes 589832 | tf_op jit(solution)/shard_map/in_core_14/ppermute | solution.py:33
  30.7 2.6 %collective-permute-start.10 = (bf16[64,1536]{1,0:T(8,128)(2,1)S(1)}, bf16[64,1536]{1,0:T(8,128)(2,1)S(1)}, u32[]{:S(2)}, u32[]{:S(2)}) collective-permute-start(bf16[64,1536]{1,0:T(8,128)(2,1)S(1)} %collective-permute-done.5.refs_9_), channel_id=1, source_target_pairs={{0,2},{2,0},{4,6},{6,4},{8,10},{10,8},{12,14},{14,12},{16,18},{18,... | collective-permute-start | bytes 589832 | tf_op jit(solution)/shard_map/in_core_6/ppermute | solution.py:33
  31.3 2.0 %collective-permute-start.13 = (bf16[64,1536]{1,0:T(8,128)(2,1)S(1)}, bf16[64,1536]{1,0:T(8,128)(2,1)S(1)}, u32[]{:S(2)}, u32[]{:S(2)}) collective-permute-start(bf16[64,1536]{1,0:T(8,128)(2,1)S(1)} %collective-permute-done.12.refs_13_), channel_id=1, source_target_pairs={{0,2},{2,0},{4,6},{6,4},{8,10},{10,8},{12,14},{14,12},{16,18},{18,... | collective-permute-start | bytes 589832 | tf_op jit(solution)/shard_map/in_core_10/ppermute | solution.py:33
  32.2 15.2 %collective-permute-start.18 = (bf16[128,1024]{1,0:T(8,128)(2,1)S(1)}, bf16[128,1024]{1,0:T(8,128)(2,1)S(1)}, u32[]{:S(2)}, u32[]{:S(2)}) collective-permute-start(bf16[128,1024]{1,0:T(8,128)(2,1)S(1)} %pad_maximum_fusion.1.refs_2_), channel_id=1, source_target_pairs={{0,8},{2,10},{4,12},{6,14},{8,0},{10,2},{12,4},{14,6},{16,24},{18,... | collective-permute-start | bytes 786440 | tf_op jit(solution)/shard_map/out_z1/ppermute | solution.py:33
  39.3 11.0 %collective-permute-start.16 = (bf16[384,512]{1,0:T(8,128)(2,1)S(1)}, bf16[384,512]{1,0:T(8,128)(2,1)S(1)}, u32[]{:S(2)}, u32[]{:S(2)}) collective-permute-start(bf16[384,512]{1,0:T(8,128)(2,1)S(1)} %get-tuple-element.21), channel_id=1, source_target_pairs={{0,1},{1,0},{2,3},{3,2},{4,5},{5,4},{6,7},{7,6},{8,9},{9,8},{10,11... | collective-permute-start | bytes 1179656 | tf_op jit(solution)/shard_map/context/ppermute | solution.py:33
  40.9 9.4 %collective-permute-start.22 = (bf16[128,1024]{1,0:T(8,128)(2,1)S(1)}, bf16[128,1024]{1,0:T(8,128)(2,1)S(1)}, u32[]{:S(2)}, u32[]{:S(2)}) collective-permute-start(bf16[128,1024]{1,0:T(8,128)(2,1)S(1)} %collective-permute-done.20.refs_6_), channel_id=1, source_target_pairs={{0,8},{2,10},{4,12},{6,14},{8,0},{10,2},{12,4},{14,6},{16,24},{18,... | collective-permute-start | bytes 786440 | tf_op jit(solution)/shard_map/out_z2/ppermute | solution.py:33
  47.3 3.0 %collective-permute-start.17 = (bf16[128,1024]{1,0:T(8,128)(2,1)S(1)}, bf16[128,1024]{1,0:T(8,128)(2,1)S(1)}, u32[]{:S(2)}, u32[]{:S(2)}) collective-permute-start(bf16[128,1024]{1,0:T(8,128)(2,1)S(1)} %pad_maximum_fusion.1.refs_2_), channel_id=1, source_target_pairs={{0,2},{2,0},{4,6},{6,4},{8,10},{10,8},{12,14},{14,12},{16,18},{18,... | collective-permute-start | bytes 786440 | tf_op jit(solution)/shard_map/out_core_0/ppermute | solution.py:33
  47.4 2.9 %collective-permute-start.19 = (bf16[128,1024]{1,0:T(8,128)(2,1)S(1)}, bf16[128,1024]{1,0:T(8,128)(2,1)S(1)}, u32[]{:S(2)}, u32[]{:S(2)}) collective-permute-start(bf16[128,1024]{1,0:T(8,128)(2,1)S(1)} %collective-permute-done.18.refs_4_), channel_id=1, source_target_pairs={{0,2},{2,0},{4,6},{6,4},{8,10},{10,8},{12,14},{14,12},{16,18},{18,... | collective-permute-start | bytes 786440 | tf_op jit(solution)/shard_map/out_core_4/ppermute | solution.py:33
  47.9 2.4 %collective-permute-start.21 = (bf16[128,1024]{1,0:T(8,128)(2,1)S(1)}, bf16[128,1024]{1,0:T(8,128)(2,1)S(1)}, u32[]{:S(2)}, u32[]{:S(2)}) collective-permute-start(bf16[128,1024]{1,0:T(8,128)(2,1)S(1)} %collective-permute-done.20.refs_6_), channel_id=1, source_target_pairs={{0,2},{2,0},{4,6},{6,4},{8,10},{10,8},{12,14},{14,12},{16,18},{18,... | collective-permute-start | bytes 786440 | tf_op jit(solution)/shard_map/out_core_12/ppermute | solution.py:33
  50.3 1.5 %collective-permute-start.23 = (bf16[128,1024]{1,0:T(8,128)(2,1)S(1)}, bf16[128,1024]{1,0:T(8,128)(2,1)S(1)}, u32[]{:S(2)}, u32[]{:S(2)}) collective-permute-start(bf16[128,1024]{1,0:T(8,128)(2,1)S(1)} %collective-permute-done.22.refs_8_), channel_id=1, source_target_pairs={{0,2},{2,0},{4,6},{6,4},{8,10},{10,8},{12,14},{14,12},{16,18},{18,... | collective-permute-start | bytes 786440 | tf_op jit(solution)/shard_map/out_core_8/ppermute | solution.py:33
  (7 other events, 57.1 us)

commit v5 on v4

--- a/solution.py
+++ b/solution.py
@@ -302,7 +302,7 @@
     out_ready = after(out_own, pieces[third])
     out_second = swap(out_ready, "dp", second, "out_z3")
     out_first = swap(out_ready, "dp", first, "out_z1")
-    before = [pieces[slot] for slot in (third, first + across[0], second + across[0])]
+    before = [pieces[third]]
     normed.extend(norm(after(sheets[k], normed[0], *before), 0) for k in range(1, strips))
 
     for slot in sorted(pieces):

time: 54 us -> 53.4 us (0.989)
  Pallas kernels: 12.8 us -> 11.1 us
  waiting for transfers between devices: 15.7 us -> 17.1 us
    ppermute x24, waiting for transfers between devices: 15.7 us -> 17.1 us  [swap(): return lax.ppermute(block, axis, [(i, i ^ distance) for i in range(size)])]
    pallas_call x1, Pallas kernels: 3.07 us -> 2.24 us  [on_device(): call(functools.partial(own_kernel, strips), strip_out, [SMEM] + [VMEM] *...]
    pallas_call x1, Pallas kernels: 6.03 us -> 5.21 us  [on_device(): call(functools.partial(project_kernel, strips, len(normed), [[slot] for s...]
  transfers between devices with their start and end apart: 24 -> 24, of which waited for: 9 -> 10; matrix products, arithmetic and copies ran while one was open for 0% -> 0% of each run, Pallas kernels for 20% -> 17%
where the time goes in v5:
time: 53.4 us; the launch traced here: 53.3 us
  starting transfers between devices  23.1 us (43%)
  waiting for transfers between devices  17.1 us (32%)
  Pallas kernels  11.1 us (21%)
  local copies, waits for them, and re-layouts  1.05 us (2%)
  between operations  0.85 us (2%)
    ppermute x24, starting transfers between devices, swap(): return lax.ppermute(block, axis, [(i, i ^ distance) for i in range(size)])  23.1 us
    ppermute x24, waiting for transfers between devices, swap(): return lax.ppermute(block, axis, [(i, i ^ distance) for i in range(size)])  17.1 us
    pallas_call x1, Pallas kernels, on_device(): call(functools.partial(project_kernel, strips, len(normed), [[slot] for s...  5.21 us
    pallas_call x1, Pallas kernels, on_device(): call(functools.partial(own_kernel, strips), strip_out, [SMEM] + [VMEM] *...  2.24 us
    pallas_call x1, Pallas kernels, on_device(): call(functools.partial(output_kernel, strips, out_slots), [jax.ShapeDtype...  2.06 us
    pallas_call x2, Pallas kernels, norm(): call(norm_kernel, jax.ShapeDtypeStruct((length, features), jnp.bfloat16),...  1.6 us
  transfers between devices with their start and end apart: 24, of which 10 were waited for; matrix products, arithmetic and copies ran while one was open for 0% of the time, Pallas kernels for 17%

profile of v5, /device:TPU:0, one launch (start us, length us, event | category | flops | bytes accessed | tf_op | source)
XLA Modules:
  0.0 53.3 jit_solution(15144365617533063496)
XLA Ops:
  0.7 1.0 %constant_dynamic-slice_fusion.2 = (bf16[64,512]{1,0:T(8,128)(2,1)S(1)}, bf16[64,512]{1,0:T(8,128)(2,1)S(1)}, bf16[64,512]{1,0:T(8,128)(2,1)S(1)}) fusion(bf16[64,3072]{1,0:T(8,128)(2,1)} %param.12, s32[]{:T(128)S(6)} %select_n.9, s32[]{:T(128)S(6)} %select_n.11, s32[]{:T(128)S(6)} %select_n.10), kind=kLoop, calls=%fused_computation.10 | loop fusion | bytes 393228 | tf_op jit(solution)/shard_map/dynamic_slice | solution.py:257
  1.7 5.1 %collective-permute-start.1 = (bf16[64,1536]{1,0:T(8,128)(2,1)S(1)}, bf16[64,1536]{1,0:T(8,128)(2,1)S(1)}, u32[]{:S(2)}, u32[]{:S(2)}) collective-permute-start(bf16[64,1536]{1,0:T(8,128)(2,1)S(1)} %pad_maximum_fusion.2.refs_3_), channel_id=1, source_target_pairs={{0,24},{2,26},{4,28},{6,30},{8,16},{10,18},{12,20},{14,22},{16,8},... | collective-permute-start | bytes 589832 | tf_op jit(solution)/shard_map/in_z3/ppermute | solution.py:33
  6.9 1.6 %collective-permute-start.4 = (bf16[64,2560]{1,0:T(8,128)(2,1)S(1)}, bf16[64,2560]{1,0:T(8,128)(2,1)S(1)}, u32[]{:S(2)}, u32[]{:S(2)}) collective-permute-start(bf16[64,2560]{1,0:T(8,128)(2,1)S(1)} %pad_maximum_fusion), channel_id=1, source_target_pairs={{0,4},{2,6},{4,0},{6,2},{8,12},{10,14},{12,8},{14,10},{16,20},{18,... | collective-permute-start | bytes 983048 | tf_op jit(solution)/shard_map/in_x/ppermute | solution.py:33
  8.5 1.6 %collective-permute-start = (bf16[400,1024]{1,0:T(8,128)(2,1)S(1)}, bf16[400,1024]{1,0:T(8,128)(2,1)S(1)}, u32[]{:S(2)}, u32[]{:S(2)}) collective-permute-start(bf16[400,1024]{1,0:T(8,128)(2,1)S(1)} %fusion.1), channel_id=1, source_target_pairs={{0,1},{1,0},{2,3},{3,2},{4,5},{5,4},{6,7},{7,6},{8,9},{9,8},{10,11... | collective-permute-start | bytes 2457608 | tf_op jit(solution)/shard_map/tokens/ppermute | solution.py:33
  10.1 2.5 %collective-permute-done.1.refs_15_ = bf16[64,1536]{1,0:T(8,128)(2,1)S(1)} collective-permute-done((bf16[64,1536]{1,0:T(8,128)(2,1)S(1)}, bf16[64,1536]{1,0:T(8,128)(2,1)S(1)}, u32[]{:S(2)}, u32[]{:S(2)}) %collective-permute-start.1) | collective-permute-done | bytes 196640 | tf_op jit(solution)/shard_map/in_z3/ppermute | solution.py:33
  12.6 3.1 %collective-permute-start.2 = (bf16[64,1536]{1,0:T(8,128)(2,1)S(1)}, bf16[64,1536]{1,0:T(8,128)(2,1)S(1)}, u32[]{:S(2)}, u32[]{:S(2)}) collective-permute-start(bf16[64,1536]{1,0:T(8,128)(2,1)S(1)} %collective-permute-done.1.refs_15_), channel_id=1, source_target_pairs={{0,8},{2,10},{4,12},{6,14},{8,0},{10,2},{12,4},{14,6},{16,24},{18,... | collective-permute-start | bytes 589832 | tf_op jit(solution)/shard_map/in_z2/ppermute | solution.py:33
  16.1 1.5 %collective-permute-start.14 = (bf16[64,1536]{1,0:T(8,128)(2,1)S(1)}, bf16[64,1536]{1,0:T(8,128)(2,1)S(1)}, u32[]{:S(2)}, u32[]{:S(2)}) collective-permute-start(bf16[64,1536]{1,0:T(8,128)(2,1)S(1)} %collective-permute-done.1.refs_15_), channel_id=1, source_target_pairs={{0,4},{2,6},{4,0},{6,2},{8,12},{10,14},{12,8},{14,10},{16,20},{18,... | collective-permute-start | bytes 589832 | tf_op jit(solution)/shard_map/in_z3_x/ppermute | solution.py:33
  17.6 0.8 %norm.2.refs_1_ = bf16[384,1024]{1,0:T(8,128)(2,1)S(1)} custom-call(bf16[384,1024]{1,0:T(8,128)(2,1)S(1)} %bitcast.12, f32[1,1024]{1,0:T(1,128)S(1)} %bitcast.15, f32[1,1024]{1,0:T(1,128)S(1)} %bitcast.17), custom_call_target="tpu_custom_call" | custom-call | flops 99999997952 | tf_op jit(solution)/shard_map/norm/pallas_call | solution.py:270
  18.4 1.9 %collective-permute-done.2.refs_11_ = bf16[64,1536]{1,0:T(8,128)(2,1)S(1)} collective-permute-done((bf16[64,1536]{1,0:T(8,128)(2,1)S(1)}, bf16[64,1536]{1,0:T(8,128)(2,1)S(1)}, u32[]{:S(2)}, u32[]{:S(2)}) %collective-permute-start.2) | collective-permute-done | bytes 196640 | tf_op jit(solution)/shard_map/in_z2/ppermute | solution.py:33
  20.2 1.5 %collective-permute-start.8 = (bf16[64,1536]{1,0:T(8,128)(2,1)S(1)}, bf16[64,1536]{1,0:T(8,128)(2,1)S(1)}, u32[]{:S(2)}, u32[]{:S(2)}) collective-permute-start(bf16[64,1536]{1,0:T(8,128)(2,1)S(1)} %collective-permute-done.6.refs_7_), channel_id=1, source_target_pairs={{0,4},{2,6},{4,0},{6,2},{8,12},{10,14},{12,8},{14,10},{16,20},{18,... | collective-permute-start | bytes 589832 | tf_op jit(solution)/shard_map/in_z1_x/ppermute | solution.py:33
  21.7 0.6 %collective-permute-start.11 = (bf16[64,1536]{1,0:T(8,128)(2,1)S(1)}, bf16[64,1536]{1,0:T(8,128)(2,1)S(1)}, u32[]{:S(2)}, u32[]{:S(2)}) collective-permute-start(bf16[64,1536]{1,0:T(8,128)(2,1)S(1)} %collective-permute-done.2.refs_11_), channel_id=1, source_target_pairs={{0,4},{2,6},{4,0},{6,2},{8,12},{10,14},{12,8},{14,10},{16,20},{18,... | collective-permute-start | bytes 589832 | tf_op jit(solution)/shard_map/in_z2_x/ppermute | solution.py:33
  22.4 1.5 %collective-permute-done.14.refs_17_ = bf16[64,1536]{1,0:T(8,128)(2,1)S(1)} collective-permute-done((bf16[64,1536]{1,0:T(8,128)(2,1)S(1)}, bf16[64,1536]{1,0:T(8,128)(2,1)S(1)}, u32[]{:S(2)}, u32[]{:S(2)}) %collective-permute-start.14) | collective-permute-done | bytes 196640 | tf_op jit(solution)/shard_map/in_z3_x/ppermute | solution.py:33
  23.9 5.1 %collective-permute-done.sheet_ref = bf16[400,1024]{1,0:T(8,128)(2,1)S(1)} collective-permute-done((bf16[400,1024]{1,0:T(8,128)(2,1)S(1)}, bf16[400,1024]{1,0:T(8,128)(2,1)S(1)}, u32[]{:S(2)}, u32[]{:S(2)}) %collective-permute-start) | collective-permute-done | bytes 819232 | tf_op jit(solution)/shard_map/tokens/ppermute | solution.py:33
  28.9 0.6 %collective-permute-start.20 = (bf16[128,1024]{1,0:T(8,128)(2,1)S(1)}, bf16[128,1024]{1,0:T(8,128)(2,1)S(1)}, u32[]{:S(2)}, u32[]{:S(2)}) collective-permute-start(bf16[128,1024]{1,0:T(8,128)(2,1)S(1)} %pad_maximum_fusion.1.refs_2_), channel_id=1, source_target_pairs={{0,24},{2,26},{4,28},{6,30},{8,16},{10,18},{12,20},{14,22},{16,8},... | collective-permute-start | bytes 786440 | tf_op jit(solution)/shard_map/out_z3/ppermute | solution.py:33
  29.6 0.8 %norm.3.refs_2_ = bf16[384,1024]{1,0:T(8,128)(2,1)S(1)} custom-call(bf16[400,1024]{1,0:T(8,128)(2,1)S(1)} %collective-permute-done.sheet_ref, f32[1,1024]{1,0:T(1,128)S(1)} %bitcast.16, f32[1,1024]{1,0:T(1,128)S(1)} %bitcast.18), custom_call_target="tpu_custom_call" | custom-call | tf_op jit(solution)/shard_map/norm/pallas_call | solution.py:270
  30.5 0.5 collective-permute-start.9
  31.9 1.1 %collective-permute-start.18 = (bf16[128,1024]{1,0:T(8,128)(2,1)S(1)}, bf16[128,1024]{1,0:T(8,128)(2,1)S(1)}, u32[]{:S(2)}, u32[]{:S(2)}) collective-permute-start(bf16[128,1024]{1,0:T(8,128)(2,1)S(1)} %pad_maximum_fusion.1.refs_2_), channel_id=1, source_target_pairs={{0,8},{2,10},{4,12},{6,14},{8,0},{10,2},{12,4},{14,6},{16,24},{18,... | collective-permute-start | bytes 786440 | tf_op jit(solution)/shard_map/out_z1/ppermute | solution.py:33
  33.0 5.2 %project.1 = (bf16[384,512]{1,0:T(8,128)(2,1)S(1)}, bf16[384,512]{1,0:T(8,128)(2,1)S(1)}, bf16[768,512]{1,0:T(8,128)(2,1)S(1)}, bf16[4,144,768]{2,1,0:T(8,128)(2,1)S(1)}) custom-call(s32[3,6]{1,0:T(4,128)S(1)} %slice_convert_fusion.refs_0_, bf16[384,1024]{1,0:T(8,128)(2,1)S(1)} %norm.2.refs_1_, bf16[384,1024]{1,0:T(8,128)(2,1)S(1)} %norm.3.refs_2_, ...), custom_call_target="tpu_custom_call" | custom-call | tf_op jit(solution)/shard_map/project/pallas_call | solution.py:319
  38.2 1.6 %collective-permute-start.16 = (bf16[384,512]{1,0:T(8,128)(2,1)S(1)}, bf16[384,512]{1,0:T(8,128)(2,1)S(1)}, u32[]{:S(2)}, u32[]{:S(2)}) collective-permute-start(bf16[384,512]{1,0:T(8,128)(2,1)S(1)} %get-tuple-element.21), channel_id=1, source_target_pairs={{0,1},{1,0},{2,3},{3,2},{4,5},{5,4},{6,7},{7,6},{8,9},{9,8},{10,11... | collective-permute-start | bytes 1179656 | tf_op jit(solution)/shard_map/context/ppermute | solution.py:33
  40.0 3.6 %collective-permute-start.22 = (bf16[128,1024]{1,0:T(8,128)(2,1)S(1)}, bf16[128,1024]{1,0:T(8,128)(2,1)S(1)}, u32[]{:S(2)}, u32[]{:S(2)}) collective-permute-start(bf16[128,1024]{1,0:T(8,128)(2,1)S(1)} %collective-permute-done.20.refs_6_), channel_id=1, source_target_pairs={{0,8},{2,10},{4,12},{6,14},{8,0},{10,2},{12,4},{14,6},{16,24},{18,... | collective-permute-start | bytes 786440 | tf_op jit(solution)/shard_map/out_z2/ppermute | solution.py:33
  43.6 2.2 %own_strip.1.refs_0_ = bf16[384,512]{1,0:T(8,128)(2,1)S(1)} custom-call(s32[3,6]{1,0:T(4,128)S(1)} %get-tuple-element.34.mask_ref, bf16[384,512]{1,0:T(8,128)(2,1)S(1)} %get-tuple-element.18.query_ref, bf16[768,512]{1,0:T(8,128)(2,1)S(1)} %get-tuple-element.19.key_ref, bf16[4,144,768]{2,1,0:T(8,128)(2,1)S(1)} %get-tuple-element.20.value_ref), custom_call_target="tpu_custom_call" | custom-call | flops 99999997952 | tf_op jit(solution)/shard_map/own_strip/pallas_call | solution.py:343
  46.5 3.2 %collective-permute-done.22.refs_8_ = bf16[128,1024]{1,0:T(8,128)(2,1)S(1)} collective-permute-done((bf16[128,1024]{1,0:T(8,128)(2,1)S(1)}, bf16[128,1024]{1,0:T(8,128)(2,1)S(1)}, u32[]{:S(2)}, u32[]{:S(2)}) %collective-permute-start.22) | collective-permute-done | bytes 262176 | tf_op jit(solution)/shard_map/out_z2/ppermute | solution.py:33
  49.7 1.5 %collective-permute-done.23.refs_9_ = bf16[128,1024]{1,0:T(8,128)(2,1)S(1)} collective-permute-done((bf16[128,1024]{1,0:T(8,128)(2,1)S(1)}, bf16[128,1024]{1,0:T(8,128)(2,1)S(1)}, u32[]{:S(2)}, u32[]{:S(2)}) %collective-permute-start.23) | collective-permute-done | bytes 262176 | tf_op jit(solution)/shard_map/out_core_8/ppermute | solution.py:33
  51.2 2.1 %output.1 = (bf16[384,1024]{1,0:T(8,128)(2,1)}, bf16[384,1024]{1,0:T(8,128)(2,1)}) custom-call(bf16[384,512]{1,0:T(8,128)(2,1)S(1)} %own_strip.1.refs_0_, bf16[384,512]{1,0:T(8,128)(2,1)S(1)} %collective-permute-done.16.refs_1_, bf16[128,1024]{1,0:T(8,128)(2,1)S(1)} %pad_maximum_fusion.1.refs_2_, bf16[128,1024]{1,0:T(8,128)(2,1)S(1)} %collective-permute-done.17.refs_3_, ...), custom_call_target="tpu_custom_call" | custom-call | flops 805306368 | bytes 2097152 | tf_op jit(solution)/shard_map/output/pallas_call | solution.py:360
  (51 shorter events, 2.4 us)
Async XLA Ops:
  1.7 10.9 %collective-permute-start.1 = (bf16[64,1536]{1,0:T(8,128)(2,1)S(1)}, bf16[64,1536]{1,0:T(8,128)(2,1)S(1)}, u32[]{:S(2)}, u32[]{:S(2)}) collective-permute-start(bf16[64,1536]{1,0:T(8,128)(2,1)S(1)} %pad_maximum_fusion.2.refs_3_), channel_id=1, source_target_pairs={{0,24},{2,26},{4,28},{6,30},{8,16},{10,18},{12,20},{14,22},{16,8},... | collective-permute-start | bytes 589832 | tf_op jit(solution)/shard_map/in_z3/ppermute | solution.py:33
  6.8 8.8 %collective-permute-start.3 = (bf16[64,1536]{1,0:T(8,128)(2,1)S(1)}, bf16[64,1536]{1,0:T(8,128)(2,1)S(1)}, u32[]{:S(2)}, u32[]{:S(2)}) collective-permute-start(bf16[64,1536]{1,0:T(8,128)(2,1)S(1)} %pad_maximum_fusion.2.refs_3_), channel_id=1, source_target_pairs={{0,2},{2,0},{4,6},{6,4},{8,10},{10,8},{12,14},{14,12},{16,18},{18,... | collective-permute-start | bytes 589832 | tf_op jit(solution)/shard_map/in_core_0/ppermute | solution.py:33
  6.8 9.2 %collective-permute-start.6 = (bf16[64,1536]{1,0:T(8,128)(2,1)S(1)}, bf16[64,1536]{1,0:T(8,128)(2,1)S(1)}, u32[]{:S(2)}, u32[]{:S(2)}) collective-permute-start(bf16[64,1536]{1,0:T(8,128)(2,1)S(1)} %pad_maximum_fusion.2.refs_3_), channel_id=1, source_target_pairs={{0,8},{2,10},{4,12},{6,14},{8,0},{10,2},{12,4},{14,6},{16,24},{18,... | collective-permute-start | bytes 589832 | tf_op jit(solution)/shard_map/in_z1/ppermute | solution.py:33
  6.9 10.7 %collective-permute-start.4 = (bf16[64,2560]{1,0:T(8,128)(2,1)S(1)}, bf16[64,2560]{1,0:T(8,128)(2,1)S(1)}, u32[]{:S(2)}, u32[]{:S(2)}) collective-permute-start(bf16[64,2560]{1,0:T(8,128)(2,1)S(1)} %pad_maximum_fusion), channel_id=1, source_target_pairs={{0,4},{2,6},{4,0},{6,2},{8,12},{10,14},{12,8},{14,10},{16,20},{18,... | collective-permute-start | bytes 983048 | tf_op jit(solution)/shard_map/in_x/ppermute | solution.py:33
  8.5 20.4 %collective-permute-start = (bf16[400,1024]{1,0:T(8,128)(2,1)S(1)}, bf16[400,1024]{1,0:T(8,128)(2,1)S(1)}, u32[]{:S(2)}, u32[]{:S(2)}) collective-permute-start(bf16[400,1024]{1,0:T(8,128)(2,1)S(1)} %fusion.1), channel_id=1, source_target_pairs={{0,1},{1,0},{2,3},{3,2},{4,5},{5,4},{6,7},{7,6},{8,9},{9,8},{10,11... | collective-permute-start | bytes 2457608 | tf_op jit(solution)/shard_map/tokens/ppermute | solution.py:33
  12.6 7.7 %collective-permute-start.2 = (bf16[64,1536]{1,0:T(8,128)(2,1)S(1)}, bf16[64,1536]{1,0:T(8,128)(2,1)S(1)}, u32[]{:S(2)}, u32[]{:S(2)}) collective-permute-start(bf16[64,1536]{1,0:T(8,128)(2,1)S(1)} %collective-permute-done.1.refs_15_), channel_id=1, source_target_pairs={{0,8},{2,10},{4,12},{6,14},{8,0},{10,2},{12,4},{14,6},{16,24},{18,... | collective-permute-start | bytes 589832 | tf_op jit(solution)/shard_map/in_z2/ppermute | solution.py:33
  15.6 6.1 %collective-permute-start.13 = (bf16[64,1536]{1,0:T(8,128)(2,1)S(1)}, bf16[64,1536]{1,0:T(8,128)(2,1)S(1)}, u32[]{:S(2)}, u32[]{:S(2)}) collective-permute-start(bf16[64,1536]{1,0:T(8,128)(2,1)S(1)} %collective-permute-done.1.refs_15_), channel_id=1, source_target_pairs={{0,2},{2,0},{4,6},{6,4},{8,10},{10,8},{12,14},{14,12},{16,18},{18,... | collective-permute-start | bytes 589832 | tf_op jit(solution)/shard_map/in_core_12/ppermute | solution.py:33
  16.1 7.8 %collective-permute-start.14 = (bf16[64,1536]{1,0:T(8,128)(2,1)S(1)}, bf16[64,1536]{1,0:T(8,128)(2,1)S(1)}, u32[]{:S(2)}, u32[]{:S(2)}) collective-permute-start(bf16[64,1536]{1,0:T(8,128)(2,1)S(1)} %collective-permute-done.1.refs_15_), channel_id=1, source_target_pairs={{0,4},{2,6},{4,0},{6,2},{8,12},{10,14},{12,8},{14,10},{16,20},{18,... | collective-permute-start | bytes 589832 | tf_op jit(solution)/shard_map/in_z3_x/ppermute | solution.py:33
  17.6 4.2 %collective-permute-start.7 = (bf16[64,1536]{1,0:T(8,128)(2,1)S(1)}, bf16[64,1536]{1,0:T(8,128)(2,1)S(1)}, u32[]{:S(2)}, u32[]{:S(2)}) collective-permute-start(bf16[64,1536]{1,0:T(8,128)(2,1)S(1)} %collective-permute-done.6.refs_7_), channel_id=1, source_target_pairs={{0,2},{2,0},{4,6},{6,4},{8,10},{10,8},{12,14},{14,12},{16,18},{18,... | collective-permute-start | bytes 589832 | tf_op jit(solution)/shard_map/in_core_4/ppermute | solution.py:33
  20.2 10.1 %collective-permute-start.8 = (bf16[64,1536]{1,0:T(8,128)(2,1)S(1)}, bf16[64,1536]{1,0:T(8,128)(2,1)S(1)}, u32[]{:S(2)}, u32[]{:S(2)}) collective-permute-start(bf16[64,1536]{1,0:T(8,128)(2,1)S(1)} %collective-permute-done.6.refs_7_), channel_id=1, source_target_pairs={{0,4},{2,6},{4,0},{6,2},{8,12},{10,14},{12,8},{14,10},{16,20},{18,... | collective-permute-start | bytes 589832 | tf_op jit(solution)/shard_map/in_z1_x/ppermute | solution.py:33
  21.7 8.7 %collective-permute-start.10 = (bf16[64,1536]{1,0:T(8,128)(2,1)S(1)}, bf16[64,1536]{1,0:T(8,128)(2,1)S(1)}, u32[]{:S(2)}, u32[]{:S(2)}) collective-permute-start(bf16[64,1536]{1,0:T(8,128)(2,1)S(1)} %collective-permute-done.2.refs_11_), channel_id=1, source_target_pairs={{0,2},{2,0},{4,6},{6,4},{8,10},{10,8},{12,14},{14,12},{16,18},{18,... | collective-permute-start | bytes 589832 | tf_op jit(solution)/shard_map/in_core_8/ppermute | solution.py:33
  21.7 9.6 %collective-permute-start.11 = (bf16[64,1536]{1,0:T(8,128)(2,1)S(1)}, bf16[64,1536]{1,0:T(8,128)(2,1)S(1)}, u32[]{:S(2)}, u32[]{:S(2)}) collective-permute-start(bf16[64,1536]{1,0:T(8,128)(2,1)S(1)} %collective-permute-done.2.refs_11_), channel_id=1, source_target_pairs={{0,4},{2,6},{4,0},{6,2},{8,12},{10,14},{12,8},{14,10},{16,20},{18,... | collective-permute-start | bytes 589832 | tf_op jit(solution)/shard_map/in_z2_x/ppermute | solution.py:33
  23.8 9.2 %collective-permute-start.5 = (bf16[64,2560]{1,0:T(8,128)(2,1)S(1)}, bf16[64,2560]{1,0:T(8,128)(2,1)S(1)}, u32[]{:S(2)}, u32[]{:S(2)}) collective-permute-start(bf16[64,2560]{1,0:T(8,128)(2,1)S(1)} %collective-permute-done.4.refs_5_), channel_id=1, source_target_pairs={{0,2},{2,0},{4,6},{6,4},{8,10},{10,8},{12,14},{14,12},{16,18},{18,... | collective-permute-start | bytes 983048 | tf_op jit(solution)/shard_map/in_core_2/ppermute | solution.py:33
  28.9 11.0 %collective-permute-start.20 = (bf16[128,1024]{1,0:T(8,128)(2,1)S(1)}, bf16[128,1024]{1,0:T(8,128)(2,1)S(1)}, u32[]{:S(2)}, u32[]{:S(2)}) collective-permute-start(bf16[128,1024]{1,0:T(8,128)(2,1)S(1)} %pad_maximum_fusion.1.refs_2_), channel_id=1, source_target_pairs={{0,24},{2,26},{4,28},{6,30},{8,16},{10,18},{12,20},{14,22},{16,8},... | collective-permute-start | bytes 786440 | tf_op jit(solution)/shard_map/out_z3/ppermute | solution.py:33
  30.4 1.5 %collective-permute-start.15 = (bf16[64,1536]{1,0:T(8,128)(2,1)S(1)}, bf16[64,1536]{1,0:T(8,128)(2,1)S(1)}, u32[]{:S(2)}, u32[]{:S(2)}) collective-permute-start(bf16[64,1536]{1,0:T(8,128)(2,1)S(1)} %collective-permute-done.14.refs_17_), channel_id=1, source_target_pairs={{0,2},{2,0},{4,6},{6,4},{8,10},{10,8},{12,14},{14,12},{16,18},{18,... | collective-permute-start | bytes 589832 | tf_op jit(solution)/shard_map/in_core_14/ppermute | solution.py:33
  30.5 2.6 %collective-permute-start.9 = (bf16[64,1536]{1,0:T(8,128)(2,1)S(1)}, bf16[64,1536]{1,0:T(8,128)(2,1)S(1)}, u32[]{:S(2)}, u32[]{:S(2)}) collective-permute-start(bf16[64,1536]{1,0:T(8,128)(2,1)S(1)} %collective-permute-done.8.refs_9_), channel_id=1, source_target_pairs={{0,2},{2,0},{4,6},{6,4},{8,10},{10,8},{12,14},{14,12},{16,18},{18,... | collective-permute-start | bytes 589832 | tf_op jit(solution)/shard_map/in_core_6/ppermute | solution.py:33
  31.4 1.6 %collective-permute-start.12 = (bf16[64,1536]{1,0:T(8,128)(2,1)S(1)}, bf16[64,1536]{1,0:T(8,128)(2,1)S(1)}, u32[]{:S(2)}, u32[]{:S(2)}) collective-permute-start(bf16[64,1536]{1,0:T(8,128)(2,1)S(1)} %collective-permute-done.11.refs_13_), channel_id=1, source_target_pairs={{0,2},{2,0},{4,6},{6,4},{8,10},{10,8},{12,14},{14,12},{16,18},{18,... | collective-permute-start | bytes 589832 | tf_op jit(solution)/shard_map/in_core_10/ppermute | solution.py:33
  31.9 14.1 %collective-permute-start.18 = (bf16[128,1024]{1,0:T(8,128)(2,1)S(1)}, bf16[128,1024]{1,0:T(8,128)(2,1)S(1)}, u32[]{:S(2)}, u32[]{:S(2)}) collective-permute-start(bf16[128,1024]{1,0:T(8,128)(2,1)S(1)} %pad_maximum_fusion.1.refs_2_), channel_id=1, source_target_pairs={{0,8},{2,10},{4,12},{6,14},{8,0},{10,2},{12,4},{14,6},{16,24},{18,... | collective-permute-start | bytes 786440 | tf_op jit(solution)/shard_map/out_z1/ppermute | solution.py:33
  38.2 11.5 %collective-permute-start.16 = (bf16[384,512]{1,0:T(8,128)(2,1)S(1)}, bf16[384,512]{1,0:T(8,128)(2,1)S(1)}, u32[]{:S(2)}, u32[]{:S(2)}) collective-permute-start(bf16[384,512]{1,0:T(8,128)(2,1)S(1)} %get-tuple-element.21), channel_id=1, source_target_pairs={{0,1},{1,0},{2,3},{3,2},{4,5},{5,4},{6,7},{7,6},{8,9},{9,8},{10,11... | collective-permute-start | bytes 1179656 | tf_op jit(solution)/shard_map/context/ppermute | solution.py:33
  40.0 9.7 %collective-permute-start.22 = (bf16[128,1024]{1,0:T(8,128)(2,1)S(1)}, bf16[128,1024]{1,0:T(8,128)(2,1)S(1)}, u32[]{:S(2)}, u32[]{:S(2)}) collective-permute-start(bf16[128,1024]{1,0:T(8,128)(2,1)S(1)} %collective-permute-done.20.refs_6_), channel_id=1, source_target_pairs={{0,8},{2,10},{4,12},{6,14},{8,0},{10,2},{12,4},{14,6},{16,24},{18,... | collective-permute-start | bytes 786440 | tf_op jit(solution)/shard_map/out_z2/ppermute | solution.py:33
  45.9 3.8 %collective-permute-start.17 = (bf16[128,1024]{1,0:T(8,128)(2,1)S(1)}, bf16[128,1024]{1,0:T(8,128)(2,1)S(1)}, u32[]{:S(2)}, u32[]{:S(2)}) collective-permute-start(bf16[128,1024]{1,0:T(8,128)(2,1)S(1)} %pad_maximum_fusion.1.refs_2_), channel_id=1, source_target_pairs={{0,2},{2,0},{4,6},{6,4},{8,10},{10,8},{12,14},{14,12},{16,18},{18,... | collective-permute-start | bytes 786440 | tf_op jit(solution)/shard_map/out_core_0/ppermute | solution.py:33
  45.9 3.8 %collective-permute-start.19 = (bf16[128,1024]{1,0:T(8,128)(2,1)S(1)}, bf16[128,1024]{1,0:T(8,128)(2,1)S(1)}, u32[]{:S(2)}, u32[]{:S(2)}) collective-permute-start(bf16[128,1024]{1,0:T(8,128)(2,1)S(1)} %collective-permute-done.18.refs_4_), channel_id=1, source_target_pairs={{0,2},{2,0},{4,6},{6,4},{8,10},{10,8},{12,14},{14,12},{16,18},{18,... | collective-permute-start | bytes 786440 | tf_op jit(solution)/shard_map/out_core_4/ppermute | solution.py:33
  46.4 3.3 %collective-permute-start.21 = (bf16[128,1024]{1,0:T(8,128)(2,1)S(1)}, bf16[128,1024]{1,0:T(8,128)(2,1)S(1)}, u32[]{:S(2)}, u32[]{:S(2)}) collective-permute-start(bf16[128,1024]{1,0:T(8,128)(2,1)S(1)} %collective-permute-done.20.refs_6_), channel_id=1, source_target_pairs={{0,2},{2,0},{4,6},{6,4},{8,10},{10,8},{12,14},{14,12},{16,18},{18,... | collective-permute-start | bytes 786440 | tf_op jit(solution)/shard_map/out_core_12/ppermute | solution.py:33
  49.7 1.5 %collective-permute-start.23 = (bf16[128,1024]{1,0:T(8,128)(2,1)S(1)}, bf16[128,1024]{1,0:T(8,128)(2,1)S(1)}, u32[]{:S(2)}, u32[]{:S(2)}) collective-permute-start(bf16[128,1024]{1,0:T(8,128)(2,1)S(1)} %collective-permute-done.22.refs_8_), channel_id=1, source_target_pairs={{0,2},{2,0},{4,6},{6,4},{8,10},{10,8},{12,14},{14,12},{16,18},{18,... | collective-permute-start | bytes 786440 | tf_op jit(solution)/shard_map/out_core_8/ppermute | solution.py:33
  (7 other events, 60.0 us)

commit v6 on v5

--- a/solution.py
+++ b/solution.py
@@ -15,6 +15,8 @@
 
 ROUND = 3
 ROWS = 16
+UNROLLED = 36
+STEP = 256
 LONG = 10**11
 
 NEG_FILL = -1e30
@@ -33,13 +35,13 @@
         return lax.ppermute(block, axis, [(i, i ^ distance) for i in range(size)])
 
 
-def call(kernel, out_shape, in_specs, scratch=(), flops=0, nbytes=0, name=None):
+def call(kernel, out_shape, in_specs, scratch=(), flops=0, nbytes=0, name=None, out_spec=VMEM):
     many = isinstance(out_shape, (list, tuple))
     return pl.pallas_call(
         kernel,
         out_shape=out_shape,
         in_specs=in_specs,
-        out_specs=[VMEM] * len(out_shape) if many else VMEM,
+        out_specs=[out_spec] * len(out_shape) if many else out_spec,
         scratch_shapes=scratch,
         compiler_params=pltpu.CompilerParams(vmem_limit_bytes=VMEM_LIMIT),
         cost_estimate=pl.CostEstimate(
@@ -81,24 +83,36 @@
     pairs = key_ref.shape[1] // PAIR
     low = lax.broadcasted_iota(jnp.int32, (BLOCK, PAIR), 1) < HEAD_DIM
 
-    def enlist(number, count):
-        index, block = number // blocks, number % blocks
+    def enlist(index, block, count):
         column = (seat ^ (block // per_strip)) * per_strip + block % per_strip
-        listed[count] = number
+        listed[0, count] = index
+        listed[1, count] = block * BLOCK
         return count + mask_ref[index, column]
 
-    count = lax.fori_loop(0, per_strip * blocks, enlist, 0)
+    count = 0
+    if per_strip * blocks <= UNROLLED:
+        for number in range(per_strip * blocks):
+            count = enlist(number // blocks, number % blocks, count)
+    else:
+        count = lax.fori_loop(
+            0,
+            per_strip * blocks,
+            lambda number, count: enlist(number // blocks, number % blocks, count),
+            count,
+        )
     for extra in range(ROUND):
-        listed[count + extra] = per_strip * blocks
+        listed[0, count + extra] = per_strip
+        listed[1, count + extra] = 0
     rounds = (count + ROUND - 1) // ROUND
 
-    tops[...] = jnp.full(tops.shape, NEG_FILL, jnp.float32)
-    sums[...] = jnp.zeros(sums.shape, jnp.float32)
+    for index in range(per_strip):
+        tops[index] = jnp.full(tops.shape[1:], NEG_FILL, jnp.float32)
+        sums[index] = jnp.zeros(sums.shape[1:], jnp.float32)
 
     def entries(turn):
         for lane in range(ROUND):
-            number = listed[turn * ROUND + lane]
-            yield number // blocks, pl.multiple_of(number % blocks * BLOCK, BLOCK)
+            at = turn * ROUND + lane
+            yield listed[0, at], pl.multiple_of(listed[1, at], BLOCK)
 
     @pl.loop(0, rounds)
     def _(turn):
@@ -149,9 +163,9 @@
                 ],
                 axis=0,
             )
-            out_ref[pl.ds(index * BLOCK, BLOCK), pl.ds(pair * PAIR, PAIR)] = both.T.astype(
+            out_ref[pl.ds(index * BLOCK, BLOCK), pl.ds(pair * PAIR, PAIR)] = both.astype(
                 jnp.bfloat16
-            )
+            ).T
 
 
 def project_kernel(strips, parts, slots, *refs):
@@ -219,21 +233,32 @@
 def output_kernel(strips, slots, *refs):
     parts = refs[:strips]
     pieces = refs[strips : strips + len(slots)]
-    sheet_ref, bias_ref, updated_ref, context_ref, weight = refs[strips + len(slots) :]
+    sheet_ref, bias_ref, updated_ref, context_ref, weight, context, updated, done = refs[strips + len(slots) :]
     seat = lax.axis_index("seq")
-    gather_rows(list(zip(slots, pieces)), weight)
     width = parts[0].shape[1]
     for strip, part in enumerate(parts):
         first = pl.multiple_of((seat ^ strip) * width, width)
-        context_ref[:, pl.ds(first, width)] = part[...]
-    step = 256
-    for first in range(0, updated_ref.shape[1], step):
-        lanes = pl.ds(first, step)
-        found = jnp.dot(
-            context_ref[...], weight[:, lanes], preferred_element_type=jnp.float32
+        context[:, pl.ds(first, width)] = part[...]
+    whole = pltpu.make_async_copy(context, context_ref, done.at[0])
+    whole.start()
+    gather_rows(list(zip(slots, pieces)), weight)
+    half = context.shape[0] // 2
+    copies = []
+    for turn in range(2):
+        rows = pl.ds(turn * half, half)
+        for first in range(0, D, STEP):
+            lanes = pl.ds(first, STEP)
+            found = jnp.dot(
+                context[rows, :], weight[:, lanes], preferred_element_type=jnp.float32
+            )
+            found = sheet_ref[rows, lanes].astype(jnp.float32) + found + bias_ref[:, lanes]
+            updated[rows, lanes] = found.astype(jnp.bfloat16)
+        copies.append(
+            pltpu.make_async_copy(updated.at[rows, :], updated_ref.at[rows, :], done.at[turn + 1])
         )
-        found = sheet_ref[:, lanes].astype(jnp.float32) + found + bias_ref[:, lanes]
-        updated_ref[:, lanes] = found.astype(jnp.bfloat16)
+        copies[-1].start()
+    for copy in (whole, *copies):
+        copy.wait()
 
 
 def after(block, *others):
@@ -299,9 +324,8 @@
 
     for x in across:
         pieces[third + x] = swap(pieces[third], "dp", x, "in_z2_x")
-    out_ready = after(out_own, pieces[third])
-    out_second = swap(out_ready, "dp", second, "out_z3")
-    out_first = swap(out_ready, "dp", first, "out_z1")
+    out_first = swap(after(out_own, pieces[third]), "dp", first, "out_z1")
+    out_second = swap(after(out_own, pieces[third]), "dp", second, "out_z3")
     before = [pieces[third]]
     normed.extend(norm(after(sheets[k], normed[0], *before), 0) for k in range(1, strips))
 
@@ -313,7 +337,7 @@
         pltpu.VMEM((per_strip + 1, pairs, total, 2 * BLOCK), jnp.float32),
         pltpu.VMEM((per_strip + 1, pairs, 8, 2 * BLOCK), jnp.float32),
         pltpu.VMEM((per_strip + 1, pairs, PAIR + 16, 2 * BLOCK), jnp.float32),
-        pltpu.SMEM((per_strip * blocks + ROUND,), jnp.int32),
+        pltpu.SMEM((2, per_strip * blocks + ROUND), jnp.int32),
     ]
     strip_out = jax.ShapeDtypeStruct((length, width), jnp.bfloat16)
     *away, query, key, value = call(
@@ -333,7 +357,7 @@
         + work,
         name="project",
     )(
-        *masks_of[1:],
+        *after(tuple(masks_of[1:]), out_first),
         *normed,
         *[pieces[slot] for slot in slots],
         qkv_bias[None],
@@ -361,10 +385,16 @@
         functools.partial(output_kernel, strips, out_slots),
         [jax.ShapeDtypeStruct((length, D), jnp.bfloat16)] * 2,
         [VMEM] * (strips + len(out_slots) + 2),
-        [pltpu.VMEM((D, D), jnp.bfloat16)],
+        [
+            pltpu.VMEM((D, D), jnp.bfloat16),
+            pltpu.VMEM((length, D), jnp.bfloat16),
+            pltpu.VMEM((length, D), jnp.bfloat16),
+            pltpu.SemaphoreType.DMA((3,)),
+        ],
         flops=2 * length * D * D,
         nbytes=2 * D * D,
         name="output",
+        out_spec=pl.BlockSpec(memory_space=pl.ANY),
     )(
         mine,
         *returned,

time: 53.4 us -> 52.9 us (level)
  waiting for transfers between devices: 17.1 us -> 13.4 us
  starting transfers between devices: 23.1 us -> 25.9 us
    ppermute x24, waiting for transfers between devices: 17.1 us -> 13.4 us  [swap(): return lax.ppermute(block, axis, [(i, i ^ distance) for i in range(size)])]
    ppermute x24, starting transfers between devices: 23.1 us -> 25.9 us  [swap(): return lax.ppermute(block, axis, [(i, i ^ distance) for i in range(size)])]
  transfers between devices with their start and end apart: 24 -> 24, of which waited for: 10 -> 11; matrix products, arithmetic and copies ran while one was open for 0% -> 0% of each run, Pallas kernels for 17% -> 18%
where the time goes in v6:
time: 52.9 us; the launch traced here: 52.7 us
  starting transfers between devices  25.9 us (49%)
  waiting for transfers between devices  13.4 us (25%)
  Pallas kernels  11.5 us (22%)
  local copies, waits for them, and re-layouts  1.05 us (2%)
  between operations  0.81 us (2%)
    ppermute x24, starting transfers between devices, swap(): return lax.ppermute(block, axis, [(i, i ^ distance) for i in range(size)])  25.9 us
    ppermute x24, waiting for transfers between devices, swap(): return lax.ppermute(block, axis, [(i, i ^ distance) for i in range(size)])  13.4 us
    pallas_call x1, Pallas kernels, on_device(): call(functools.partial(project_kernel, strips, len(normed), [[slot] for s...  5.41 us
    pallas_call x1, Pallas kernels, on_device(): call(functools.partial(own_kernel, strips), strip_out, [SMEM] + [VMEM] *...  2.5 us
    pallas_call x1, Pallas kernels, on_device(): call(functools.partial(output_kernel, strips, out_slots), [jax.ShapeDtype...  1.97 us
    pallas_call x2, Pallas kernels, norm(): call(norm_kernel, jax.ShapeDtypeStruct((length, features), jnp.bfloat16),...  1.59 us
  transfers between devices with their start and end apart: 24, of which 11 were waited for; matrix products, arithmetic and copies ran while one was open for 0% of the time, Pallas kernels for 18%

profile of v6, /device:TPU:0, one launch (start us, length us, event | category | flops | bytes accessed | tf_op | source)
XLA Modules:
  0.0 52.7 jit_solution(13063760101186793379)
XLA Ops:
  0.7 1.0 %constant_dynamic-slice_fusion.2 = (bf16[64,512]{1,0:T(8,128)(2,1)S(1)}, bf16[64,512]{1,0:T(8,128)(2,1)S(1)}, bf16[64,512]{1,0:T(8,128)(2,1)S(1)}) fusion(bf16[64,3072]{1,0:T(8,128)(2,1)} %param.12, s32[]{:T(128)S(6)} %select_n.9, s32[]{:T(128)S(6)} %select_n.11, s32[]{:T(128)S(6)} %select_n.10), kind=kLoop, calls=%fused_computation.10 | loop fusion | bytes 393228 | tf_op jit(solution)/shard_map/dynamic_slice | solution.py:282
  1.7 5.1 %collective-permute-start.2 = (bf16[64,1536]{1,0:T(8,128)(2,1)S(1)}, bf16[64,1536]{1,0:T(8,128)(2,1)S(1)}, u32[]{:S(2)}, u32[]{:S(2)}) collective-permute-start(bf16[64,1536]{1,0:T(8,128)(2,1)S(1)} %pad_maximum_fusion.2.refs_3_), channel_id=1, source_target_pairs={{0,24},{2,26},{4,28},{6,30},{8,16},{10,18},{12,20},{14,22},{16,8},... | collective-permute-start | bytes 589832 | tf_op jit(solution)/shard_map/in_z3/ppermute | solution.py:35
  6.9 1.6 %collective-permute-start.1 = (bf16[64,2560]{1,0:T(8,128)(2,1)S(1)}, bf16[64,2560]{1,0:T(8,128)(2,1)S(1)}, u32[]{:S(2)}, u32[]{:S(2)}) collective-permute-start(bf16[64,2560]{1,0:T(8,128)(2,1)S(1)} %pad_maximum_fusion), channel_id=1, source_target_pairs={{0,4},{2,6},{4,0},{6,2},{8,12},{10,14},{12,8},{14,10},{16,20},{18,... | collective-permute-start | bytes 983048 | tf_op jit(solution)/shard_map/in_x/ppermute | solution.py:35
  8.5 1.6 %collective-permute-start = (bf16[400,1024]{1,0:T(8,128)(2,1)S(1)}, bf16[400,1024]{1,0:T(8,128)(2,1)S(1)}, u32[]{:S(2)}, u32[]{:S(2)}) collective-permute-start(bf16[400,1024]{1,0:T(8,128)(2,1)S(1)} %fusion.1), channel_id=1, source_target_pairs={{0,1},{1,0},{2,3},{3,2},{4,5},{5,4},{6,7},{7,6},{8,9},{9,8},{10,11... | collective-permute-start | bytes 2457608 | tf_op jit(solution)/shard_map/tokens/ppermute | solution.py:35
  10.1 2.5 %collective-permute-done.2.refs_15_ = bf16[64,1536]{1,0:T(8,128)(2,1)S(1)} collective-permute-done((bf16[64,1536]{1,0:T(8,128)(2,1)S(1)}, bf16[64,1536]{1,0:T(8,128)(2,1)S(1)}, u32[]{:S(2)}, u32[]{:S(2)}) %collective-permute-start.2) | collective-permute-done | bytes 196640 | tf_op jit(solution)/shard_map/in_z3/ppermute | solution.py:35
  12.6 3.1 %collective-permute-start.3 = (bf16[64,1536]{1,0:T(8,128)(2,1)S(1)}, bf16[64,1536]{1,0:T(8,128)(2,1)S(1)}, u32[]{:S(2)}, u32[]{:S(2)}) collective-permute-start(bf16[64,1536]{1,0:T(8,128)(2,1)S(1)} %collective-permute-done.2.refs_15_), channel_id=1, source_target_pairs={{0,8},{2,10},{4,12},{6,14},{8,0},{10,2},{12,4},{14,6},{16,24},{18,... | collective-permute-start | bytes 589832 | tf_op jit(solution)/shard_map/in_z2/ppermute | solution.py:35
  16.1 1.5 %collective-permute-start.15 = (bf16[64,1536]{1,0:T(8,128)(2,1)S(1)}, bf16[64,1536]{1,0:T(8,128)(2,1)S(1)}, u32[]{:S(2)}, u32[]{:S(2)}) collective-permute-start(bf16[64,1536]{1,0:T(8,128)(2,1)S(1)} %collective-permute-done.2.refs_15_), channel_id=1, source_target_pairs={{0,4},{2,6},{4,0},{6,2},{8,12},{10,14},{12,8},{14,10},{16,20},{18,... | collective-permute-start | bytes 589832 | tf_op jit(solution)/shard_map/in_z3_x/ppermute | solution.py:35
  17.6 0.8 %norm.2.refs_1_ = bf16[384,1024]{1,0:T(8,128)(2,1)S(1)} custom-call(bf16[384,1024]{1,0:T(8,128)(2,1)S(1)} %bitcast.12, f32[1,1024]{1,0:T(1,128)S(1)} %bitcast.15, f32[1,1024]{1,0:T(1,128)S(1)} %bitcast.17), custom_call_target="tpu_custom_call" | custom-call | flops 99999997952 | tf_op jit(solution)/shard_map/norm/pallas_call | solution.py:295
  18.4 1.8 %collective-permute-done.3.refs_11_ = bf16[64,1536]{1,0:T(8,128)(2,1)S(1)} collective-permute-done((bf16[64,1536]{1,0:T(8,128)(2,1)S(1)}, bf16[64,1536]{1,0:T(8,128)(2,1)S(1)}, u32[]{:S(2)}, u32[]{:S(2)}) %collective-permute-start.3) | collective-permute-done | bytes 196640 | tf_op jit(solution)/shard_map/in_z2/ppermute | solution.py:35
  20.2 1.5 %collective-permute-start.9 = (bf16[64,1536]{1,0:T(8,128)(2,1)S(1)}, bf16[64,1536]{1,0:T(8,128)(2,1)S(1)}, u32[]{:S(2)}, u32[]{:S(2)}) collective-permute-start(bf16[64,1536]{1,0:T(8,128)(2,1)S(1)} %collective-permute-done.7.refs_7_), channel_id=1, source_target_pairs={{0,4},{2,6},{4,0},{6,2},{8,12},{10,14},{12,8},{14,10},{16,20},{18,... | collective-permute-start | bytes 589832 | tf_op jit(solution)/shard_map/in_z1_x/ppermute | solution.py:35
  21.8 1.8 %collective-permute-start.4 = (bf16[128,1024]{1,0:T(8,128)(2,1)S(1)}, bf16[128,1024]{1,0:T(8,128)(2,1)S(1)}, u32[]{:S(2)}, u32[]{:S(2)}) collective-permute-start(bf16[128,1024]{1,0:T(8,128)(2,1)S(1)} %pad_maximum_fusion.1.refs_2_), channel_id=1, source_target_pairs={{0,8},{2,10},{4,12},{6,14},{8,0},{10,2},{12,4},{14,6},{16,24},{18,... | collective-permute-start | bytes 786440 | tf_op jit(solution)/shard_map/out_z1/ppermute | solution.py:35
  23.8 1.5 %collective-permute-start.12 = (bf16[64,1536]{1,0:T(8,128)(2,1)S(1)}, bf16[64,1536]{1,0:T(8,128)(2,1)S(1)}, u32[]{:S(2)}, u32[]{:S(2)}) collective-permute-start(bf16[64,1536]{1,0:T(8,128)(2,1)S(1)} %collective-permute-done.3.refs_11_), channel_id=1, source_target_pairs={{0,4},{2,6},{4,0},{6,2},{8,12},{10,14},{12,8},{14,10},{16,20},{18,... | collective-permute-start | bytes 589832 | tf_op jit(solution)/shard_map/in_z2_x/ppermute | solution.py:35
  25.3 2.3 %collective-permute-done.9.refs_9_ = bf16[64,1536]{1,0:T(8,128)(2,1)S(1)} collective-permute-done((bf16[64,1536]{1,0:T(8,128)(2,1)S(1)}, bf16[64,1536]{1,0:T(8,128)(2,1)S(1)}, u32[]{:S(2)}, u32[]{:S(2)}) %collective-permute-start.9) | collective-permute-done | bytes 196640 | tf_op jit(solution)/shard_map/in_z1_x/ppermute | solution.py:35
  27.7 2.9 %collective-permute-start.20 = (bf16[128,1024]{1,0:T(8,128)(2,1)S(1)}, bf16[128,1024]{1,0:T(8,128)(2,1)S(1)}, u32[]{:S(2)}, u32[]{:S(2)}) collective-permute-start(bf16[128,1024]{1,0:T(8,128)(2,1)S(1)} %pad_maximum_fusion.1.refs_2_), channel_id=1, source_target_pairs={{0,24},{2,26},{4,28},{6,30},{8,16},{10,18},{12,20},{14,22},{16,8},... | collective-permute-start | bytes 786440 | tf_op jit(solution)/shard_map/out_z3/ppermute | solution.py:35
  30.6 0.8 %collective-permute-done.12.refs_13_ = bf16[64,1536]{1,0:T(8,128)(2,1)S(1)} collective-permute-done((bf16[64,1536]{1,0:T(8,128)(2,1)S(1)}, bf16[64,1536]{1,0:T(8,128)(2,1)S(1)}, u32[]{:S(2)}, u32[]{:S(2)}) %collective-permute-start.12) | collective-permute-done | bytes 196640 | tf_op jit(solution)/shard_map/in_z2_x/ppermute | solution.py:35
  32.0 0.8 %norm.3.refs_2_ = bf16[384,1024]{1,0:T(8,128)(2,1)S(1)} custom-call(bf16[400,1024]{1,0:T(8,128)(2,1)S(1)} %collective-permute-done.sheet_ref, f32[1,1024]{1,0:T(1,128)S(1)} %bitcast.16, f32[1,1024]{1,0:T(1,128)S(1)} %bitcast.18), custom_call_target="tpu_custom_call" | custom-call | tf_op jit(solution)/shard_map/norm/pallas_call | solution.py:295
  33.4 5.4 %project.1 = (bf16[384,512]{1,0:T(8,128)(2,1)S(1)}, bf16[384,512]{1,0:T(8,128)(2,1)S(1)}, bf16[768,512]{1,0:T(8,128)(2,1)S(1)}, bf16[4,144,768]{2,1,0:T(8,128)(2,1)S(1)}) custom-call(s32[3,6]{1,0:T(4,128)S(1)} %slice_convert_fusion.refs_0_, bf16[384,1024]{1,0:T(8,128)(2,1)S(1)} %norm.2.refs_1_, bf16[384,1024]{1,0:T(8,128)(2,1)S(1)} %norm.3.refs_2_, ...), custom_call_target="tpu_custom_call" | custom-call | tf_op jit(solution)/shard_map/project/pallas_call | solution.py:343
  38.8 1.6 %collective-permute-start.17 = (bf16[384,512]{1,0:T(8,128)(2,1)S(1)}, bf16[384,512]{1,0:T(8,128)(2,1)S(1)}, u32[]{:S(2)}, u32[]{:S(2)}) collective-permute-start(bf16[384,512]{1,0:T(8,128)(2,1)S(1)} %get-tuple-element.24), channel_id=1, source_target_pairs={{0,1},{1,0},{2,3},{3,2},{4,5},{5,4},{6,7},{7,6},{8,9},{9,8},{10,11... | collective-permute-start | bytes 1179656 | tf_op jit(solution)/shard_map/context/ppermute | solution.py:35
  40.4 2.6 %collective-permute-start.22 = (bf16[128,1024]{1,0:T(8,128)(2,1)S(1)}, bf16[128,1024]{1,0:T(8,128)(2,1)S(1)}, u32[]{:S(2)}, u32[]{:S(2)}) collective-permute-start(bf16[128,1024]{1,0:T(8,128)(2,1)S(1)} %collective-permute-done.20.refs_6_), channel_id=1, source_target_pairs={{0,8},{2,10},{4,12},{6,14},{8,0},{10,2},{12,4},{14,6},{16,24},{18,... | collective-permute-start | bytes 786440 | tf_op jit(solution)/shard_map/out_z2/ppermute | solution.py:35
  43.0 2.5 %own_strip.1.refs_0_ = bf16[384,512]{1,0:T(8,128)(2,1)S(1)} custom-call(s32[3,6]{1,0:T(4,128)S(1)} %get-tuple-element.36.mask_ref, bf16[384,512]{1,0:T(8,128)(2,1)S(1)} %get-tuple-element.21.query_ref, bf16[768,512]{1,0:T(8,128)(2,1)S(1)} %get-tuple-element.22.key_ref, bf16[4,144,768]{2,1,0:T(8,128)(2,1)S(1)} %get-tuple-element.23.value_ref), custom_call_target="tpu_custom_call" | custom-call | flops 99999997952 | tf_op jit(solution)/shard_map/own_strip/pallas_call | solution.py:367
  46.2 3.0 %collective-permute-done.22.refs_8_ = bf16[128,1024]{1,0:T(8,128)(2,1)S(1)} collective-permute-done((bf16[128,1024]{1,0:T(8,128)(2,1)S(1)}, bf16[128,1024]{1,0:T(8,128)(2,1)S(1)}, u32[]{:S(2)}, u32[]{:S(2)}) %collective-permute-start.22) | collective-permute-done | bytes 262176 | tf_op jit(solution)/shard_map/out_z2/ppermute | solution.py:35
  49.3 0.9 %collective-permute-done.17.refs_1_ = bf16[384,512]{1,0:T(8,128)(2,1)S(1)} collective-permute-done((bf16[384,512]{1,0:T(8,128)(2,1)S(1)}, bf16[384,512]{1,0:T(8,128)(2,1)S(1)}, u32[]{:S(2)}, u32[]{:S(2)}) %collective-permute-start.17) | collective-permute-done | bytes 393248 | tf_op jit(solution)/shard_map/context/ppermute | solution.py:35
  50.1 0.6 %collective-permute-done.23.refs_9_ = bf16[128,1024]{1,0:T(8,128)(2,1)S(1)} collective-permute-done((bf16[128,1024]{1,0:T(8,128)(2,1)S(1)}, bf16[128,1024]{1,0:T(8,128)(2,1)S(1)}, u32[]{:S(2)}, u32[]{:S(2)}) %collective-permute-start.23) | collective-permute-done | bytes 262176 | tf_op jit(solution)/shard_map/out_core_8/ppermute | solution.py:35
  50.8 2.0 %output.1 = (bf16[384,1024]{1,0:T(8,128)(2,1)}, bf16[384,1024]{1,0:T(8,128)(2,1)}) custom-call(bf16[384,512]{1,0:T(8,128)(2,1)S(1)} %own_strip.1.refs_0_, bf16[384,512]{1,0:T(8,128)(2,1)S(1)} %collective-permute-done.17.refs_1_, bf16[128,1024]{1,0:T(8,128)(2,1)S(1)} %pad_maximum_fusion.1.refs_2_, bf16[128,1024]{1,0:T(8,128)(2,1)S(1)} %collective-permute-done.18.refs_3_, ...), custom_call_target="tpu_custom_call" | custom-call | flops 805306368 | bytes 2097152 | tf_op jit(solution)/shard_map/output/pallas_call | solution.py:384
  (51 shorter events, 2.8 us)
Async XLA Ops:
  1.7 10.9 %collective-permute-start.2 = (bf16[64,1536]{1,0:T(8,128)(2,1)S(1)}, bf16[64,1536]{1,0:T(8,128)(2,1)S(1)}, u32[]{:S(2)}, u32[]{:S(2)}) collective-permute-start(bf16[64,1536]{1,0:T(8,128)(2,1)S(1)} %pad_maximum_fusion.2.refs_3_), channel_id=1, source_target_pairs={{0,24},{2,26},{4,28},{6,30},{8,16},{10,18},{12,20},{14,22},{16,8},... | collective-permute-start | bytes 589832 | tf_op jit(solution)/shard_map/in_z3/ppermute | solution.py:35
  6.8 8.8 %collective-permute-start.5 = (bf16[64,1536]{1,0:T(8,128)(2,1)S(1)}, bf16[64,1536]{1,0:T(8,128)(2,1)S(1)}, u32[]{:S(2)}, u32[]{:S(2)}) collective-permute-start(bf16[64,1536]{1,0:T(8,128)(2,1)S(1)} %pad_maximum_fusion.2.refs_3_), channel_id=1, source_target_pairs={{0,2},{2,0},{4,6},{6,4},{8,10},{10,8},{12,14},{14,12},{16,18},{18,... | collective-permute-start | bytes 589832 | tf_op jit(solution)/shard_map/in_core_0/ppermute | solution.py:35
  6.8 9.2 %collective-permute-start.7 = (bf16[64,1536]{1,0:T(8,128)(2,1)S(1)}, bf16[64,1536]{1,0:T(8,128)(2,1)S(1)}, u32[]{:S(2)}, u32[]{:S(2)}) collective-permute-start(bf16[64,1536]{1,0:T(8,128)(2,1)S(1)} %pad_maximum_fusion.2.refs_3_), channel_id=1, source_target_pairs={{0,8},{2,10},{4,12},{6,14},{8,0},{10,2},{12,4},{14,6},{16,24},{18,... | collective-permute-start | bytes 589832 | tf_op jit(solution)/shard_map/in_z1/ppermute | solution.py:35
  6.9 10.7 %collective-permute-start.1 = (bf16[64,2560]{1,0:T(8,128)(2,1)S(1)}, bf16[64,2560]{1,0:T(8,128)(2,1)S(1)}, u32[]{:S(2)}, u32[]{:S(2)}) collective-permute-start(bf16[64,2560]{1,0:T(8,128)(2,1)S(1)} %pad_maximum_fusion), channel_id=1, source_target_pairs={{0,4},{2,6},{4,0},{6,2},{8,12},{10,14},{12,8},{14,10},{16,20},{18,... | collective-permute-start | bytes 983048 | tf_op jit(solution)/shard_map/in_x/ppermute | solution.py:35
  8.5 23.4 %collective-permute-start = (bf16[400,1024]{1,0:T(8,128)(2,1)S(1)}, bf16[400,1024]{1,0:T(8,128)(2,1)S(1)}, u32[]{:S(2)}, u32[]{:S(2)}) collective-permute-start(bf16[400,1024]{1,0:T(8,128)(2,1)S(1)} %fusion.1), channel_id=1, source_target_pairs={{0,1},{1,0},{2,3},{3,2},{4,5},{5,4},{6,7},{7,6},{8,9},{9,8},{10,11... | collective-permute-start | bytes 2457608 | tf_op jit(solution)/shard_map/tokens/ppermute | solution.py:35
  12.6 7.7 %collective-permute-start.3 = (bf16[64,1536]{1,0:T(8,128)(2,1)S(1)}, bf16[64,1536]{1,0:T(8,128)(2,1)S(1)}, u32[]{:S(2)}, u32[]{:S(2)}) collective-permute-start(bf16[64,1536]{1,0:T(8,128)(2,1)S(1)} %collective-permute-done.2.refs_15_), channel_id=1, source_target_pairs={{0,8},{2,10},{4,12},{6,14},{8,0},{10,2},{12,4},{14,6},{16,24},{18,... | collective-permute-start | bytes 589832 | tf_op jit(solution)/shard_map/in_z2/ppermute | solution.py:35
  15.6 7.9 %collective-permute-start.14 = (bf16[64,1536]{1,0:T(8,128)(2,1)S(1)}, bf16[64,1536]{1,0:T(8,128)(2,1)S(1)}, u32[]{:S(2)}, u32[]{:S(2)}) collective-permute-start(bf16[64,1536]{1,0:T(8,128)(2,1)S(1)} %collective-permute-done.2.refs_15_), channel_id=1, source_target_pairs={{0,2},{2,0},{4,6},{6,4},{8,10},{10,8},{12,14},{14,12},{16,18},{18,... | collective-permute-start | bytes 589832 | tf_op jit(solution)/shard_map/in_core_12/ppermute | solution.py:35
  16.1 7.8 %collective-permute-start.15 = (bf16[64,1536]{1,0:T(8,128)(2,1)S(1)}, bf16[64,1536]{1,0:T(8,128)(2,1)S(1)}, u32[]{:S(2)}, u32[]{:S(2)}) collective-permute-start(bf16[64,1536]{1,0:T(8,128)(2,1)S(1)} %collective-permute-done.2.refs_15_), channel_id=1, source_target_pairs={{0,4},{2,6},{4,0},{6,2},{8,12},{10,14},{12,8},{14,10},{16,20},{18,... | collective-permute-start | bytes 589832 | tf_op jit(solution)/shard_map/in_z3_x/ppermute | solution.py:35
  17.6 4.2 %collective-permute-start.8 = (bf16[64,1536]{1,0:T(8,128)(2,1)S(1)}, bf16[64,1536]{1,0:T(8,128)(2,1)S(1)}, u32[]{:S(2)}, u32[]{:S(2)}) collective-permute-start(bf16[64,1536]{1,0:T(8,128)(2,1)S(1)} %collective-permute-done.7.refs_7_), channel_id=1, source_target_pairs={{0,2},{2,0},{4,6},{6,4},{8,10},{10,8},{12,14},{14,12},{16,18},{18,... | collective-permute-start | bytes 589832 | tf_op jit(solution)/shard_map/in_core_4/ppermute | solution.py:35
  20.2 7.4 %collective-permute-start.9 = (bf16[64,1536]{1,0:T(8,128)(2,1)S(1)}, bf16[64,1536]{1,0:T(8,128)(2,1)S(1)}, u32[]{:S(2)}, u32[]{:S(2)}) collective-permute-start(bf16[64,1536]{1,0:T(8,128)(2,1)S(1)} %collective-permute-done.7.refs_7_), channel_id=1, source_target_pairs={{0,4},{2,6},{4,0},{6,2},{8,12},{10,14},{12,8},{14,10},{16,20},{18,... | collective-permute-start | bytes 589832 | tf_op jit(solution)/shard_map/in_z1_x/ppermute | solution.py:35
  21.8 9.6 %collective-permute-start.4 = (bf16[128,1024]{1,0:T(8,128)(2,1)S(1)}, bf16[128,1024]{1,0:T(8,128)(2,1)S(1)}, u32[]{:S(2)}, u32[]{:S(2)}) collective-permute-start(bf16[128,1024]{1,0:T(8,128)(2,1)S(1)} %pad_maximum_fusion.1.refs_2_), channel_id=1, source_target_pairs={{0,8},{2,10},{4,12},{6,14},{8,0},{10,2},{12,4},{14,6},{16,24},{18,... | collective-permute-start | bytes 786440 | tf_op jit(solution)/shard_map/out_z1/ppermute | solution.py:35
  23.5 4.1 %collective-permute-start.11 = (bf16[64,1536]{1,0:T(8,128)(2,1)S(1)}, bf16[64,1536]{1,0:T(8,128)(2,1)S(1)}, u32[]{:S(2)}, u32[]{:S(2)}) collective-permute-start(bf16[64,1536]{1,0:T(8,128)(2,1)S(1)} %collective-permute-done.3.refs_11_), channel_id=1, source_target_pairs={{0,2},{2,0},{4,6},{6,4},{8,10},{10,8},{12,14},{14,12},{16,18},{18,... | collective-permute-start | bytes 589832 | tf_op jit(solution)/shard_map/in_core_8/ppermute | solution.py:35
  23.8 7.6 %collective-permute-start.12 = (bf16[64,1536]{1,0:T(8,128)(2,1)S(1)}, bf16[64,1536]{1,0:T(8,128)(2,1)S(1)}, u32[]{:S(2)}, u32[]{:S(2)}) collective-permute-start(bf16[64,1536]{1,0:T(8,128)(2,1)S(1)} %collective-permute-done.3.refs_11_), channel_id=1, source_target_pairs={{0,4},{2,6},{4,0},{6,2},{8,12},{10,14},{12,8},{14,10},{16,20},{18,... | collective-permute-start | bytes 589832 | tf_op jit(solution)/shard_map/in_z2_x/ppermute | solution.py:35
  27.6 5.2 %collective-permute-start.6 = (bf16[64,2560]{1,0:T(8,128)(2,1)S(1)}, bf16[64,2560]{1,0:T(8,128)(2,1)S(1)}, u32[]{:S(2)}, u32[]{:S(2)}) collective-permute-start(bf16[64,2560]{1,0:T(8,128)(2,1)S(1)} %collective-permute-done.1.refs_5_), channel_id=1, source_target_pairs={{0,2},{2,0},{4,6},{6,4},{8,10},{10,8},{12,14},{14,12},{16,18},{18,... | collective-permute-start | bytes 983048 | tf_op jit(solution)/shard_map/in_core_2/ppermute | solution.py:35
  27.7 12.8 %collective-permute-start.20 = (bf16[128,1024]{1,0:T(8,128)(2,1)S(1)}, bf16[128,1024]{1,0:T(8,128)(2,1)S(1)}, u32[]{:S(2)}, u32[]{:S(2)}) collective-permute-start(bf16[128,1024]{1,0:T(8,128)(2,1)S(1)} %pad_maximum_fusion.1.refs_2_), channel_id=1, source_target_pairs={{0,24},{2,26},{4,28},{6,30},{8,16},{10,18},{12,20},{14,22},{16,8},... | collective-permute-start | bytes 786440 | tf_op jit(solution)/shard_map/out_z3/ppermute | solution.py:35
  31.4 1.4 %collective-permute-start.16 = (bf16[64,1536]{1,0:T(8,128)(2,1)S(1)}, bf16[64,1536]{1,0:T(8,128)(2,1)S(1)}, u32[]{:S(2)}, u32[]{:S(2)}) collective-permute-start(bf16[64,1536]{1,0:T(8,128)(2,1)S(1)} %collective-permute-done.15.refs_17_), channel_id=1, source_target_pairs={{0,2},{2,0},{4,6},{6,4},{8,10},{10,8},{12,14},{14,12},{16,18},{18,... | collective-permute-start | bytes 589832 | tf_op jit(solution)/shard_map/in_core_14/ppermute | solution.py:35
  31.4 1.7 %collective-permute-start.10 = (bf16[64,1536]{1,0:T(8,128)(2,1)S(1)}, bf16[64,1536]{1,0:T(8,128)(2,1)S(1)}, u32[]{:S(2)}, u32[]{:S(2)}) collective-permute-start(bf16[64,1536]{1,0:T(8,128)(2,1)S(1)} %collective-permute-done.9.refs_9_), channel_id=1, source_target_pairs={{0,2},{2,0},{4,6},{6,4},{8,10},{10,8},{12,14},{14,12},{16,18},{18,... | collective-permute-start | bytes 589832 | tf_op jit(solution)/shard_map/in_core_6/ppermute | solution.py:35
  31.9 1.5 %collective-permute-start.13 = (bf16[64,1536]{1,0:T(8,128)(2,1)S(1)}, bf16[64,1536]{1,0:T(8,128)(2,1)S(1)}, u32[]{:S(2)}, u32[]{:S(2)}) collective-permute-start(bf16[64,1536]{1,0:T(8,128)(2,1)S(1)} %collective-permute-done.12.refs_13_), channel_id=1, source_target_pairs={{0,2},{2,0},{4,6},{6,4},{8,10},{10,8},{12,14},{14,12},{16,18},{18,... | collective-permute-start | bytes 589832 | tf_op jit(solution)/shard_map/in_core_10/ppermute | solution.py:35
  38.8 11.3 %collective-permute-start.17 = (bf16[384,512]{1,0:T(8,128)(2,1)S(1)}, bf16[384,512]{1,0:T(8,128)(2,1)S(1)}, u32[]{:S(2)}, u32[]{:S(2)}) collective-permute-start(bf16[384,512]{1,0:T(8,128)(2,1)S(1)} %get-tuple-element.24), channel_id=1, source_target_pairs={{0,1},{1,0},{2,3},{3,2},{4,5},{5,4},{6,7},{7,6},{8,9},{9,8},{10,11... | collective-permute-start | bytes 1179656 | tf_op jit(solution)/shard_map/context/ppermute | solution.py:35
  40.4 8.8 %collective-permute-start.22 = (bf16[128,1024]{1,0:T(8,128)(2,1)S(1)}, bf16[128,1024]{1,0:T(8,128)(2,1)S(1)}, u32[]{:S(2)}, u32[]{:S(2)}) collective-permute-start(bf16[128,1024]{1,0:T(8,128)(2,1)S(1)} %collective-permute-done.20.refs_6_), channel_id=1, source_target_pairs={{0,8},{2,10},{4,12},{6,14},{8,0},{10,2},{12,4},{14,6},{16,24},{18,... | collective-permute-start | bytes 786440 | tf_op jit(solution)/shard_map/out_z2/ppermute | solution.py:35
  45.5 3.7 %collective-permute-start.18 = (bf16[128,1024]{1,0:T(8,128)(2,1)S(1)}, bf16[128,1024]{1,0:T(8,128)(2,1)S(1)}, u32[]{:S(2)}, u32[]{:S(2)}) collective-permute-start(bf16[128,1024]{1,0:T(8,128)(2,1)S(1)} %pad_maximum_fusion.1.refs_2_), channel_id=1, source_target_pairs={{0,2},{2,0},{4,6},{6,4},{8,10},{10,8},{12,14},{14,12},{16,18},{18,... | collective-permute-start | bytes 786440 | tf_op jit(solution)/shard_map/out_core_0/ppermute | solution.py:35
  45.6 3.6 %collective-permute-start.19 = (bf16[128,1024]{1,0:T(8,128)(2,1)S(1)}, bf16[128,1024]{1,0:T(8,128)(2,1)S(1)}, u32[]{:S(2)}, u32[]{:S(2)}) collective-permute-start(bf16[128,1024]{1,0:T(8,128)(2,1)S(1)} %collective-permute-done.4.refs_4_), channel_id=1, source_target_pairs={{0,2},{2,0},{4,6},{6,4},{8,10},{10,8},{12,14},{14,12},{16,18},{18,... | collective-permute-start | bytes 786440 | tf_op jit(solution)/shard_map/out_core_4/ppermute | solution.py:35
  46.1 3.1 %collective-permute-start.21 = (bf16[128,1024]{1,0:T(8,128)(2,1)S(1)}, bf16[128,1024]{1,0:T(8,128)(2,1)S(1)}, u32[]{:S(2)}, u32[]{:S(2)}) collective-permute-start(bf16[128,1024]{1,0:T(8,128)(2,1)S(1)} %collective-permute-done.20.refs_6_), channel_id=1, source_target_pairs={{0,2},{2,0},{4,6},{6,4},{8,10},{10,8},{12,14},{14,12},{16,18},{18,... | collective-permute-start | bytes 786440 | tf_op jit(solution)/shard_map/out_core_12/ppermute | solution.py:35
  49.2 1.5 %collective-permute-start.23 = (bf16[128,1024]{1,0:T(8,128)(2,1)S(1)}, bf16[128,1024]{1,0:T(8,128)(2,1)S(1)}, u32[]{:S(2)}, u32[]{:S(2)}) collective-permute-start(bf16[128,1024]{1,0:T(8,128)(2,1)S(1)} %collective-permute-done.22.refs_8_), channel_id=1, source_target_pairs={{0,2},{2,0},{4,6},{6,4},{8,10},{10,8},{12,14},{14,12},{16,18},{18,... | collective-permute-start | bytes 786440 | tf_op jit(solution)/shard_map/out_core_8/ppermute | solution.py:35
  (7 other events, 62.6 us)

commit v7 on v6

--- a/solution.py
+++ b/solution.py
@@ -323,14 +323,15 @@
         pieces[second + x] = swap(pieces[second], "dp", x, "in_z3_x")
 
     for x in across:
-        pieces[third + x] = swap(pieces[third], "dp", x, "in_z2_x")
+        pieces[third + x] = swap(after(pieces[third], pieces[second + x]), "dp", x, "in_z2_x")
     out_first = swap(after(out_own, pieces[third]), "dp", first, "out_z1")
     out_second = swap(after(out_own, pieces[third]), "dp", second, "out_z3")
     before = [pieces[third]]
     normed.extend(norm(after(sheets[k], normed[0], *before), 0) for k in range(1, strips))
 
     for slot in sorted(pieces):
-        pieces[slot + 1] = swap(pieces[slot], "dp", 1, f"in_core_{slot}")
+        ready = after(pieces[slot], *normed[1:]) if slot == first + across[-1] else pieces[slot]
+        pieces[slot + 1] = swap(ready, "dp", 1, f"in_core_{slot}")
     slots = sorted(pieces)
 
     work = [

time: 52.9 us -> 52.7 us (level)
  Pallas kernels: 11.5 us -> 9.85 us
  waiting for transfers between devices: 13.4 us -> 14.9 us
    ppermute x24, waiting for transfers between devices: 13.4 us -> 14.9 us  [swap(): return lax.ppermute(block, axis, [(i, i ^ distance) for i in range(size)])]
    pallas_call x1, Pallas kernels: 2.5 us -> 1.67 us  [on_device(): call(functools.partial(own_kernel, strips), strip_out, [SMEM] + [VMEM] *...]
    pallas_call x1, Pallas kernels: 5.41 us -> 4.61 us  [on_device(): call(functools.partial(project_kernel, strips, len(normed), [[slot] for s...]
  transfers between devices with their start and end apart: 24 -> 24, of which waited for: 11 -> 10; matrix products, arithmetic and copies ran while one was open for 0% -> 0% of each run, Pallas kernels for 18% -> 15%
where the time goes in v7:
time: 52.7 us; the launch traced here: 52.6 us
  starting transfers between devices  25.9 us (49%)
  waiting for transfers between devices  14.9 us (28%)
  Pallas kernels  9.85 us (19%)
  local copies, waits for them, and re-layouts  1.05 us (2%)
  between operations  0.83 us (2%)
    ppermute x24, starting transfers between devices, swap(): return lax.ppermute(block, axis, [(i, i ^ distance) for i in range(size)])  25.9 us
    ppermute x24, waiting for transfers between devices, swap(): return lax.ppermute(block, axis, [(i, i ^ distance) for i in range(size)])  14.9 us
    pallas_call x1, Pallas kernels, on_device(): call(functools.partial(project_kernel, strips, len(normed), [[slot] for s...  4.61 us
    pallas_call x1, Pallas kernels, on_device(): call(functools.partial(output_kernel, strips, out_slots), [jax.ShapeDtype...  1.97 us
    pallas_call x1, Pallas kernels, on_device(): call(functools.partial(own_kernel, strips), strip_out, [SMEM] + [VMEM] *...  1.67 us
    pallas_call x2, Pallas kernels, norm(): call(norm_kernel, jax.ShapeDtypeStruct((length, features), jnp.bfloat16),...  1.6 us
  transfers between devices with their start and end apart: 24, of which 10 were waited for; matrix products, arithmetic and copies ran while one was open for 0% of the time, Pallas kernels for 15%

profile of v7, /device:TPU:0, one launch (start us, length us, event | category | flops | bytes accessed | tf_op | source)
XLA Modules:
  0.0 52.6 jit_solution(5318648207024705566)
XLA Ops:
  0.7 1.0 %constant_dynamic-slice_fusion.2 = (bf16[64,512]{1,0:T(8,128)(2,1)S(1)}, bf16[64,512]{1,0:T(8,128)(2,1)S(1)}, bf16[64,512]{1,0:T(8,128)(2,1)S(1)}) fusion(bf16[64,3072]{1,0:T(8,128)(2,1)} %param.12, s32[]{:T(128)S(6)} %select_n.9, s32[]{:T(128)S(6)} %select_n.11, s32[]{:T(128)S(6)} %select_n.10), kind=kLoop, calls=%fused_computation.10 | loop fusion | bytes 393228 | tf_op jit(solution)/shard_map/dynamic_slice | solution.py:282
  1.7 5.1 %collective-permute-start.2 = (bf16[64,1536]{1,0:T(8,128)(2,1)S(1)}, bf16[64,1536]{1,0:T(8,128)(2,1)S(1)}, u32[]{:S(2)}, u32[]{:S(2)}) collective-permute-start(bf16[64,1536]{1,0:T(8,128)(2,1)S(1)} %pad_maximum_fusion.2.refs_3_), channel_id=1, source_target_pairs={{0,24},{2,26},{4,28},{6,30},{8,16},{10,18},{12,20},{14,22},{16,8},... | collective-permute-start | bytes 589832 | tf_op jit(solution)/shard_map/in_z3/ppermute | solution.py:35
  6.9 1.6 %collective-permute-start.1 = (bf16[64,2560]{1,0:T(8,128)(2,1)S(1)}, bf16[64,2560]{1,0:T(8,128)(2,1)S(1)}, u32[]{:S(2)}, u32[]{:S(2)}) collective-permute-start(bf16[64,2560]{1,0:T(8,128)(2,1)S(1)} %pad_maximum_fusion), channel_id=1, source_target_pairs={{0,4},{2,6},{4,0},{6,2},{8,12},{10,14},{12,8},{14,10},{16,20},{18,... | collective-permute-start | bytes 983048 | tf_op jit(solution)/shard_map/in_x/ppermute | solution.py:35
  8.5 1.6 %collective-permute-start = (bf16[400,1024]{1,0:T(8,128)(2,1)S(1)}, bf16[400,1024]{1,0:T(8,128)(2,1)S(1)}, u32[]{:S(2)}, u32[]{:S(2)}) collective-permute-start(bf16[400,1024]{1,0:T(8,128)(2,1)S(1)} %fusion.1), channel_id=1, source_target_pairs={{0,1},{1,0},{2,3},{3,2},{4,5},{5,4},{6,7},{7,6},{8,9},{9,8},{10,11... | collective-permute-start | bytes 2457608 | tf_op jit(solution)/shard_map/tokens/ppermute | solution.py:35
  10.1 2.5 %collective-permute-done.2.refs_15_ = bf16[64,1536]{1,0:T(8,128)(2,1)S(1)} collective-permute-done((bf16[64,1536]{1,0:T(8,128)(2,1)S(1)}, bf16[64,1536]{1,0:T(8,128)(2,1)S(1)}, u32[]{:S(2)}, u32[]{:S(2)}) %collective-permute-start.2) | collective-permute-done | bytes 196640 | tf_op jit(solution)/shard_map/in_z3/ppermute | solution.py:35
  12.6 3.1 %collective-permute-start.3 = (bf16[64,1536]{1,0:T(8,128)(2,1)S(1)}, bf16[64,1536]{1,0:T(8,128)(2,1)S(1)}, u32[]{:S(2)}, u32[]{:S(2)}) collective-permute-start(bf16[64,1536]{1,0:T(8,128)(2,1)S(1)} %collective-permute-done.2.refs_15_), channel_id=1, source_target_pairs={{0,8},{2,10},{4,12},{6,14},{8,0},{10,2},{12,4},{14,6},{16,24},{18,... | collective-permute-start | bytes 589832 | tf_op jit(solution)/shard_map/in_z2/ppermute | solution.py:35
  15.6 1.5 %collective-permute-start.12 = (bf16[64,1536]{1,0:T(8,128)(2,1)S(1)}, bf16[64,1536]{1,0:T(8,128)(2,1)S(1)}, u32[]{:S(2)}, u32[]{:S(2)}) collective-permute-start(bf16[64,1536]{1,0:T(8,128)(2,1)S(1)} %collective-permute-done.2.refs_15_), channel_id=1, source_target_pairs={{0,4},{2,6},{4,0},{6,2},{8,12},{10,14},{12,8},{14,10},{16,20},{18,... | collective-permute-start | bytes 589832 | tf_op jit(solution)/shard_map/in_z3_x/ppermute | solution.py:35
  17.7 0.8 %norm.2.refs_1_ = bf16[384,1024]{1,0:T(8,128)(2,1)S(1)} custom-call(bf16[384,1024]{1,0:T(8,128)(2,1)S(1)} %bitcast.12, f32[1,1024]{1,0:T(1,128)S(1)} %bitcast.15, f32[1,1024]{1,0:T(1,128)S(1)} %bitcast.17), custom_call_target="tpu_custom_call" | custom-call | flops 99999997952 | tf_op jit(solution)/shard_map/norm/pallas_call | solution.py:295
  18.5 1.8 %collective-permute-done.3.refs_11_ = bf16[64,1536]{1,0:T(8,128)(2,1)S(1)} collective-permute-done((bf16[64,1536]{1,0:T(8,128)(2,1)S(1)}, bf16[64,1536]{1,0:T(8,128)(2,1)S(1)}, u32[]{:S(2)}, u32[]{:S(2)}) %collective-permute-start.3) | collective-permute-done | bytes 196640 | tf_op jit(solution)/shard_map/in_z2/ppermute | solution.py:35
  20.2 1.5 %collective-permute-start.9 = (bf16[64,1536]{1,0:T(8,128)(2,1)S(1)}, bf16[64,1536]{1,0:T(8,128)(2,1)S(1)}, u32[]{:S(2)}, u32[]{:S(2)}) collective-permute-start(bf16[64,1536]{1,0:T(8,128)(2,1)S(1)} %collective-permute-done.7.refs_7_), channel_id=1, source_target_pairs={{0,4},{2,6},{4,0},{6,2},{8,12},{10,14},{12,8},{14,10},{16,20},{18,... | collective-permute-start | bytes 589832 | tf_op jit(solution)/shard_map/in_z1_x/ppermute | solution.py:35
  21.8 1.8 %collective-permute-start.4 = (bf16[128,1024]{1,0:T(8,128)(2,1)S(1)}, bf16[128,1024]{1,0:T(8,128)(2,1)S(1)}, u32[]{:S(2)}, u32[]{:S(2)}) collective-permute-start(bf16[128,1024]{1,0:T(8,128)(2,1)S(1)} %pad_maximum_fusion.1.refs_2_), channel_id=1, source_target_pairs={{0,8},{2,10},{4,12},{6,14},{8,0},{10,2},{12,4},{14,6},{16,24},{18,... | collective-permute-start | bytes 786440 | tf_op jit(solution)/shard_map/out_z1/ppermute | solution.py:35
  23.5 1.0 %collective-permute-start.13 = (bf16[64,1536]{1,0:T(8,128)(2,1)S(1)}, bf16[64,1536]{1,0:T(8,128)(2,1)S(1)}, u32[]{:S(2)}, u32[]{:S(2)}) collective-permute-start(bf16[64,1536]{1,0:T(8,128)(2,1)S(1)} %collective-permute-done.3.refs_11_), channel_id=1, source_target_pairs={{0,4},{2,6},{4,0},{6,2},{8,12},{10,14},{12,8},{14,10},{16,20},{18,... | collective-permute-start | bytes 589832 | tf_op jit(solution)/shard_map/in_z2_x/ppermute | solution.py:35
  24.6 1.4 %collective-permute-done.9.refs_9_ = bf16[64,1536]{1,0:T(8,128)(2,1)S(1)} collective-permute-done((bf16[64,1536]{1,0:T(8,128)(2,1)S(1)}, bf16[64,1536]{1,0:T(8,128)(2,1)S(1)}, u32[]{:S(2)}, u32[]{:S(2)}) %collective-permute-start.9) | collective-permute-done | bytes 196640 | tf_op jit(solution)/shard_map/in_z1_x/ppermute | solution.py:35
  25.9 3.0 %collective-permute-done.sheet_ref = bf16[400,1024]{1,0:T(8,128)(2,1)S(1)} collective-permute-done((bf16[400,1024]{1,0:T(8,128)(2,1)S(1)}, bf16[400,1024]{1,0:T(8,128)(2,1)S(1)}, u32[]{:S(2)}, u32[]{:S(2)}) %collective-permute-start) | collective-permute-done | bytes 819232 | tf_op jit(solution)/shard_map/tokens/ppermute | solution.py:35
  28.9 0.6 %collective-permute-start.20 = (bf16[128,1024]{1,0:T(8,128)(2,1)S(1)}, bf16[128,1024]{1,0:T(8,128)(2,1)S(1)}, u32[]{:S(2)}, u32[]{:S(2)}) collective-permute-start(bf16[128,1024]{1,0:T(8,128)(2,1)S(1)} %pad_maximum_fusion.1.refs_2_), channel_id=1, source_target_pairs={{0,24},{2,26},{4,28},{6,30},{8,16},{10,18},{12,20},{14,22},{16,8},... | collective-permute-start | bytes 786440 | tf_op jit(solution)/shard_map/out_z3/ppermute | solution.py:35
  29.6 0.8 %norm.3.refs_2_ = bf16[384,1024]{1,0:T(8,128)(2,1)S(1)} custom-call(bf16[400,1024]{1,0:T(8,128)(2,1)S(1)} %collective-permute-done.sheet_ref, f32[1,1024]{1,0:T(1,128)S(1)} %bitcast.16, f32[1,1024]{1,0:T(1,128)S(1)} %bitcast.18), custom_call_target="tpu_custom_call" | custom-call | tf_op jit(solution)/shard_map/norm/pallas_call | solution.py:295
  31.4 0.5 collective-permute-done.16.refs_18_
  32.6 4.6 %project.1 = (bf16[384,512]{1,0:T(8,128)(2,1)S(1)}, bf16[384,512]{1,0:T(8,128)(2,1)S(1)}, bf16[768,512]{1,0:T(8,128)(2,1)S(1)}, bf16[4,144,768]{2,1,0:T(8,128)(2,1)S(1)}) custom-call(s32[3,6]{1,0:T(4,128)S(1)} %slice_convert_fusion.refs_0_, bf16[384,1024]{1,0:T(8,128)(2,1)S(1)} %norm.2.refs_1_, bf16[384,1024]{1,0:T(8,128)(2,1)S(1)} %norm.3.refs_2_, ...), custom_call_target="tpu_custom_call" | custom-call | tf_op jit(solution)/shard_map/project/pallas_call | solution.py:344
  37.2 1.6 %collective-permute-start.17 = (bf16[384,512]{1,0:T(8,128)(2,1)S(1)}, bf16[384,512]{1,0:T(8,128)(2,1)S(1)}, u32[]{:S(2)}, u32[]{:S(2)}) collective-permute-start(bf16[384,512]{1,0:T(8,128)(2,1)S(1)} %get-tuple-element.28), channel_id=1, source_target_pairs={{0,1},{1,0},{2,3},{3,2},{4,5},{5,4},{6,7},{7,6},{8,9},{9,8},{10,11... | collective-permute-start | bytes 1179656 | tf_op jit(solution)/shard_map/context/ppermute | solution.py:35
  38.8 4.8 %collective-permute-start.22 = (bf16[128,1024]{1,0:T(8,128)(2,1)S(1)}, bf16[128,1024]{1,0:T(8,128)(2,1)S(1)}, u32[]{:S(2)}, u32[]{:S(2)}) collective-permute-start(bf16[128,1024]{1,0:T(8,128)(2,1)S(1)} %collective-permute-done.20.refs_6_), channel_id=1, source_target_pairs={{0,8},{2,10},{4,12},{6,14},{8,0},{10,2},{12,4},{14,6},{16,24},{18,... | collective-permute-start | bytes 786440 | tf_op jit(solution)/shard_map/out_z2/ppermute | solution.py:35
  43.6 1.7 %own_strip.1.refs_0_ = bf16[384,512]{1,0:T(8,128)(2,1)S(1)} custom-call(s32[3,6]{1,0:T(4,128)S(1)} %get-tuple-element.40.mask_ref, bf16[384,512]{1,0:T(8,128)(2,1)S(1)} %get-tuple-element.25.query_ref, bf16[768,512]{1,0:T(8,128)(2,1)S(1)} %get-tuple-element.26.key_ref, bf16[4,144,768]{2,1,0:T(8,128)(2,1)S(1)} %get-tuple-element.27.value_ref), custom_call_target="tpu_custom_call" | custom-call | flops 99999997952 | tf_op jit(solution)/shard_map/own_strip/pallas_call | solution.py:368
  45.9 3.1 %collective-permute-done.22.refs_8_ = bf16[128,1024]{1,0:T(8,128)(2,1)S(1)} collective-permute-done((bf16[128,1024]{1,0:T(8,128)(2,1)S(1)}, bf16[128,1024]{1,0:T(8,128)(2,1)S(1)}, u32[]{:S(2)}, u32[]{:S(2)}) %collective-permute-start.22) | collective-permute-done | bytes 262176 | tf_op jit(solution)/shard_map/out_z2/ppermute | solution.py:35
  49.1 1.5 %collective-permute-done.23.refs_9_ = bf16[128,1024]{1,0:T(8,128)(2,1)S(1)} collective-permute-done((bf16[128,1024]{1,0:T(8,128)(2,1)S(1)}, bf16[128,1024]{1,0:T(8,128)(2,1)S(1)}, u32[]{:S(2)}, u32[]{:S(2)}) %collective-permute-start.23) | collective-permute-done | bytes 262176 | tf_op jit(solution)/shard_map/out_core_8/ppermute | solution.py:35
  50.6 2.0 %output.1 = (bf16[384,1024]{1,0:T(8,128)(2,1)}, bf16[384,1024]{1,0:T(8,128)(2,1)}) custom-call(bf16[384,512]{1,0:T(8,128)(2,1)S(1)} %own_strip.1.refs_0_, bf16[384,512]{1,0:T(8,128)(2,1)S(1)} %collective-permute-done.17.refs_1_, bf16[128,1024]{1,0:T(8,128)(2,1)S(1)} %pad_maximum_fusion.1.refs_2_, bf16[128,1024]{1,0:T(8,128)(2,1)S(1)} %collective-permute-done.18.refs_3_, ...), custom_call_target="tpu_custom_call" | custom-call | flops 805306368 | bytes 2097152 | tf_op jit(solution)/shard_map/output/pallas_call | solution.py:385
  (51 shorter events, 3.0 us)
Async XLA Ops:
  1.7 10.9 %collective-permute-start.2 = (bf16[64,1536]{1,0:T(8,128)(2,1)S(1)}, bf16[64,1536]{1,0:T(8,128)(2,1)S(1)}, u32[]{:S(2)}, u32[]{:S(2)}) collective-permute-start(bf16[64,1536]{1,0:T(8,128)(2,1)S(1)} %pad_maximum_fusion.2.refs_3_), channel_id=1, source_target_pairs={{0,24},{2,26},{4,28},{6,30},{8,16},{10,18},{12,20},{14,22},{16,8},... | collective-permute-start | bytes 589832 | tf_op jit(solution)/shard_map/in_z3/ppermute | solution.py:35
  6.8 8.8 %collective-permute-start.5 = (bf16[64,1536]{1,0:T(8,128)(2,1)S(1)}, bf16[64,1536]{1,0:T(8,128)(2,1)S(1)}, u32[]{:S(2)}, u32[]{:S(2)}) collective-permute-start(bf16[64,1536]{1,0:T(8,128)(2,1)S(1)} %pad_maximum_fusion.2.refs_3_), channel_id=1, source_target_pairs={{0,2},{2,0},{4,6},{6,4},{8,10},{10,8},{12,14},{14,12},{16,18},{18,... | collective-permute-start | bytes 589832 | tf_op jit(solution)/shard_map/in_core_0/ppermute | solution.py:35
  6.8 10.3 %collective-permute-start.7 = (bf16[64,1536]{1,0:T(8,128)(2,1)S(1)}, bf16[64,1536]{1,0:T(8,128)(2,1)S(1)}, u32[]{:S(2)}, u32[]{:S(2)}) collective-permute-start(bf16[64,1536]{1,0:T(8,128)(2,1)S(1)} %pad_maximum_fusion.2.refs_3_), channel_id=1, source_target_pairs={{0,8},{2,10},{4,12},{6,14},{8,0},{10,2},{12,4},{14,6},{16,24},{18,... | collective-permute-start | bytes 589832 | tf_op jit(solution)/shard_map/in_z1/ppermute | solution.py:35
  6.9 10.3 %collective-permute-start.1 = (bf16[64,2560]{1,0:T(8,128)(2,1)S(1)}, bf16[64,2560]{1,0:T(8,128)(2,1)S(1)}, u32[]{:S(2)}, u32[]{:S(2)}) collective-permute-start(bf16[64,2560]{1,0:T(8,128)(2,1)S(1)} %pad_maximum_fusion), channel_id=1, source_target_pairs={{0,4},{2,6},{4,0},{6,2},{8,12},{10,14},{12,8},{14,10},{16,20},{18,... | collective-permute-start | bytes 983048 | tf_op jit(solution)/shard_map/in_x/ppermute | solution.py:35
  8.5 20.4 %collective-permute-start = (bf16[400,1024]{1,0:T(8,128)(2,1)S(1)}, bf16[400,1024]{1,0:T(8,128)(2,1)S(1)}, u32[]{:S(2)}, u32[]{:S(2)}) collective-permute-start(bf16[400,1024]{1,0:T(8,128)(2,1)S(1)} %fusion.1), channel_id=1, source_target_pairs={{0,1},{1,0},{2,3},{3,2},{4,5},{5,4},{6,7},{7,6},{8,9},{9,8},{10,11... | collective-permute-start | bytes 2457608 | tf_op jit(solution)/shard_map/tokens/ppermute | solution.py:35
  12.6 7.7 %collective-permute-start.3 = (bf16[64,1536]{1,0:T(8,128)(2,1)S(1)}, bf16[64,1536]{1,0:T(8,128)(2,1)S(1)}, u32[]{:S(2)}, u32[]{:S(2)}) collective-permute-start(bf16[64,1536]{1,0:T(8,128)(2,1)S(1)} %collective-permute-done.2.refs_15_), channel_id=1, source_target_pairs={{0,8},{2,10},{4,12},{6,14},{8,0},{10,2},{12,4},{14,6},{16,24},{18,... | collective-permute-start | bytes 589832 | tf_op jit(solution)/shard_map/in_z2/ppermute | solution.py:35
  15.6 6.1 %collective-permute-start.12 = (bf16[64,1536]{1,0:T(8,128)(2,1)S(1)}, bf16[64,1536]{1,0:T(8,128)(2,1)S(1)}, u32[]{:S(2)}, u32[]{:S(2)}) collective-permute-start(bf16[64,1536]{1,0:T(8,128)(2,1)S(1)} %collective-permute-done.2.refs_15_), channel_id=1, source_target_pairs={{0,4},{2,6},{4,0},{6,2},{8,12},{10,14},{12,8},{14,10},{16,20},{18,... | collective-permute-start | bytes 589832 | tf_op jit(solution)/shard_map/in_z3_x/ppermute | solution.py:35
  17.1 6.4 %collective-permute-start.15 = (bf16[64,1536]{1,0:T(8,128)(2,1)S(1)}, bf16[64,1536]{1,0:T(8,128)(2,1)S(1)}, u32[]{:S(2)}, u32[]{:S(2)}) collective-permute-start(bf16[64,1536]{1,0:T(8,128)(2,1)S(1)} %collective-permute-done.2.refs_15_), channel_id=1, source_target_pairs={{0,2},{2,0},{4,6},{6,4},{8,10},{10,8},{12,14},{14,12},{16,18},{18,... | collective-permute-start | bytes 589832 | tf_op jit(solution)/shard_map/in_core_12/ppermute | solution.py:35
  17.1 6.4 %collective-permute-start.8 = (bf16[64,1536]{1,0:T(8,128)(2,1)S(1)}, bf16[64,1536]{1,0:T(8,128)(2,1)S(1)}, u32[]{:S(2)}, u32[]{:S(2)}) collective-permute-start(bf16[64,1536]{1,0:T(8,128)(2,1)S(1)} %collective-permute-done.7.refs_7_), channel_id=1, source_target_pairs={{0,2},{2,0},{4,6},{6,4},{8,10},{10,8},{12,14},{14,12},{16,18},{18,... | collective-permute-start | bytes 589832 | tf_op jit(solution)/shard_map/in_core_4/ppermute | solution.py:35
  20.2 5.7 %collective-permute-start.9 = (bf16[64,1536]{1,0:T(8,128)(2,1)S(1)}, bf16[64,1536]{1,0:T(8,128)(2,1)S(1)}, u32[]{:S(2)}, u32[]{:S(2)}) collective-permute-start(bf16[64,1536]{1,0:T(8,128)(2,1)S(1)} %collective-permute-done.7.refs_7_), channel_id=1, source_target_pairs={{0,4},{2,6},{4,0},{6,2},{8,12},{10,14},{12,8},{14,10},{16,20},{18,... | collective-permute-start | bytes 589832 | tf_op jit(solution)/shard_map/in_z1_x/ppermute | solution.py:35
  21.8 9.2 %collective-permute-start.4 = (bf16[128,1024]{1,0:T(8,128)(2,1)S(1)}, bf16[128,1024]{1,0:T(8,128)(2,1)S(1)}, u32[]{:S(2)}, u32[]{:S(2)}) collective-permute-start(bf16[128,1024]{1,0:T(8,128)(2,1)S(1)} %pad_maximum_fusion.1.refs_2_), channel_id=1, source_target_pairs={{0,8},{2,10},{4,12},{6,14},{8,0},{10,2},{12,4},{14,6},{16,24},{18,... | collective-permute-start | bytes 786440 | tf_op jit(solution)/shard_map/out_z1/ppermute | solution.py:35
  23.5 6.8 %collective-permute-start.11 = (bf16[64,1536]{1,0:T(8,128)(2,1)S(1)}, bf16[64,1536]{1,0:T(8,128)(2,1)S(1)}, u32[]{:S(2)}, u32[]{:S(2)}) collective-permute-start(bf16[64,1536]{1,0:T(8,128)(2,1)S(1)} %collective-permute-done.3.refs_11_), channel_id=1, source_target_pairs={{0,2},{2,0},{4,6},{6,4},{8,10},{10,8},{12,14},{14,12},{16,18},{18,... | collective-permute-start | bytes 589832 | tf_op jit(solution)/shard_map/in_core_8/ppermute | solution.py:35
  23.5 7.3 %collective-permute-start.13 = (bf16[64,1536]{1,0:T(8,128)(2,1)S(1)}, bf16[64,1536]{1,0:T(8,128)(2,1)S(1)}, u32[]{:S(2)}, u32[]{:S(2)}) collective-permute-start(bf16[64,1536]{1,0:T(8,128)(2,1)S(1)} %collective-permute-done.3.refs_11_), channel_id=1, source_target_pairs={{0,4},{2,6},{4,0},{6,2},{8,12},{10,14},{12,8},{14,10},{16,20},{18,... | collective-permute-start | bytes 589832 | tf_op jit(solution)/shard_map/in_z2_x/ppermute | solution.py:35
  25.9 5.9 %collective-permute-start.6 = (bf16[64,2560]{1,0:T(8,128)(2,1)S(1)}, bf16[64,2560]{1,0:T(8,128)(2,1)S(1)}, u32[]{:S(2)}, u32[]{:S(2)}) collective-permute-start(bf16[64,2560]{1,0:T(8,128)(2,1)S(1)} %collective-permute-done.1.refs_5_), channel_id=1, source_target_pairs={{0,2},{2,0},{4,6},{6,4},{8,10},{10,8},{12,14},{14,12},{16,18},{18,... | collective-permute-start | bytes 983048 | tf_op jit(solution)/shard_map/in_core_2/ppermute | solution.py:35
  28.9 9.8 %collective-permute-start.20 = (bf16[128,1024]{1,0:T(8,128)(2,1)S(1)}, bf16[128,1024]{1,0:T(8,128)(2,1)S(1)}, u32[]{:S(2)}, u32[]{:S(2)}) collective-permute-start(bf16[128,1024]{1,0:T(8,128)(2,1)S(1)} %pad_maximum_fusion.1.refs_2_), channel_id=1, source_target_pairs={{0,24},{2,26},{4,28},{6,30},{8,16},{10,18},{12,20},{14,22},{16,8},... | collective-permute-start | bytes 786440 | tf_op jit(solution)/shard_map/out_z3/ppermute | solution.py:35
  30.4 1.5 %collective-permute-start.16 = (bf16[64,1536]{1,0:T(8,128)(2,1)S(1)}, bf16[64,1536]{1,0:T(8,128)(2,1)S(1)}, u32[]{:S(2)}, u32[]{:S(2)}) collective-permute-start(bf16[64,1536]{1,0:T(8,128)(2,1)S(1)} %collective-permute-done.12.refs_17_), channel_id=1, source_target_pairs={{0,2},{2,0},{4,6},{6,4},{8,10},{10,8},{12,14},{14,12},{16,18},{18,... | collective-permute-start | bytes 589832 | tf_op jit(solution)/shard_map/in_core_14/ppermute | solution.py:35
  30.8 1.4 %collective-permute-start.14 = (bf16[64,1536]{1,0:T(8,128)(2,1)S(1)}, bf16[64,1536]{1,0:T(8,128)(2,1)S(1)}, u32[]{:S(2)}, u32[]{:S(2)}) collective-permute-start(bf16[64,1536]{1,0:T(8,128)(2,1)S(1)} %collective-permute-done.13.refs_13_), channel_id=1, source_target_pairs={{0,2},{2,0},{4,6},{6,4},{8,10},{10,8},{12,14},{14,12},{16,18},{18,... | collective-permute-start | bytes 589832 | tf_op jit(solution)/shard_map/in_core_10/ppermute | solution.py:35
  31.0 1.6 %collective-permute-start.10 = (bf16[64,1536]{1,0:T(8,128)(2,1)S(1)}, bf16[64,1536]{1,0:T(8,128)(2,1)S(1)}, u32[]{:S(2)}, u32[]{:S(2)}) collective-permute-start(bf16[64,1536]{1,0:T(8,128)(2,1)S(1)} %collective-permute-done.9.refs_9_), channel_id=1, source_target_pairs={{0,2},{2,0},{4,6},{6,4},{8,10},{10,8},{12,14},{14,12},{16,18},{18,... | collective-permute-start | bytes 589832 | tf_op jit(solution)/shard_map/in_core_6/ppermute | solution.py:35
  37.2 11.9 %collective-permute-start.17 = (bf16[384,512]{1,0:T(8,128)(2,1)S(1)}, bf16[384,512]{1,0:T(8,128)(2,1)S(1)}, u32[]{:S(2)}, u32[]{:S(2)}) collective-permute-start(bf16[384,512]{1,0:T(8,128)(2,1)S(1)} %get-tuple-element.28), channel_id=1, source_target_pairs={{0,1},{1,0},{2,3},{3,2},{4,5},{5,4},{6,7},{7,6},{8,9},{9,8},{10,11... | collective-permute-start | bytes 1179656 | tf_op jit(solution)/shard_map/context/ppermute | solution.py:35
  38.8 10.3 %collective-permute-start.22 = (bf16[128,1024]{1,0:T(8,128)(2,1)S(1)}, bf16[128,1024]{1,0:T(8,128)(2,1)S(1)}, u32[]{:S(2)}, u32[]{:S(2)}) collective-permute-start(bf16[128,1024]{1,0:T(8,128)(2,1)S(1)} %collective-permute-done.20.refs_6_), channel_id=1, source_target_pairs={{0,8},{2,10},{4,12},{6,14},{8,0},{10,2},{12,4},{14,6},{16,24},{18,... | collective-permute-start | bytes 786440 | tf_op jit(solution)/shard_map/out_z2/ppermute | solution.py:35
  45.3 3.8 %collective-permute-start.18 = (bf16[128,1024]{1,0:T(8,128)(2,1)S(1)}, bf16[128,1024]{1,0:T(8,128)(2,1)S(1)}, u32[]{:S(2)}, u32[]{:S(2)}) collective-permute-start(bf16[128,1024]{1,0:T(8,128)(2,1)S(1)} %pad_maximum_fusion.1.refs_2_), channel_id=1, source_target_pairs={{0,2},{2,0},{4,6},{6,4},{8,10},{10,8},{12,14},{14,12},{16,18},{18,... | collective-permute-start | bytes 786440 | tf_op jit(solution)/shard_map/out_core_0/ppermute | solution.py:35
  45.4 3.7 %collective-permute-start.19 = (bf16[128,1024]{1,0:T(8,128)(2,1)S(1)}, bf16[128,1024]{1,0:T(8,128)(2,1)S(1)}, u32[]{:S(2)}, u32[]{:S(2)}) collective-permute-start(bf16[128,1024]{1,0:T(8,128)(2,1)S(1)} %collective-permute-done.4.refs_4_), channel_id=1, source_target_pairs={{0,2},{2,0},{4,6},{6,4},{8,10},{10,8},{12,14},{14,12},{16,18},{18,... | collective-permute-start | bytes 786440 | tf_op jit(solution)/shard_map/out_core_4/ppermute | solution.py:35
  45.9 3.2 %collective-permute-start.21 = (bf16[128,1024]{1,0:T(8,128)(2,1)S(1)}, bf16[128,1024]{1,0:T(8,128)(2,1)S(1)}, u32[]{:S(2)}, u32[]{:S(2)}) collective-permute-start(bf16[128,1024]{1,0:T(8,128)(2,1)S(1)} %collective-permute-done.20.refs_6_), channel_id=1, source_target_pairs={{0,2},{2,0},{4,6},{6,4},{8,10},{10,8},{12,14},{14,12},{16,18},{18,... | collective-permute-start | bytes 786440 | tf_op jit(solution)/shard_map/out_core_12/ppermute | solution.py:35
  49.1 1.5 %collective-permute-start.23 = (bf16[128,1024]{1,0:T(8,128)(2,1)S(1)}, bf16[128,1024]{1,0:T(8,128)(2,1)S(1)}, u32[]{:S(2)}, u32[]{:S(2)}) collective-permute-start(bf16[128,1024]{1,0:T(8,128)(2,1)S(1)} %collective-permute-done.22.refs_8_), channel_id=1, source_target_pairs={{0,2},{2,0},{4,6},{6,4},{8,10},{10,8},{12,14},{14,12},{16,18},{18,... | collective-permute-start | bytes 786440 | tf_op jit(solution)/shard_map/out_core_8/ppermute | solution.py:35
  (7 other events, 61.2 us)

commit v8 on v7

--- a/solution.py
+++ b/solution.py
@@ -242,19 +242,19 @@
     whole = pltpu.make_async_copy(context, context_ref, done.at[0])
     whole.start()
     gather_rows(list(zip(slots, pieces)), weight)
-    half = context.shape[0] // 2
+    half = D // 2
     copies = []
     for turn in range(2):
-        rows = pl.ds(turn * half, half)
-        for first in range(0, D, STEP):
+        for first in range(turn * half, (turn + 1) * half, STEP):
             lanes = pl.ds(first, STEP)
             found = jnp.dot(
-                context[rows, :], weight[:, lanes], preferred_element_type=jnp.float32
+                context[...], weight[:, lanes], preferred_element_type=jnp.float32
             )
-            found = sheet_ref[rows, lanes].astype(jnp.float32) + found + bias_ref[:, lanes]
-            updated[rows, lanes] = found.astype(jnp.bfloat16)
+            found = sheet_ref[:, lanes].astype(jnp.float32) + found + bias_ref[:, lanes]
+            updated[:, lanes] = found.astype(jnp.bfloat16)
+        part = pl.ds(turn * half, half)
         copies.append(
-            pltpu.make_async_copy(updated.at[rows, :], updated_ref.at[rows, :], done.at[turn + 1])
+            pltpu.make_async_copy(updated.at[:, part], updated_ref.at[:, part], done.at[turn + 1])
         )
         copies[-1].start()
     for copy in (whole, *copies):

time: 52.7 us -> 52.9 us (level)
  waiting for transfers between devices: 14.9 us -> 14.1 us
  Pallas kernels: 9.85 us -> 10.6 us
    ppermute x24, waiting for transfers between devices: 14.9 us -> 14.1 us  [swap(): return lax.ppermute(block, axis, [(i, i ^ distance) for i in range(size)])]
    pallas_call x1, Pallas kernels: 1.67 us -> 2.48 us  [on_device(): call(functools.partial(own_kernel, strips), strip_out, [SMEM] + [VMEM] *...]
  transfers between devices with their start and end apart: 24 -> 24, of which waited for: 10 -> 10; matrix products, arithmetic and copies ran while one was open for 0% -> 0% of each run, Pallas kernels for 15% -> 16%
where the time goes in v8:
time: 52.9 us
  starting transfers between devices  26.2 us (50%)
  waiting for transfers between devices  14.1 us (27%)
  Pallas kernels  10.6 us (20%)
  local copies, waits for them, and re-layouts  1.05 us (2%)
  between operations  0.83 us (2%)
    ppermute x24, starting transfers between devices, swap(): return lax.ppermute(block, axis, [(i, i ^ distance) for i in range(size)])  26.2 us
    ppermute x24, waiting for transfers between devices, swap(): return lax.ppermute(block, axis, [(i, i ^ distance) for i in range(size)])  14.1 us
    pallas_call x1, Pallas kernels, on_device(): call(functools.partial(project_kernel, strips, len(normed), [[slot] for s...  4.61 us
    pallas_call x1, Pallas kernels, on_device(): call(functools.partial(own_kernel, strips), strip_out, [SMEM] + [VMEM] *...  2.48 us
    pallas_call x1, Pallas kernels, on_device(): call(functools.partial(output_kernel, strips, out_slots), [jax.ShapeDtype...  1.95 us
    pallas_call x2, Pallas kernels, norm(): call(norm_kernel, jax.ShapeDtypeStruct((length, features), jnp.bfloat16),...  1.6 us
  transfers between devices with their start and end apart: 24, of which 10 were waited for; matrix products, arithmetic and copies ran while one was open for 0% of the time, Pallas kernels for 16%

profile of v8, /device:TPU:0, one launch (start us, length us, event | category | flops | bytes accessed | tf_op | source)
XLA Modules:
  0.0 52.9 jit_solution(10826932681983167232)
XLA Ops:
  0.7 1.0 %constant_dynamic-slice_fusion.2 = (bf16[64,512]{1,0:T(8,128)(2,1)S(1)}, bf16[64,512]{1,0:T(8,128)(2,1)S(1)}, bf16[64,512]{1,0:T(8,128)(2,1)S(1)}) fusion(bf16[64,3072]{1,0:T(8,128)(2,1)} %param.12, s32[]{:T(128)S(6)} %select_n.9, s32[]{:T(128)S(6)} %select_n.11, s32[]{:T(128)S(6)} %select_n.10), kind=kLoop, calls=%fused_computation.10 | loop fusion | bytes 393228 | tf_op jit(solution)/shard_map/dynamic_slice | solution.py:282
  1.7 5.1 %collective-permute-start.2 = (bf16[64,1536]{1,0:T(8,128)(2,1)S(1)}, bf16[64,1536]{1,0:T(8,128)(2,1)S(1)}, u32[]{:S(2)}, u32[]{:S(2)}) collective-permute-start(bf16[64,1536]{1,0:T(8,128)(2,1)S(1)} %pad_maximum_fusion.2.refs_3_), channel_id=1, source_target_pairs={{0,24},{2,26},{4,28},{6,30},{8,16},{10,18},{12,20},{14,22},{16,8},... | collective-permute-start | bytes 589832 | tf_op jit(solution)/shard_map/in_z3/ppermute | solution.py:35
  6.9 1.6 %collective-permute-start.1 = (bf16[64,2560]{1,0:T(8,128)(2,1)S(1)}, bf16[64,2560]{1,0:T(8,128)(2,1)S(1)}, u32[]{:S(2)}, u32[]{:S(2)}) collective-permute-start(bf16[64,2560]{1,0:T(8,128)(2,1)S(1)} %pad_maximum_fusion), channel_id=1, source_target_pairs={{0,4},{2,6},{4,0},{6,2},{8,12},{10,14},{12,8},{14,10},{16,20},{18,... | collective-permute-start | bytes 983048 | tf_op jit(solution)/shard_map/in_x/ppermute | solution.py:35
  8.5 1.6 %collective-permute-start = (bf16[400,1024]{1,0:T(8,128)(2,1)S(1)}, bf16[400,1024]{1,0:T(8,128)(2,1)S(1)}, u32[]{:S(2)}, u32[]{:S(2)}) collective-permute-start(bf16[400,1024]{1,0:T(8,128)(2,1)S(1)} %fusion.1), channel_id=1, source_target_pairs={{0,1},{1,0},{2,3},{3,2},{4,5},{5,4},{6,7},{7,6},{8,9},{9,8},{10,11... | collective-permute-start | bytes 2457608 | tf_op jit(solution)/shard_map/tokens/ppermute | solution.py:35
  10.1 2.5 %collective-permute-done.2.refs_15_ = bf16[64,1536]{1,0:T(8,128)(2,1)S(1)} collective-permute-done((bf16[64,1536]{1,0:T(8,128)(2,1)S(1)}, bf16[64,1536]{1,0:T(8,128)(2,1)S(1)}, u32[]{:S(2)}, u32[]{:S(2)}) %collective-permute-start.2) | collective-permute-done | bytes 196640 | tf_op jit(solution)/shard_map/in_z3/ppermute | solution.py:35
  12.6 3.1 %collective-permute-start.3 = (bf16[64,1536]{1,0:T(8,128)(2,1)S(1)}, bf16[64,1536]{1,0:T(8,128)(2,1)S(1)}, u32[]{:S(2)}, u32[]{:S(2)}) collective-permute-start(bf16[64,1536]{1,0:T(8,128)(2,1)S(1)} %collective-permute-done.2.refs_15_), channel_id=1, source_target_pairs={{0,8},{2,10},{4,12},{6,14},{8,0},{10,2},{12,4},{14,6},{16,24},{18,... | collective-permute-start | bytes 589832 | tf_op jit(solution)/shard_map/in_z2/ppermute | solution.py:35
  15.6 1.5 %collective-permute-start.12 = (bf16[64,1536]{1,0:T(8,128)(2,1)S(1)}, bf16[64,1536]{1,0:T(8,128)(2,1)S(1)}, u32[]{:S(2)}, u32[]{:S(2)}) collective-permute-start(bf16[64,1536]{1,0:T(8,128)(2,1)S(1)} %collective-permute-done.2.refs_15_), channel_id=1, source_target_pairs={{0,4},{2,6},{4,0},{6,2},{8,12},{10,14},{12,8},{14,10},{16,20},{18,... | collective-permute-start | bytes 589832 | tf_op jit(solution)/shard_map/in_z3_x/ppermute | solution.py:35
  17.7 0.8 %norm.2.refs_1_ = bf16[384,1024]{1,0:T(8,128)(2,1)S(1)} custom-call(bf16[384,1024]{1,0:T(8,128)(2,1)S(1)} %bitcast.12, f32[1,1024]{1,0:T(1,128)S(1)} %bitcast.15, f32[1,1024]{1,0:T(1,128)S(1)} %bitcast.17), custom_call_target="tpu_custom_call" | custom-call | flops 99999997952 | tf_op jit(solution)/shard_map/norm/pallas_call | solution.py:295
  18.5 1.8 %collective-permute-done.3.refs_11_ = bf16[64,1536]{1,0:T(8,128)(2,1)S(1)} collective-permute-done((bf16[64,1536]{1,0:T(8,128)(2,1)S(1)}, bf16[64,1536]{1,0:T(8,128)(2,1)S(1)}, u32[]{:S(2)}, u32[]{:S(2)}) %collective-permute-start.3) | collective-permute-done | bytes 196640 | tf_op jit(solution)/shard_map/in_z2/ppermute | solution.py:35
  20.2 1.5 %collective-permute-start.9 = (bf16[64,1536]{1,0:T(8,128)(2,1)S(1)}, bf16[64,1536]{1,0:T(8,128)(2,1)S(1)}, u32[]{:S(2)}, u32[]{:S(2)}) collective-permute-start(bf16[64,1536]{1,0:T(8,128)(2,1)S(1)} %collective-permute-done.7.refs_7_), channel_id=1, source_target_pairs={{0,4},{2,6},{4,0},{6,2},{8,12},{10,14},{12,8},{14,10},{16,20},{18,... | collective-permute-start | bytes 589832 | tf_op jit(solution)/shard_map/in_z1_x/ppermute | solution.py:35
  21.8 1.8 %collective-permute-start.4 = (bf16[128,1024]{1,0:T(8,128)(2,1)S(1)}, bf16[128,1024]{1,0:T(8,128)(2,1)S(1)}, u32[]{:S(2)}, u32[]{:S(2)}) collective-permute-start(bf16[128,1024]{1,0:T(8,128)(2,1)S(1)} %pad_maximum_fusion.1.refs_2_), channel_id=1, source_target_pairs={{0,8},{2,10},{4,12},{6,14},{8,0},{10,2},{12,4},{14,6},{16,24},{18,... | collective-permute-start | bytes 786440 | tf_op jit(solution)/shard_map/out_z1/ppermute | solution.py:35
  23.5 1.0 %collective-permute-start.13 = (bf16[64,1536]{1,0:T(8,128)(2,1)S(1)}, bf16[64,1536]{1,0:T(8,128)(2,1)S(1)}, u32[]{:S(2)}, u32[]{:S(2)}) collective-permute-start(bf16[64,1536]{1,0:T(8,128)(2,1)S(1)} %collective-permute-done.3.refs_11_), channel_id=1, source_target_pairs={{0,4},{2,6},{4,0},{6,2},{8,12},{10,14},{12,8},{14,10},{16,20},{18,... | collective-permute-start | bytes 589832 | tf_op jit(solution)/shard_map/in_z2_x/ppermute | solution.py:35
  24.6 1.4 %collective-permute-done.9.refs_9_ = bf16[64,1536]{1,0:T(8,128)(2,1)S(1)} collective-permute-done((bf16[64,1536]{1,0:T(8,128)(2,1)S(1)}, bf16[64,1536]{1,0:T(8,128)(2,1)S(1)}, u32[]{:S(2)}, u32[]{:S(2)}) %collective-permute-start.9) | collective-permute-done | bytes 196640 | tf_op jit(solution)/shard_map/in_z1_x/ppermute | solution.py:35
  25.9 3.0 %collective-permute-done.sheet_ref = bf16[400,1024]{1,0:T(8,128)(2,1)S(1)} collective-permute-done((bf16[400,1024]{1,0:T(8,128)(2,1)S(1)}, bf16[400,1024]{1,0:T(8,128)(2,1)S(1)}, u32[]{:S(2)}, u32[]{:S(2)}) %collective-permute-start) | collective-permute-done | bytes 819232 | tf_op jit(solution)/shard_map/tokens/ppermute | solution.py:35
  28.9 0.6 %collective-permute-start.20 = (bf16[128,1024]{1,0:T(8,128)(2,1)S(1)}, bf16[128,1024]{1,0:T(8,128)(2,1)S(1)}, u32[]{:S(2)}, u32[]{:S(2)}) collective-permute-start(bf16[128,1024]{1,0:T(8,128)(2,1)S(1)} %pad_maximum_fusion.1.refs_2_), channel_id=1, source_target_pairs={{0,24},{2,26},{4,28},{6,30},{8,16},{10,18},{12,20},{14,22},{16,8},... | collective-permute-start | bytes 786440 | tf_op jit(solution)/shard_map/out_z3/ppermute | solution.py:35
  29.6 0.8 %norm.3.refs_2_ = bf16[384,1024]{1,0:T(8,128)(2,1)S(1)} custom-call(bf16[400,1024]{1,0:T(8,128)(2,1)S(1)} %collective-permute-done.sheet_ref, f32[1,1024]{1,0:T(1,128)S(1)} %bitcast.16, f32[1,1024]{1,0:T(1,128)S(1)} %bitcast.18), custom_call_target="tpu_custom_call" | custom-call | tf_op jit(solution)/shard_map/norm/pallas_call | solution.py:295
  31.4 0.5 collective-permute-done.16.refs_18_
  32.6 4.6 %project.1 = (bf16[384,512]{1,0:T(8,128)(2,1)S(1)}, bf16[384,512]{1,0:T(8,128)(2,1)S(1)}, bf16[768,512]{1,0:T(8,128)(2,1)S(1)}, bf16[4,144,768]{2,1,0:T(8,128)(2,1)S(1)}) custom-call(s32[3,6]{1,0:T(4,128)S(1)} %slice_convert_fusion.refs_0_, bf16[384,1024]{1,0:T(8,128)(2,1)S(1)} %norm.2.refs_1_, bf16[384,1024]{1,0:T(8,128)(2,1)S(1)} %norm.3.refs_2_, ...), custom_call_target="tpu_custom_call" | custom-call | tf_op jit(solution)/shard_map/project/pallas_call | solution.py:344
  37.2 2.4 %collective-permute-start.17 = (bf16[384,512]{1,0:T(8,128)(2,1)S(1)}, bf16[384,512]{1,0:T(8,128)(2,1)S(1)}, u32[]{:S(2)}, u32[]{:S(2)}) collective-permute-start(bf16[384,512]{1,0:T(8,128)(2,1)S(1)} %get-tuple-element.28), channel_id=1, source_target_pairs={{0,1},{1,0},{2,3},{3,2},{4,5},{5,4},{6,7},{7,6},{8,9},{9,8},{10,11... | collective-permute-start | bytes 1179656 | tf_op jit(solution)/shard_map/context/ppermute | solution.py:35
  39.6 4.0 %collective-permute-start.22 = (bf16[128,1024]{1,0:T(8,128)(2,1)S(1)}, bf16[128,1024]{1,0:T(8,128)(2,1)S(1)}, u32[]{:S(2)}, u32[]{:S(2)}) collective-permute-start(bf16[128,1024]{1,0:T(8,128)(2,1)S(1)} %collective-permute-done.20.refs_6_), channel_id=1, source_target_pairs={{0,8},{2,10},{4,12},{6,14},{8,0},{10,2},{12,4},{14,6},{16,24},{18,... | collective-permute-start | bytes 786440 | tf_op jit(solution)/shard_map/out_z2/ppermute | solution.py:35
  43.6 2.5 %own_strip.1.refs_0_ = bf16[384,512]{1,0:T(8,128)(2,1)S(1)} custom-call(s32[3,6]{1,0:T(4,128)S(1)} %get-tuple-element.40.mask_ref, bf16[384,512]{1,0:T(8,128)(2,1)S(1)} %get-tuple-element.25.query_ref, bf16[768,512]{1,0:T(8,128)(2,1)S(1)} %get-tuple-element.26.key_ref, bf16[4,144,768]{2,1,0:T(8,128)(2,1)S(1)} %get-tuple-element.27.value_ref), custom_call_target="tpu_custom_call" | custom-call | flops 99999997952 | tf_op jit(solution)/shard_map/own_strip/pallas_call | solution.py:368
  47.1 2.3 %collective-permute-done.22.refs_8_ = bf16[128,1024]{1,0:T(8,128)(2,1)S(1)} collective-permute-done((bf16[128,1024]{1,0:T(8,128)(2,1)S(1)}, bf16[128,1024]{1,0:T(8,128)(2,1)S(1)}, u32[]{:S(2)}, u32[]{:S(2)}) %collective-permute-start.22) | collective-permute-done | bytes 262176 | tf_op jit(solution)/shard_map/out_z2/ppermute | solution.py:35
  49.4 1.5 %collective-permute-done.23.refs_9_ = bf16[128,1024]{1,0:T(8,128)(2,1)S(1)} collective-permute-done((bf16[128,1024]{1,0:T(8,128)(2,1)S(1)}, bf16[128,1024]{1,0:T(8,128)(2,1)S(1)}, u32[]{:S(2)}, u32[]{:S(2)}) %collective-permute-start.23) | collective-permute-done | bytes 262176 | tf_op jit(solution)/shard_map/out_core_8/ppermute | solution.py:35
  50.9 1.9 %output.1 = (bf16[384,1024]{1,0:T(8,128)(2,1)}, bf16[384,1024]{1,0:T(8,128)(2,1)}) custom-call(bf16[384,512]{1,0:T(8,128)(2,1)S(1)} %own_strip.1.refs_0_, bf16[384,512]{1,0:T(8,128)(2,1)S(1)} %collective-permute-done.17.refs_1_, bf16[128,1024]{1,0:T(8,128)(2,1)S(1)} %pad_maximum_fusion.1.refs_2_, bf16[128,1024]{1,0:T(8,128)(2,1)S(1)} %collective-permute-done.18.refs_3_, ...), custom_call_target="tpu_custom_call" | custom-call | flops 805306368 | bytes 2097152 | tf_op jit(solution)/shard_map/output/pallas_call | solution.py:385
  (51 shorter events, 3.4 us)
Async XLA Ops:
  1.7 10.9 %collective-permute-start.2 = (bf16[64,1536]{1,0:T(8,128)(2,1)S(1)}, bf16[64,1536]{1,0:T(8,128)(2,1)S(1)}, u32[]{:S(2)}, u32[]{:S(2)}) collective-permute-start(bf16[64,1536]{1,0:T(8,128)(2,1)S(1)} %pad_maximum_fusion.2.refs_3_), channel_id=1, source_target_pairs={{0,24},{2,26},{4,28},{6,30},{8,16},{10,18},{12,20},{14,22},{16,8},... | collective-permute-start | bytes 589832 | tf_op jit(solution)/shard_map/in_z3/ppermute | solution.py:35
  6.8 8.8 %collective-permute-start.5 = (bf16[64,1536]{1,0:T(8,128)(2,1)S(1)}, bf16[64,1536]{1,0:T(8,128)(2,1)S(1)}, u32[]{:S(2)}, u32[]{:S(2)}) collective-permute-start(bf16[64,1536]{1,0:T(8,128)(2,1)S(1)} %pad_maximum_fusion.2.refs_3_), channel_id=1, source_target_pairs={{0,2},{2,0},{4,6},{6,4},{8,10},{10,8},{12,14},{14,12},{16,18},{18,... | collective-permute-start | bytes 589832 | tf_op jit(solution)/shard_map/in_core_0/ppermute | solution.py:35
  6.8 10.3 %collective-permute-start.7 = (bf16[64,1536]{1,0:T(8,128)(2,1)S(1)}, bf16[64,1536]{1,0:T(8,128)(2,1)S(1)}, u32[]{:S(2)}, u32[]{:S(2)}) collective-permute-start(bf16[64,1536]{1,0:T(8,128)(2,1)S(1)} %pad_maximum_fusion.2.refs_3_), channel_id=1, source_target_pairs={{0,8},{2,10},{4,12},{6,14},{8,0},{10,2},{12,4},{14,6},{16,24},{18,... | collective-permute-start | bytes 589832 | tf_op jit(solution)/shard_map/in_z1/ppermute | solution.py:35
  6.9 10.3 %collective-permute-start.1 = (bf16[64,2560]{1,0:T(8,128)(2,1)S(1)}, bf16[64,2560]{1,0:T(8,128)(2,1)S(1)}, u32[]{:S(2)}, u32[]{:S(2)}) collective-permute-start(bf16[64,2560]{1,0:T(8,128)(2,1)S(1)} %pad_maximum_fusion), channel_id=1, source_target_pairs={{0,4},{2,6},{4,0},{6,2},{8,12},{10,14},{12,8},{14,10},{16,20},{18,... | collective-permute-start | bytes 983048 | tf_op jit(solution)/shard_map/in_x/ppermute | solution.py:35
  8.5 20.4 %collective-permute-start = (bf16[400,1024]{1,0:T(8,128)(2,1)S(1)}, bf16[400,1024]{1,0:T(8,128)(2,1)S(1)}, u32[]{:S(2)}, u32[]{:S(2)}) collective-permute-start(bf16[400,1024]{1,0:T(8,128)(2,1)S(1)} %fusion.1), channel_id=1, source_target_pairs={{0,1},{1,0},{2,3},{3,2},{4,5},{5,4},{6,7},{7,6},{8,9},{9,8},{10,11... | collective-permute-start | bytes 2457608 | tf_op jit(solution)/shard_map/tokens/ppermute | solution.py:35
  12.6 7.7 %collective-permute-start.3 = (bf16[64,1536]{1,0:T(8,128)(2,1)S(1)}, bf16[64,1536]{1,0:T(8,128)(2,1)S(1)}, u32[]{:S(2)}, u32[]{:S(2)}) collective-permute-start(bf16[64,1536]{1,0:T(8,128)(2,1)S(1)} %collective-permute-done.2.refs_15_), channel_id=1, source_target_pairs={{0,8},{2,10},{4,12},{6,14},{8,0},{10,2},{12,4},{14,6},{16,24},{18,... | collective-permute-start | bytes 589832 | tf_op jit(solution)/shard_map/in_z2/ppermute | solution.py:35
  15.6 6.1 %collective-permute-start.12 = (bf16[64,1536]{1,0:T(8,128)(2,1)S(1)}, bf16[64,1536]{1,0:T(8,128)(2,1)S(1)}, u32[]{:S(2)}, u32[]{:S(2)}) collective-permute-start(bf16[64,1536]{1,0:T(8,128)(2,1)S(1)} %collective-permute-done.2.refs_15_), channel_id=1, source_target_pairs={{0,4},{2,6},{4,0},{6,2},{8,12},{10,14},{12,8},{14,10},{16,20},{18,... | collective-permute-start | bytes 589832 | tf_op jit(solution)/shard_map/in_z3_x/ppermute | solution.py:35
  17.1 6.4 %collective-permute-start.15 = (bf16[64,1536]{1,0:T(8,128)(2,1)S(1)}, bf16[64,1536]{1,0:T(8,128)(2,1)S(1)}, u32[]{:S(2)}, u32[]{:S(2)}) collective-permute-start(bf16[64,1536]{1,0:T(8,128)(2,1)S(1)} %collective-permute-done.2.refs_15_), channel_id=1, source_target_pairs={{0,2},{2,0},{4,6},{6,4},{8,10},{10,8},{12,14},{14,12},{16,18},{18,... | collective-permute-start | bytes 589832 | tf_op jit(solution)/shard_map/in_core_12/ppermute | solution.py:35
  17.1 6.4 %collective-permute-start.8 = (bf16[64,1536]{1,0:T(8,128)(2,1)S(1)}, bf16[64,1536]{1,0:T(8,128)(2,1)S(1)}, u32[]{:S(2)}, u32[]{:S(2)}) collective-permute-start(bf16[64,1536]{1,0:T(8,128)(2,1)S(1)} %collective-permute-done.7.refs_7_), channel_id=1, source_target_pairs={{0,2},{2,0},{4,6},{6,4},{8,10},{10,8},{12,14},{14,12},{16,18},{18,... | collective-permute-start | bytes 589832 | tf_op jit(solution)/shard_map/in_core_4/ppermute | solution.py:35
  20.2 5.7 %collective-permute-start.9 = (bf16[64,1536]{1,0:T(8,128)(2,1)S(1)}, bf16[64,1536]{1,0:T(8,128)(2,1)S(1)}, u32[]{:S(2)}, u32[]{:S(2)}) collective-permute-start(bf16[64,1536]{1,0:T(8,128)(2,1)S(1)} %collective-permute-done.7.refs_7_), channel_id=1, source_target_pairs={{0,4},{2,6},{4,0},{6,2},{8,12},{10,14},{12,8},{14,10},{16,20},{18,... | collective-permute-start | bytes 589832 | tf_op jit(solution)/shard_map/in_z1_x/ppermute | solution.py:35
  21.8 9.2 %collective-permute-start.4 = (bf16[128,1024]{1,0:T(8,128)(2,1)S(1)}, bf16[128,1024]{1,0:T(8,128)(2,1)S(1)}, u32[]{:S(2)}, u32[]{:S(2)}) collective-permute-start(bf16[128,1024]{1,0:T(8,128)(2,1)S(1)} %pad_maximum_fusion.1.refs_2_), channel_id=1, source_target_pairs={{0,8},{2,10},{4,12},{6,14},{8,0},{10,2},{12,4},{14,6},{16,24},{18,... | collective-permute-start | bytes 786440 | tf_op jit(solution)/shard_map/out_z1/ppermute | solution.py:35
  23.5 6.8 %collective-permute-start.11 = (bf16[64,1536]{1,0:T(8,128)(2,1)S(1)}, bf16[64,1536]{1,0:T(8,128)(2,1)S(1)}, u32[]{:S(2)}, u32[]{:S(2)}) collective-permute-start(bf16[64,1536]{1,0:T(8,128)(2,1)S(1)} %collective-permute-done.3.refs_11_), channel_id=1, source_target_pairs={{0,2},{2,0},{4,6},{6,4},{8,10},{10,8},{12,14},{14,12},{16,18},{18,... | collective-permute-start | bytes 589832 | tf_op jit(solution)/shard_map/in_core_8/ppermute | solution.py:35
  23.5 7.3 %collective-permute-start.13 = (bf16[64,1536]{1,0:T(8,128)(2,1)S(1)}, bf16[64,1536]{1,0:T(8,128)(2,1)S(1)}, u32[]{:S(2)}, u32[]{:S(2)}) collective-permute-start(bf16[64,1536]{1,0:T(8,128)(2,1)S(1)} %collective-permute-done.3.refs_11_), channel_id=1, source_target_pairs={{0,4},{2,6},{4,0},{6,2},{8,12},{10,14},{12,8},{14,10},{16,20},{18,... | collective-permute-start | bytes 589832 | tf_op jit(solution)/shard_map/in_z2_x/ppermute | solution.py:35
  25.9 5.9 %collective-permute-start.6 = (bf16[64,2560]{1,0:T(8,128)(2,1)S(1)}, bf16[64,2560]{1,0:T(8,128)(2,1)S(1)}, u32[]{:S(2)}, u32[]{:S(2)}) collective-permute-start(bf16[64,2560]{1,0:T(8,128)(2,1)S(1)} %collective-permute-done.1.refs_5_), channel_id=1, source_target_pairs={{0,2},{2,0},{4,6},{6,4},{8,10},{10,8},{12,14},{14,12},{16,18},{18,... | collective-permute-start | bytes 983048 | tf_op jit(solution)/shard_map/in_core_2/ppermute | solution.py:35
  28.9 10.6 %collective-permute-start.20 = (bf16[128,1024]{1,0:T(8,128)(2,1)S(1)}, bf16[128,1024]{1,0:T(8,128)(2,1)S(1)}, u32[]{:S(2)}, u32[]{:S(2)}) collective-permute-start(bf16[128,1024]{1,0:T(8,128)(2,1)S(1)} %pad_maximum_fusion.1.refs_2_), channel_id=1, source_target_pairs={{0,24},{2,26},{4,28},{6,30},{8,16},{10,18},{12,20},{14,22},{16,8},... | collective-permute-start | bytes 786440 | tf_op jit(solution)/shard_map/out_z3/ppermute | solution.py:35
  30.4 1.5 %collective-permute-start.16 = (bf16[64,1536]{1,0:T(8,128)(2,1)S(1)}, bf16[64,1536]{1,0:T(8,128)(2,1)S(1)}, u32[]{:S(2)}, u32[]{:S(2)}) collective-permute-start(bf16[64,1536]{1,0:T(8,128)(2,1)S(1)} %collective-permute-done.12.refs_17_), channel_id=1, source_target_pairs={{0,2},{2,0},{4,6},{6,4},{8,10},{10,8},{12,14},{14,12},{16,18},{18,... | collective-permute-start | bytes 589832 | tf_op jit(solution)/shard_map/in_core_14/ppermute | solution.py:35
  30.8 1.4 %collective-permute-start.14 = (bf16[64,1536]{1,0:T(8,128)(2,1)S(1)}, bf16[64,1536]{1,0:T(8,128)(2,1)S(1)}, u32[]{:S(2)}, u32[]{:S(2)}) collective-permute-start(bf16[64,1536]{1,0:T(8,128)(2,1)S(1)} %collective-permute-done.13.refs_13_), channel_id=1, source_target_pairs={{0,2},{2,0},{4,6},{6,4},{8,10},{10,8},{12,14},{14,12},{16,18},{18,... | collective-permute-start | bytes 589832 | tf_op jit(solution)/shard_map/in_core_10/ppermute | solution.py:35
  31.0 1.6 %collective-permute-start.10 = (bf16[64,1536]{1,0:T(8,128)(2,1)S(1)}, bf16[64,1536]{1,0:T(8,128)(2,1)S(1)}, u32[]{:S(2)}, u32[]{:S(2)}) collective-permute-start(bf16[64,1536]{1,0:T(8,128)(2,1)S(1)} %collective-permute-done.9.refs_9_), channel_id=1, source_target_pairs={{0,2},{2,0},{4,6},{6,4},{8,10},{10,8},{12,14},{14,12},{16,18},{18,... | collective-permute-start | bytes 589832 | tf_op jit(solution)/shard_map/in_core_6/ppermute | solution.py:35
  37.2 12.2 %collective-permute-start.17 = (bf16[384,512]{1,0:T(8,128)(2,1)S(1)}, bf16[384,512]{1,0:T(8,128)(2,1)S(1)}, u32[]{:S(2)}, u32[]{:S(2)}) collective-permute-start(bf16[384,512]{1,0:T(8,128)(2,1)S(1)} %get-tuple-element.28), channel_id=1, source_target_pairs={{0,1},{1,0},{2,3},{3,2},{4,5},{5,4},{6,7},{7,6},{8,9},{9,8},{10,11... | collective-permute-start | bytes 1179656 | tf_op jit(solution)/shard_map/context/ppermute | solution.py:35
  39.6 9.8 %collective-permute-start.22 = (bf16[128,1024]{1,0:T(8,128)(2,1)S(1)}, bf16[128,1024]{1,0:T(8,128)(2,1)S(1)}, u32[]{:S(2)}, u32[]{:S(2)}) collective-permute-start(bf16[128,1024]{1,0:T(8,128)(2,1)S(1)} %collective-permute-done.20.refs_6_), channel_id=1, source_target_pairs={{0,8},{2,10},{4,12},{6,14},{8,0},{10,2},{12,4},{14,6},{16,24},{18,... | collective-permute-start | bytes 786440 | tf_op jit(solution)/shard_map/out_z2/ppermute | solution.py:35
  46.1 3.3 %collective-permute-start.18 = (bf16[128,1024]{1,0:T(8,128)(2,1)S(1)}, bf16[128,1024]{1,0:T(8,128)(2,1)S(1)}, u32[]{:S(2)}, u32[]{:S(2)}) collective-permute-start(bf16[128,1024]{1,0:T(8,128)(2,1)S(1)} %pad_maximum_fusion.1.refs_2_), channel_id=1, source_target_pairs={{0,2},{2,0},{4,6},{6,4},{8,10},{10,8},{12,14},{14,12},{16,18},{18,... | collective-permute-start | bytes 786440 | tf_op jit(solution)/shard_map/out_core_0/ppermute | solution.py:35
  46.5 2.8 %collective-permute-start.19 = (bf16[128,1024]{1,0:T(8,128)(2,1)S(1)}, bf16[128,1024]{1,0:T(8,128)(2,1)S(1)}, u32[]{:S(2)}, u32[]{:S(2)}) collective-permute-start(bf16[128,1024]{1,0:T(8,128)(2,1)S(1)} %collective-permute-done.4.refs_4_), channel_id=1, source_target_pairs={{0,2},{2,0},{4,6},{6,4},{8,10},{10,8},{12,14},{14,12},{16,18},{18,... | collective-permute-start | bytes 786440 | tf_op jit(solution)/shard_map/out_core_4/ppermute | solution.py:35
  46.7 2.7 %collective-permute-start.21 = (bf16[128,1024]{1,0:T(8,128)(2,1)S(1)}, bf16[128,1024]{1,0:T(8,128)(2,1)S(1)}, u32[]{:S(2)}, u32[]{:S(2)}) collective-permute-start(bf16[128,1024]{1,0:T(8,128)(2,1)S(1)} %collective-permute-done.20.refs_6_), channel_id=1, source_target_pairs={{0,2},{2,0},{4,6},{6,4},{8,10},{10,8},{12,14},{14,12},{16,18},{18,... | collective-permute-start | bytes 786440 | tf_op jit(solution)/shard_map/out_core_12/ppermute | solution.py:35
  49.4 1.5 %collective-permute-start.23 = (bf16[128,1024]{1,0:T(8,128)(2,1)S(1)}, bf16[128,1024]{1,0:T(8,128)(2,1)S(1)}, u32[]{:S(2)}, u32[]{:S(2)}) collective-permute-start(bf16[128,1024]{1,0:T(8,128)(2,1)S(1)} %collective-permute-done.22.refs_8_), channel_id=1, source_target_pairs={{0,2},{2,0},{4,6},{6,4},{8,10},{10,8},{12,14},{14,12},{16,18},{18,... | collective-permute-start | bytes 786440 | tf_op jit(solution)/shard_map/out_core_8/ppermute | solution.py:35
  (7 other events, 61.5 us)

commit v9 on v7

--- a/solution.py
+++ b/solution.py
@@ -13,7 +13,7 @@
 HEAD_DIM = D // HEADS
 PAIR = 2 * HEAD_DIM
 
-ROUND = 3
+ROUND = 4
 ROWS = 16
 UNROLLED = 36
 STEP = 256

time: 52.7 us -> 52.7 us (level)
  Pallas kernels: 9.85 us -> 12.1 us
  waiting for transfers between devices: 14.9 us -> 13.8 us
  starting transfers between devices: 25.9 us -> 24.8 us
    pallas_call x1, Pallas kernels: 1.67 us -> 2.8 us  [on_device(): call(functools.partial(own_kernel, strips), strip_out, [SMEM] + [VMEM] *...]
    ppermute x24, waiting for transfers between devices: 14.9 us -> 13.8 us  [swap(): return lax.ppermute(block, axis, [(i, i ^ distance) for i in range(size)])]
    ppermute x24, starting transfers between devices: 25.9 us -> 24.8 us  [swap(): return lax.ppermute(block, axis, [(i, i ^ distance) for i in range(size)])]
    pallas_call x1, Pallas kernels: 4.61 us -> 5.72 us  [on_device(): call(functools.partial(project_kernel, strips, len(normed), [[slot] for s...]
  transfers between devices with their start and end apart: 24 -> 24, of which waited for: 10 -> 11; matrix products, arithmetic and copies ran while one was open for 0% -> 0% of each run, Pallas kernels for 15% -> 19%
where the time goes in v9:
time: 52.7 us; the launch traced here: 52.6 us
  starting transfers between devices  24.8 us (47%)
  waiting for transfers between devices  13.8 us (26%)
  Pallas kernels  12.1 us (23%)
  local copies, waits for them, and re-layouts  1.05 us (2%)
  between operations  0.83 us (2%)
    ppermute x24, starting transfers between devices, swap(): return lax.ppermute(block, axis, [(i, i ^ distance) for i in range(size)])  24.8 us
    ppermute x24, waiting for transfers between devices, swap(): return lax.ppermute(block, axis, [(i, i ^ distance) for i in range(size)])  13.8 us
    pallas_call x1, Pallas kernels, on_device(): call(functools.partial(project_kernel, strips, len(normed), [[slot] for s...  5.72 us
    pallas_call x1, Pallas kernels, on_device(): call(functools.partial(own_kernel, strips), strip_out, [SMEM] + [VMEM] *...  2.8 us
    pallas_call x1, Pallas kernels, on_device(): call(functools.partial(output_kernel, strips, out_slots), [jax.ShapeDtype...  1.97 us
    pallas_call x2, Pallas kernels, norm(): call(norm_kernel, jax.ShapeDtypeStruct((length, features), jnp.bfloat16),...  1.6 us
  transfers between devices with their start and end apart: 24, of which 11 were waited for; matrix products, arithmetic and copies ran while one was open for 0% of the time, Pallas kernels for 19%

profile of v9, /device:TPU:0, one launch (start us, length us, event | category | flops | bytes accessed | tf_op | source)
XLA Modules:
  0.0 52.6 jit_solution(9603577849442660769)
XLA Ops:
  0.7 1.0 %constant_dynamic-slice_fusion.2 = (bf16[64,512]{1,0:T(8,128)(2,1)S(1)}, bf16[64,512]{1,0:T(8,128)(2,1)S(1)}, bf16[64,512]{1,0:T(8,128)(2,1)S(1)}) fusion(bf16[64,3072]{1,0:T(8,128)(2,1)} %param.12, s32[]{:T(128)S(6)} %select_n.9, s32[]{:T(128)S(6)} %select_n.11, s32[]{:T(128)S(6)} %select_n.10), kind=kLoop, calls=%fused_computation.10 | loop fusion | bytes 393228 | tf_op jit(solution)/shard_map/dynamic_slice | solution.py:282
  1.7 5.1 %collective-permute-start.2 = (bf16[64,1536]{1,0:T(8,128)(2,1)S(1)}, bf16[64,1536]{1,0:T(8,128)(2,1)S(1)}, u32[]{:S(2)}, u32[]{:S(2)}) collective-permute-start(bf16[64,1536]{1,0:T(8,128)(2,1)S(1)} %pad_maximum_fusion.2.refs_3_), channel_id=1, source_target_pairs={{0,24},{2,26},{4,28},{6,30},{8,16},{10,18},{12,20},{14,22},{16,8},... | collective-permute-start | bytes 589832 | tf_op jit(solution)/shard_map/in_z3/ppermute | solution.py:35
  6.9 1.6 %collective-permute-start.1 = (bf16[64,2560]{1,0:T(8,128)(2,1)S(1)}, bf16[64,2560]{1,0:T(8,128)(2,1)S(1)}, u32[]{:S(2)}, u32[]{:S(2)}) collective-permute-start(bf16[64,2560]{1,0:T(8,128)(2,1)S(1)} %pad_maximum_fusion), channel_id=1, source_target_pairs={{0,4},{2,6},{4,0},{6,2},{8,12},{10,14},{12,8},{14,10},{16,20},{18,... | collective-permute-start | bytes 983048 | tf_op jit(solution)/shard_map/in_x/ppermute | solution.py:35
  8.5 1.6 %collective-permute-start = (bf16[400,1024]{1,0:T(8,128)(2,1)S(1)}, bf16[400,1024]{1,0:T(8,128)(2,1)S(1)}, u32[]{:S(2)}, u32[]{:S(2)}) collective-permute-start(bf16[400,1024]{1,0:T(8,128)(2,1)S(1)} %fusion.1), channel_id=1, source_target_pairs={{0,1},{1,0},{2,3},{3,2},{4,5},{5,4},{6,7},{7,6},{8,9},{9,8},{10,11... | collective-permute-start | bytes 2457608 | tf_op jit(solution)/shard_map/tokens/ppermute | solution.py:35
  10.1 2.5 %collective-permute-done.2.refs_15_ = bf16[64,1536]{1,0:T(8,128)(2,1)S(1)} collective-permute-done((bf16[64,1536]{1,0:T(8,128)(2,1)S(1)}, bf16[64,1536]{1,0:T(8,128)(2,1)S(1)}, u32[]{:S(2)}, u32[]{:S(2)}) %collective-permute-start.2) | collective-permute-done | bytes 196640 | tf_op jit(solution)/shard_map/in_z3/ppermute | solution.py:35
  12.6 3.1 %collective-permute-start.3 = (bf16[64,1536]{1,0:T(8,128)(2,1)S(1)}, bf16[64,1536]{1,0:T(8,128)(2,1)S(1)}, u32[]{:S(2)}, u32[]{:S(2)}) collective-permute-start(bf16[64,1536]{1,0:T(8,128)(2,1)S(1)} %collective-permute-done.2.refs_15_), channel_id=1, source_target_pairs={{0,8},{2,10},{4,12},{6,14},{8,0},{10,2},{12,4},{14,6},{16,24},{18,... | collective-permute-start | bytes 589832 | tf_op jit(solution)/shard_map/in_z2/ppermute | solution.py:35
  15.6 1.5 %collective-permute-start.12 = (bf16[64,1536]{1,0:T(8,128)(2,1)S(1)}, bf16[64,1536]{1,0:T(8,128)(2,1)S(1)}, u32[]{:S(2)}, u32[]{:S(2)}) collective-permute-start(bf16[64,1536]{1,0:T(8,128)(2,1)S(1)} %collective-permute-done.2.refs_15_), channel_id=1, source_target_pairs={{0,4},{2,6},{4,0},{6,2},{8,12},{10,14},{12,8},{14,10},{16,20},{18,... | collective-permute-start | bytes 589832 | tf_op jit(solution)/shard_map/in_z3_x/ppermute | solution.py:35
  17.7 0.8 %norm.2.refs_1_ = bf16[384,1024]{1,0:T(8,128)(2,1)S(1)} custom-call(bf16[384,1024]{1,0:T(8,128)(2,1)S(1)} %bitcast.12, f32[1,1024]{1,0:T(1,128)S(1)} %bitcast.15, f32[1,1024]{1,0:T(1,128)S(1)} %bitcast.17), custom_call_target="tpu_custom_call" | custom-call | flops 99999997952 | tf_op jit(solution)/shard_map/norm/pallas_call | solution.py:295
  18.5 1.8 %collective-permute-done.3.refs_11_ = bf16[64,1536]{1,0:T(8,128)(2,1)S(1)} collective-permute-done((bf16[64,1536]{1,0:T(8,128)(2,1)S(1)}, bf16[64,1536]{1,0:T(8,128)(2,1)S(1)}, u32[]{:S(2)}, u32[]{:S(2)}) %collective-permute-start.3) | collective-permute-done | bytes 196640 | tf_op jit(solution)/shard_map/in_z2/ppermute | solution.py:35
  20.2 1.5 %collective-permute-start.9 = (bf16[64,1536]{1,0:T(8,128)(2,1)S(1)}, bf16[64,1536]{1,0:T(8,128)(2,1)S(1)}, u32[]{:S(2)}, u32[]{:S(2)}) collective-permute-start(bf16[64,1536]{1,0:T(8,128)(2,1)S(1)} %collective-permute-done.7.refs_7_), channel_id=1, source_target_pairs={{0,4},{2,6},{4,0},{6,2},{8,12},{10,14},{12,8},{14,10},{16,20},{18,... | collective-permute-start | bytes 589832 | tf_op jit(solution)/shard_map/in_z1_x/ppermute | solution.py:35
  21.8 1.8 %collective-permute-start.4 = (bf16[128,1024]{1,0:T(8,128)(2,1)S(1)}, bf16[128,1024]{1,0:T(8,128)(2,1)S(1)}, u32[]{:S(2)}, u32[]{:S(2)}) collective-permute-start(bf16[128,1024]{1,0:T(8,128)(2,1)S(1)} %pad_maximum_fusion.1.refs_2_), channel_id=1, source_target_pairs={{0,8},{2,10},{4,12},{6,14},{8,0},{10,2},{12,4},{14,6},{16,24},{18,... | collective-permute-start | bytes 786440 | tf_op jit(solution)/shard_map/out_z1/ppermute | solution.py:35
  23.5 1.0 %collective-permute-start.13 = (bf16[64,1536]{1,0:T(8,128)(2,1)S(1)}, bf16[64,1536]{1,0:T(8,128)(2,1)S(1)}, u32[]{:S(2)}, u32[]{:S(2)}) collective-permute-start(bf16[64,1536]{1,0:T(8,128)(2,1)S(1)} %collective-permute-done.3.refs_11_), channel_id=1, source_target_pairs={{0,4},{2,6},{4,0},{6,2},{8,12},{10,14},{12,8},{14,10},{16,20},{18,... | collective-permute-start | bytes 589832 | tf_op jit(solution)/shard_map/in_z2_x/ppermute | solution.py:35
  24.6 1.4 %collective-permute-done.9.refs_9_ = bf16[64,1536]{1,0:T(8,128)(2,1)S(1)} collective-permute-done((bf16[64,1536]{1,0:T(8,128)(2,1)S(1)}, bf16[64,1536]{1,0:T(8,128)(2,1)S(1)}, u32[]{:S(2)}, u32[]{:S(2)}) %collective-permute-start.9) | collective-permute-done | bytes 196640 | tf_op jit(solution)/shard_map/in_z1_x/ppermute | solution.py:35
  25.9 3.0 %collective-permute-done.sheet_ref = bf16[400,1024]{1,0:T(8,128)(2,1)S(1)} collective-permute-done((bf16[400,1024]{1,0:T(8,128)(2,1)S(1)}, bf16[400,1024]{1,0:T(8,128)(2,1)S(1)}, u32[]{:S(2)}, u32[]{:S(2)}) %collective-permute-start) | collective-permute-done | bytes 819232 | tf_op jit(solution)/shard_map/tokens/ppermute | solution.py:35
  28.9 0.6 %collective-permute-start.20 = (bf16[128,1024]{1,0:T(8,128)(2,1)S(1)}, bf16[128,1024]{1,0:T(8,128)(2,1)S(1)}, u32[]{:S(2)}, u32[]{:S(2)}) collective-permute-start(bf16[128,1024]{1,0:T(8,128)(2,1)S(1)} %pad_maximum_fusion.1.refs_2_), channel_id=1, source_target_pairs={{0,24},{2,26},{4,28},{6,30},{8,16},{10,18},{12,20},{14,22},{16,8},... | collective-permute-start | bytes 786440 | tf_op jit(solution)/shard_map/out_z3/ppermute | solution.py:35
  29.6 0.8 %norm.3.refs_2_ = bf16[384,1024]{1,0:T(8,128)(2,1)S(1)} custom-call(bf16[400,1024]{1,0:T(8,128)(2,1)S(1)} %collective-permute-done.sheet_ref, f32[1,1024]{1,0:T(1,128)S(1)} %bitcast.16, f32[1,1024]{1,0:T(1,128)S(1)} %bitcast.18), custom_call_target="tpu_custom_call" | custom-call | tf_op jit(solution)/shard_map/norm/pallas_call | solution.py:295
  31.4 0.5 collective-permute-done.16.refs_18_
  32.6 5.7 %project.1 = (bf16[384,512]{1,0:T(8,128)(2,1)S(1)}, bf16[384,512]{1,0:T(8,128)(2,1)S(1)}, bf16[768,512]{1,0:T(8,128)(2,1)S(1)}, bf16[4,144,768]{2,1,0:T(8,128)(2,1)S(1)}) custom-call(s32[3,6]{1,0:T(4,128)S(1)} %slice_convert_fusion.refs_0_, bf16[384,1024]{1,0:T(8,128)(2,1)S(1)} %norm.2.refs_1_, bf16[384,1024]{1,0:T(8,128)(2,1)S(1)} %norm.3.refs_2_, ...), custom_call_target="tpu_custom_call" | custom-call | tf_op jit(solution)/shard_map/project/pallas_call | solution.py:344
  38.3 1.6 %collective-permute-start.17 = (bf16[384,512]{1,0:T(8,128)(2,1)S(1)}, bf16[384,512]{1,0:T(8,128)(2,1)S(1)}, u32[]{:S(2)}, u32[]{:S(2)}) collective-permute-start(bf16[384,512]{1,0:T(8,128)(2,1)S(1)} %get-tuple-element.28), channel_id=1, source_target_pairs={{0,1},{1,0},{2,3},{3,2},{4,5},{5,4},{6,7},{7,6},{8,9},{9,8},{10,11... | collective-permute-start | bytes 1179656 | tf_op jit(solution)/shard_map/context/ppermute | solution.py:35
  39.9 3.7 %collective-permute-start.22 = (bf16[128,1024]{1,0:T(8,128)(2,1)S(1)}, bf16[128,1024]{1,0:T(8,128)(2,1)S(1)}, u32[]{:S(2)}, u32[]{:S(2)}) collective-permute-start(bf16[128,1024]{1,0:T(8,128)(2,1)S(1)} %collective-permute-done.20.refs_6_), channel_id=1, source_target_pairs={{0,8},{2,10},{4,12},{6,14},{8,0},{10,2},{12,4},{14,6},{16,24},{18,... | collective-permute-start | bytes 786440 | tf_op jit(solution)/shard_map/out_z2/ppermute | solution.py:35
  43.6 2.8 %own_strip.1.refs_0_ = bf16[384,512]{1,0:T(8,128)(2,1)S(1)} custom-call(s32[3,6]{1,0:T(4,128)S(1)} %get-tuple-element.40.mask_ref, bf16[384,512]{1,0:T(8,128)(2,1)S(1)} %get-tuple-element.25.query_ref, bf16[768,512]{1,0:T(8,128)(2,1)S(1)} %get-tuple-element.26.key_ref, bf16[4,144,768]{2,1,0:T(8,128)(2,1)S(1)} %get-tuple-element.27.value_ref), custom_call_target="tpu_custom_call" | custom-call | flops 99999997952 | tf_op jit(solution)/shard_map/own_strip/pallas_call | solution.py:368
  47.1 2.0 %collective-permute-done.22.refs_8_ = bf16[128,1024]{1,0:T(8,128)(2,1)S(1)} collective-permute-done((bf16[128,1024]{1,0:T(8,128)(2,1)S(1)}, bf16[128,1024]{1,0:T(8,128)(2,1)S(1)}, u32[]{:S(2)}, u32[]{:S(2)}) %collective-permute-start.22) | collective-permute-done | bytes 262176 | tf_op jit(solution)/shard_map/out_z2/ppermute | solution.py:35
  49.6 1.0 %collective-permute-done.23.refs_9_ = bf16[128,1024]{1,0:T(8,128)(2,1)S(1)} collective-permute-done((bf16[128,1024]{1,0:T(8,128)(2,1)S(1)}, bf16[128,1024]{1,0:T(8,128)(2,1)S(1)}, u32[]{:S(2)}, u32[]{:S(2)}) %collective-permute-start.23) | collective-permute-done | bytes 262176 | tf_op jit(solution)/shard_map/out_core_8/ppermute | solution.py:35
  50.6 2.0 %output.1 = (bf16[384,1024]{1,0:T(8,128)(2,1)}, bf16[384,1024]{1,0:T(8,128)(2,1)}) custom-call(bf16[384,512]{1,0:T(8,128)(2,1)S(1)} %own_strip.1.refs_0_, bf16[384,512]{1,0:T(8,128)(2,1)S(1)} %collective-permute-done.17.refs_1_, bf16[128,1024]{1,0:T(8,128)(2,1)S(1)} %pad_maximum_fusion.1.refs_2_, bf16[128,1024]{1,0:T(8,128)(2,1)S(1)} %collective-permute-done.18.refs_3_, ...), custom_call_target="tpu_custom_call" | custom-call | flops 805306368 | bytes 2097152 | tf_op jit(solution)/shard_map/output/pallas_call | solution.py:385
  (51 shorter events, 3.5 us)
Async XLA Ops:
  1.7 10.9 %collective-permute-start.2 = (bf16[64,1536]{1,0:T(8,128)(2,1)S(1)}, bf16[64,1536]{1,0:T(8,128)(2,1)S(1)}, u32[]{:S(2)}, u32[]{:S(2)}) collective-permute-start(bf16[64,1536]{1,0:T(8,128)(2,1)S(1)} %pad_maximum_fusion.2.refs_3_), channel_id=1, source_target_pairs={{0,24},{2,26},{4,28},{6,30},{8,16},{10,18},{12,20},{14,22},{16,8},... | collective-permute-start | bytes 589832 | tf_op jit(solution)/shard_map/in_z3/ppermute | solution.py:35
  6.8 8.8 %collective-permute-start.5 = (bf16[64,1536]{1,0:T(8,128)(2,1)S(1)}, bf16[64,1536]{1,0:T(8,128)(2,1)S(1)}, u32[]{:S(2)}, u32[]{:S(2)}) collective-permute-start(bf16[64,1536]{1,0:T(8,128)(2,1)S(1)} %pad_maximum_fusion.2.refs_3_), channel_id=1, source_target_pairs={{0,2},{2,0},{4,6},{6,4},{8,10},{10,8},{12,14},{14,12},{16,18},{18,... | collective-permute-start | bytes 589832 | tf_op jit(solution)/shard_map/in_core_0/ppermute | solution.py:35
  6.8 10.3 %collective-permute-start.7 = (bf16[64,1536]{1,0:T(8,128)(2,1)S(1)}, bf16[64,1536]{1,0:T(8,128)(2,1)S(1)}, u32[]{:S(2)}, u32[]{:S(2)}) collective-permute-start(bf16[64,1536]{1,0:T(8,128)(2,1)S(1)} %pad_maximum_fusion.2.refs_3_), channel_id=1, source_target_pairs={{0,8},{2,10},{4,12},{6,14},{8,0},{10,2},{12,4},{14,6},{16,24},{18,... | collective-permute-start | bytes 589832 | tf_op jit(solution)/shard_map/in_z1/ppermute | solution.py:35
  6.9 10.3 %collective-permute-start.1 = (bf16[64,2560]{1,0:T(8,128)(2,1)S(1)}, bf16[64,2560]{1,0:T(8,128)(2,1)S(1)}, u32[]{:S(2)}, u32[]{:S(2)}) collective-permute-start(bf16[64,2560]{1,0:T(8,128)(2,1)S(1)} %pad_maximum_fusion), channel_id=1, source_target_pairs={{0,4},{2,6},{4,0},{6,2},{8,12},{10,14},{12,8},{14,10},{16,20},{18,... | collective-permute-start | bytes 983048 | tf_op jit(solution)/shard_map/in_x/ppermute | solution.py:35
  8.5 20.4 %collective-permute-start = (bf16[400,1024]{1,0:T(8,128)(2,1)S(1)}, bf16[400,1024]{1,0:T(8,128)(2,1)S(1)}, u32[]{:S(2)}, u32[]{:S(2)}) collective-permute-start(bf16[400,1024]{1,0:T(8,128)(2,1)S(1)} %fusion.1), channel_id=1, source_target_pairs={{0,1},{1,0},{2,3},{3,2},{4,5},{5,4},{6,7},{7,6},{8,9},{9,8},{10,11... | collective-permute-start | bytes 2457608 | tf_op jit(solution)/shard_map/tokens/ppermute | solution.py:35
  12.6 7.7 %collective-permute-start.3 = (bf16[64,1536]{1,0:T(8,128)(2,1)S(1)}, bf16[64,1536]{1,0:T(8,128)(2,1)S(1)}, u32[]{:S(2)}, u32[]{:S(2)}) collective-permute-start(bf16[64,1536]{1,0:T(8,128)(2,1)S(1)} %collective-permute-done.2.refs_15_), channel_id=1, source_target_pairs={{0,8},{2,10},{4,12},{6,14},{8,0},{10,2},{12,4},{14,6},{16,24},{18,... | collective-permute-start | bytes 589832 | tf_op jit(solution)/shard_map/in_z2/ppermute | solution.py:35
  15.6 6.1 %collective-permute-start.12 = (bf16[64,1536]{1,0:T(8,128)(2,1)S(1)}, bf16[64,1536]{1,0:T(8,128)(2,1)S(1)}, u32[]{:S(2)}, u32[]{:S(2)}) collective-permute-start(bf16[64,1536]{1,0:T(8,128)(2,1)S(1)} %collective-permute-done.2.refs_15_), channel_id=1, source_target_pairs={{0,4},{2,6},{4,0},{6,2},{8,12},{10,14},{12,8},{14,10},{16,20},{18,... | collective-permute-start | bytes 589832 | tf_op jit(solution)/shard_map/in_z3_x/ppermute | solution.py:35
  17.1 6.4 %collective-permute-start.15 = (bf16[64,1536]{1,0:T(8,128)(2,1)S(1)}, bf16[64,1536]{1,0:T(8,128)(2,1)S(1)}, u32[]{:S(2)}, u32[]{:S(2)}) collective-permute-start(bf16[64,1536]{1,0:T(8,128)(2,1)S(1)} %collective-permute-done.2.refs_15_), channel_id=1, source_target_pairs={{0,2},{2,0},{4,6},{6,4},{8,10},{10,8},{12,14},{14,12},{16,18},{18,... | collective-permute-start | bytes 589832 | tf_op jit(solution)/shard_map/in_core_12/ppermute | solution.py:35
  17.1 6.4 %collective-permute-start.8 = (bf16[64,1536]{1,0:T(8,128)(2,1)S(1)}, bf16[64,1536]{1,0:T(8,128)(2,1)S(1)}, u32[]{:S(2)}, u32[]{:S(2)}) collective-permute-start(bf16[64,1536]{1,0:T(8,128)(2,1)S(1)} %collective-permute-done.7.refs_7_), channel_id=1, source_target_pairs={{0,2},{2,0},{4,6},{6,4},{8,10},{10,8},{12,14},{14,12},{16,18},{18,... | collective-permute-start | bytes 589832 | tf_op jit(solution)/shard_map/in_core_4/ppermute | solution.py:35
  20.2 5.7 %collective-permute-start.9 = (bf16[64,1536]{1,0:T(8,128)(2,1)S(1)}, bf16[64,1536]{1,0:T(8,128)(2,1)S(1)}, u32[]{:S(2)}, u32[]{:S(2)}) collective-permute-start(bf16[64,1536]{1,0:T(8,128)(2,1)S(1)} %collective-permute-done.7.refs_7_), channel_id=1, source_target_pairs={{0,4},{2,6},{4,0},{6,2},{8,12},{10,14},{12,8},{14,10},{16,20},{18,... | collective-permute-start | bytes 589832 | tf_op jit(solution)/shard_map/in_z1_x/ppermute | solution.py:35
  21.8 9.2 %collective-permute-start.4 = (bf16[128,1024]{1,0:T(8,128)(2,1)S(1)}, bf16[128,1024]{1,0:T(8,128)(2,1)S(1)}, u32[]{:S(2)}, u32[]{:S(2)}) collective-permute-start(bf16[128,1024]{1,0:T(8,128)(2,1)S(1)} %pad_maximum_fusion.1.refs_2_), channel_id=1, source_target_pairs={{0,8},{2,10},{4,12},{6,14},{8,0},{10,2},{12,4},{14,6},{16,24},{18,... | collective-permute-start | bytes 786440 | tf_op jit(solution)/shard_map/out_z1/ppermute | solution.py:35
  23.5 6.8 %collective-permute-start.11 = (bf16[64,1536]{1,0:T(8,128)(2,1)S(1)}, bf16[64,1536]{1,0:T(8,128)(2,1)S(1)}, u32[]{:S(2)}, u32[]{:S(2)}) collective-permute-start(bf16[64,1536]{1,0:T(8,128)(2,1)S(1)} %collective-permute-done.3.refs_11_), channel_id=1, source_target_pairs={{0,2},{2,0},{4,6},{6,4},{8,10},{10,8},{12,14},{14,12},{16,18},{18,... | collective-permute-start | bytes 589832 | tf_op jit(solution)/shard_map/in_core_8/ppermute | solution.py:35
  23.5 7.3 %collective-permute-start.13 = (bf16[64,1536]{1,0:T(8,128)(2,1)S(1)}, bf16[64,1536]{1,0:T(8,128)(2,1)S(1)}, u32[]{:S(2)}, u32[]{:S(2)}) collective-permute-start(bf16[64,1536]{1,0:T(8,128)(2,1)S(1)} %collective-permute-done.3.refs_11_), channel_id=1, source_target_pairs={{0,4},{2,6},{4,0},{6,2},{8,12},{10,14},{12,8},{14,10},{16,20},{18,... | collective-permute-start | bytes 589832 | tf_op jit(solution)/shard_map/in_z2_x/ppermute | solution.py:35
  25.9 5.9 %collective-permute-start.6 = (bf16[64,2560]{1,0:T(8,128)(2,1)S(1)}, bf16[64,2560]{1,0:T(8,128)(2,1)S(1)}, u32[]{:S(2)}, u32[]{:S(2)}) collective-permute-start(bf16[64,2560]{1,0:T(8,128)(2,1)S(1)} %collective-permute-done.1.refs_5_), channel_id=1, source_target_pairs={{0,2},{2,0},{4,6},{6,4},{8,10},{10,8},{12,14},{14,12},{16,18},{18,... | collective-permute-start | bytes 983048 | tf_op jit(solution)/shard_map/in_core_2/ppermute | solution.py:35
  28.9 10.9 %collective-permute-start.20 = (bf16[128,1024]{1,0:T(8,128)(2,1)S(1)}, bf16[128,1024]{1,0:T(8,128)(2,1)S(1)}, u32[]{:S(2)}, u32[]{:S(2)}) collective-permute-start(bf16[128,1024]{1,0:T(8,128)(2,1)S(1)} %pad_maximum_fusion.1.refs_2_), channel_id=1, source_target_pairs={{0,24},{2,26},{4,28},{6,30},{8,16},{10,18},{12,20},{14,22},{16,8},... | collective-permute-start | bytes 786440 | tf_op jit(solution)/shard_map/out_z3/ppermute | solution.py:35
  30.4 1.5 %collective-permute-start.16 = (bf16[64,1536]{1,0:T(8,128)(2,1)S(1)}, bf16[64,1536]{1,0:T(8,128)(2,1)S(1)}, u32[]{:S(2)}, u32[]{:S(2)}) collective-permute-start(bf16[64,1536]{1,0:T(8,128)(2,1)S(1)} %collective-permute-done.12.refs_17_), channel_id=1, source_target_pairs={{0,2},{2,0},{4,6},{6,4},{8,10},{10,8},{12,14},{14,12},{16,18},{18,... | collective-permute-start | bytes 589832 | tf_op jit(solution)/shard_map/in_core_14/ppermute | solution.py:35
  30.8 1.4 %collective-permute-start.14 = (bf16[64,1536]{1,0:T(8,128)(2,1)S(1)}, bf16[64,1536]{1,0:T(8,128)(2,1)S(1)}, u32[]{:S(2)}, u32[]{:S(2)}) collective-permute-start(bf16[64,1536]{1,0:T(8,128)(2,1)S(1)} %collective-permute-done.13.refs_13_), channel_id=1, source_target_pairs={{0,2},{2,0},{4,6},{6,4},{8,10},{10,8},{12,14},{14,12},{16,18},{18,... | collective-permute-start | bytes 589832 | tf_op jit(solution)/shard_map/in_core_10/ppermute | solution.py:35
  31.0 1.6 %collective-permute-start.10 = (bf16[64,1536]{1,0:T(8,128)(2,1)S(1)}, bf16[64,1536]{1,0:T(8,128)(2,1)S(1)}, u32[]{:S(2)}, u32[]{:S(2)}) collective-permute-start(bf16[64,1536]{1,0:T(8,128)(2,1)S(1)} %collective-permute-done.9.refs_9_), channel_id=1, source_target_pairs={{0,2},{2,0},{4,6},{6,4},{8,10},{10,8},{12,14},{14,12},{16,18},{18,... | collective-permute-start | bytes 589832 | tf_op jit(solution)/shard_map/in_core_6/ppermute | solution.py:35
  38.3 11.3 %collective-permute-start.17 = (bf16[384,512]{1,0:T(8,128)(2,1)S(1)}, bf16[384,512]{1,0:T(8,128)(2,1)S(1)}, u32[]{:S(2)}, u32[]{:S(2)}) collective-permute-start(bf16[384,512]{1,0:T(8,128)(2,1)S(1)} %get-tuple-element.28), channel_id=1, source_target_pairs={{0,1},{1,0},{2,3},{3,2},{4,5},{5,4},{6,7},{7,6},{8,9},{9,8},{10,11... | collective-permute-start | bytes 1179656 | tf_op jit(solution)/shard_map/context/ppermute | solution.py:35
  39.9 9.2 %collective-permute-start.22 = (bf16[128,1024]{1,0:T(8,128)(2,1)S(1)}, bf16[128,1024]{1,0:T(8,128)(2,1)S(1)}, u32[]{:S(2)}, u32[]{:S(2)}) collective-permute-start(bf16[128,1024]{1,0:T(8,128)(2,1)S(1)} %collective-permute-done.20.refs_6_), channel_id=1, source_target_pairs={{0,8},{2,10},{4,12},{6,14},{8,0},{10,2},{12,4},{14,6},{16,24},{18,... | collective-permute-start | bytes 786440 | tf_op jit(solution)/shard_map/out_z2/ppermute | solution.py:35
  46.4 2.7 %collective-permute-start.18 = (bf16[128,1024]{1,0:T(8,128)(2,1)S(1)}, bf16[128,1024]{1,0:T(8,128)(2,1)S(1)}, u32[]{:S(2)}, u32[]{:S(2)}) collective-permute-start(bf16[128,1024]{1,0:T(8,128)(2,1)S(1)} %pad_maximum_fusion.1.refs_2_), channel_id=1, source_target_pairs={{0,2},{2,0},{4,6},{6,4},{8,10},{10,8},{12,14},{14,12},{16,18},{18,... | collective-permute-start | bytes 786440 | tf_op jit(solution)/shard_map/out_core_0/ppermute | solution.py:35
  46.5 2.6 %collective-permute-start.19 = (bf16[128,1024]{1,0:T(8,128)(2,1)S(1)}, bf16[128,1024]{1,0:T(8,128)(2,1)S(1)}, u32[]{:S(2)}, u32[]{:S(2)}) collective-permute-start(bf16[128,1024]{1,0:T(8,128)(2,1)S(1)} %collective-permute-done.4.refs_4_), channel_id=1, source_target_pairs={{0,2},{2,0},{4,6},{6,4},{8,10},{10,8},{12,14},{14,12},{16,18},{18,... | collective-permute-start | bytes 786440 | tf_op jit(solution)/shard_map/out_core_4/ppermute | solution.py:35
  47.0 2.1 %collective-permute-start.21 = (bf16[128,1024]{1,0:T(8,128)(2,1)S(1)}, bf16[128,1024]{1,0:T(8,128)(2,1)S(1)}, u32[]{:S(2)}, u32[]{:S(2)}) collective-permute-start(bf16[128,1024]{1,0:T(8,128)(2,1)S(1)} %collective-permute-done.20.refs_6_), channel_id=1, source_target_pairs={{0,2},{2,0},{4,6},{6,4},{8,10},{10,8},{12,14},{14,12},{16,18},{18,... | collective-permute-start | bytes 786440 | tf_op jit(solution)/shard_map/out_core_12/ppermute | solution.py:35
  49.1 1.5 %collective-permute-start.23 = (bf16[128,1024]{1,0:T(8,128)(2,1)S(1)}, bf16[128,1024]{1,0:T(8,128)(2,1)S(1)}, u32[]{:S(2)}, u32[]{:S(2)}) collective-permute-start(bf16[128,1024]{1,0:T(8,128)(2,1)S(1)} %collective-permute-done.22.refs_8_), channel_id=1, source_target_pairs={{0,2},{2,0},{4,6},{6,4},{8,10},{10,8},{12,14},{14,12},{16,18},{18,... | collective-permute-start | bytes 786440 | tf_op jit(solution)/shard_map/out_core_8/ppermute | solution.py:35
  (7 other events, 61.2 us)
